TPU v7x, 128 devices: a whole 4x4x4 slice. The times are simulated.
128 devices in a mesh: grp: 8 (over y, core), exp: 16 (over x, z).
Axes of the slice: x: 4, y: 4, z: 4, core: 2. Of those that a mesh axis runs over, the one named last changes fastest.
Arguments:
- tokens: bfloat16 [1024, 7168], P(('grp', 'exp')), may hold values from -6 to 6
- routes: int32 [1024, 8], P(('grp', 'exp')), may hold values from 0 to 63, as said below
- weights_q: int32 [1024, 8], P(('grp', 'exp')), may hold values from 1 to 255
- cotangent: bfloat16 [1024, 7168], P(('grp', 'exp')), may hold values from -6 to 6
- expert_gate: bfloat16 [128, 7168, 512], P(('grp', 'exp')), may hold values from -0.0625 to 0.0625
- expert_up: bfloat16 [128, 7168, 512], P(('grp', 'exp')), may hold values from -0.0625 to 0.0625
- expert_down: bfloat16 [128, 512, 7168], P(('grp', 'exp')), may hold values from -0.1875 to 0.1875
- shared_gate: bfloat16 [7168, 1024], P(None, 'exp'), may hold values from -0.0625 to 0.0625
- shared_up: bfloat16 [7168, 1024], P(None, 'exp'), may hold values from -0.0625 to 0.0625
- shared_down: bfloat16 [1024, 7168], P('exp'), may hold values from -0.1875 to 0.1875
Outputs:
- mixed: bfloat16 [1024, 7168], P(('grp', 'exp'))
- token_grad: bfloat16 [1024, 7168], P(('grp', 'exp'))
Inputs may be any that keep to these rules, and one draw needn't show every extreme that they name: `routes`: each row names 8 different experts, 2 of them in each of 4 different groups, where expert e belongs to group e // 8. Among the rows of one device (aligned blocks of 8 rows) no expert is named more than 2 times.
All inputs are finite; a program needn't handle non-finite values.
Results may differ from a plain program's by a relative error of at most 0.014.
Values may be sent and summed in bfloat16 or wider, within the bound.
No kernel may reach another device: no remote copies, remote signals or barrier semaphores. Data moves between devices by JAX's collectives and lax.ppermute only.
A program may use at most 128 MiB of HBM per device.

v0:
```python
import functools

import jax
import jax.numpy as jnp
from jax import lax
from jax.experimental import pallas as pl
from jax.experimental.pallas import tpu as pltpu
from jax.sharding import PartitionSpec as P

SPLIT = 2
TOP = 8
CAP = 2
N_Y, N_X, N_Z = 4, 4, 4
INFO = 128
BLK = 1024

F32, BF16, I32 = jnp.float32, jnp.bfloat16, jnp.int32


def silu_parts(values):
    logistic = 1.0 / (1.0 + jnp.exp(-values))
    return values * logistic, logistic * (1.0 + values * (1.0 - logistic))


def dot(a, b):
    return jnp.dot(a, b, preferred_element_type=F32)


def dot_t(a, b):
    return lax.dot_general(a, b, (((1,), (1,)), ((), ())), preferred_element_type=F32)


def dot_a(a, b):
    return lax.dot_general(a, b, (((0,), (0,)), ((), ())), preferred_element_type=F32)


def turn(order, v):
    return jnp.dot(order, v, precision=lax.Precision.HIGHEST, preferred_element_type=F32)


def grid_ids(rows, cols):
    return lax.broadcasted_iota(I32, (rows, cols), 0), lax.broadcasted_iota(I32, (rows, cols), 1)


def move_y(v, k):
    return lax.ppermute(v, "grp", [(y * 2 + c, (y + k) % N_Y * 2 + c) for y in range(N_Y) for c in range(2)])


def swap_core(v):
    return lax.ppermute(v, "grp", [(g, g ^ 1) for g in range(N_Y * 2)])


def move_x(v, k):
    return lax.ppermute(v, "exp", [(x * 4 + z, (x + k) % N_X * 4 + z) for x in range(N_X) for z in range(N_Z)])


def move_z(v, k):
    return lax.ppermute(v, "exp", [(x * 4 + z, x * 4 + (z + k) % N_Z) for x in range(N_X) for z in range(N_Z)])


def ring(move, v):
    return [v] + [move(v, k) for k in (1, 2, 3)]


def ring_sum(move, parts):
    total = parts[0].astype(F32)
    for k in (1, 2, 3):
        total = total + move(parts[k], -k).astype(F32)
    return total


def call(kernel, grid, ins, outs, scratch, flops, moved):
    in_specs = [
        pl.BlockSpec(memory_space=pltpu.SMEM)
        if block == "smem"
        else pl.BlockSpec(memory_space=pl.ANY)
        if block == "any"
        else pl.BlockSpec(block, at)
        for _, block, at in ins
    ]
    return pl.pallas_call(
        kernel,
        grid=(grid,),
        in_specs=in_specs,
        out_specs=[pl.BlockSpec(block, at) for _, _, block, at in outs],
        out_shape=[jax.ShapeDtypeStruct(shape, dtype) for shape, dtype, _, _ in outs],
        scratch_shapes=scratch,
        compiler_params=pltpu.CompilerParams(vmem_limit_bytes=28 * 1024 * 1024),
        cost_estimate=pl.CostEstimate(flops=flops, bytes_accessed=moved, transcendentals=0),
    )(*[a for a, _, _ in ins])


COL = lambda i: (0, i)
FIX = lambda i: (0, 0)


def slots_of(info, expert, block, rank):
    rows = info.shape[0]
    a, b = grid_ids(2 * TOP, INFO)
    across = dot_t((a == b).astype(BF16), info)
    want = expert.astype(F32)
    named = jnp.zeros(expert.shape, F32)
    scale = jnp.zeros(expert.shape, F32)
    for k in range(TOP):
        hit = across[k : k + 1, :] == want
        named = named + jnp.where(hit, 1.0, 0.0)
        scale = scale + jnp.where(hit, across[TOP + k : TOP + k + 1, :], 0.0)
    a, b = grid_ids(rows, rows)
    earlier = jnp.where(((a >> 3) == (b >> 3)) & (a < b), 1.0, 0.0).astype(BF16)
    before = dot(named.astype(BF16), earlier)
    _, row = grid_ids(*expert.shape)
    taken = (named > 0.5) & (before == rank.astype(F32)) & ((row >> 3) == block)
    return jnp.where(taken, 1.0, 0.0).astype(BF16), jnp.where(taken, scale * (1.0 / 256.0), 0.0).astype(BF16)


def cot_pick_kernel(at, g0, g1, i0, i1, sent, mix, hot):
    @pl.when(pl.program_id(0) == 0)
    def _():
        slot, _ = grid_ids(256, 64)
        info = jnp.concatenate([i0[...], i1[...]], axis=0)
        one, scaled = slots_of(info, at[0] * 8 + (slot >> 5), (slot >> 1) & 7, slot & 1)
        hot[...] = one
        mix[...] = scaled

    sent[...] = dot(hot[...], jnp.concatenate([g0[...], g1[...]], axis=0)).astype(BF16)


def tok_pick_kernel(at, _, b0, b1, b2, b3, i0, i1, i2, i3, sg, su, *rest):
    sent, (mix, gate, up, hot, acc) = rest[:8], rest[8:]
    step = pl.program_id(0)

    @pl.when(step == 0)
    def _():
        slot, _ = grid_ids(256, 128)
        info = jnp.concatenate([i0[...], i1[...], i2[...], i3[...]], axis=0)
        y = (at[0] // 2 + (slot >> 6)) & 3
        c = (at[0] + (slot >> 5)) & 1
        one, scaled = slots_of(info, (y * 2 + c) * 8 + at[1] // SPLIT, (slot >> 1) & 15, slot & 1)
        hot[...] = one
        mix[...] = scaled
        acc[...] = jnp.zeros_like(acc)

    rows = jnp.concatenate([b0[...], b1[...], b2[...], b3[...]], axis=0)
    picked = dot(hot[...], rows).astype(BF16)
    for n in range(8):
        sent[n][...] = picked[n * 32 : n * 32 + 32]
    acc[:, :64] += dot(rows, sg[...])
    acc[:, 64:] += dot(rows, su[...])

    @pl.when(step == pl.num_programs(0) - 1)
    def _():
        gate[...] = acc[:, :64]
        up[...] = acc[:, 64:]


def forward_kernel(*refs):
    xs, (gw, uw, dw), ys, (act, slope, acc_g, acc_u, hid) = refs[:8], refs[8:11], refs[11:19], refs[19:]
    step = pl.program_id(0)
    half = pl.num_programs(0) // 2

    @pl.when(step == 0)
    def _():
        acc_g[...] = jnp.zeros_like(acc_g)
        acc_u[...] = jnp.zeros_like(acc_u)

    @pl.when(step < half)
    def _():
        rows = jnp.concatenate([x[...] for x in xs], axis=0)
        acc_g[...] += dot(rows, gw[0])
        acc_u[...] += dot(rows, uw[0])

    @pl.when(step == half - 1)
    def _():
        silu, prime = silu_parts(acc_g[...])
        act[...] = silu
        slope[...] = acc_u[...] * prime
        hid[...] = (silu * acc_u[...]).astype(BF16)

    @pl.when(step >= half)
    def _():
        out = dot(hid[...], dw[0]).astype(BF16)
        for n in range(8):
            ys[n][...] = out[n * 32 : n * 32 + 32]


def grad_hidden_kernel(g, dw, out):
    @pl.when(pl.program_id(0) == 0)
    def _():
        out[...] = jnp.zeros_like(out)

    out[...] += dot_t(g[...], dw[0])


def backward_kernel(at, grad, act, slope, gw, uw, dx, dg, du):
    @pl.when(pl.program_id(0) == 0)
    def _():
        to, i = grid_ids(256, 256)
        x = (at[1] // 4 - ((i >> 1) & 3)) & 3
        z = (at[1] - ((i >> 3) & 3)) & 3
        order = jnp.where(to == ((x * 4 + z) * 8 + (i >> 5)) * 2 + (i & 1), 1.0, 0.0)
        dg[...] = (grad[...] * turn(order, slope[...])).astype(BF16)
        du[...] = (grad[...] * turn(order, act[...])).astype(BF16)

    dx[...] = (dot_t(dg[...], gw[0]) + dot_t(du[...], uw[0])).astype(BF16)


def out_sum_kernel(*refs):
    ys, (mix, gate, up, sd), outs, (hid,) = refs[:8], refs[8:12], refs[12:16], refs[16:]

    @pl.when(pl.program_id(0) == 0)
    def _():
        silu, _ = silu_parts(gate[...])
        hid[...] = (silu * up[...]).astype(BF16)

    rows = jnp.concatenate([y[...] for y in ys], axis=0)
    total = (dot_a(mix[...], rows) + dot(hid[...], sd[...])).astype(BF16)
    for n in range(4):
        outs[n][...] = total[n * 32 : n * 32 + 32]


def back_sum_kernel(rows, mix, mine, other):
    total = dot_a(mix[...], rows[...])
    mine[...] = total[:32]
    other[...] = total[32:].astype(BF16)


def shared_back_kernel(at, g, gate, up, sd, sg, su, o0, o1, o2, o3, acc, dg, du):
    step = pl.program_id(0)
    half = pl.num_programs(0) // 2

    @pl.when(step == 0)
    def _():
        acc[...] = jnp.zeros_like(acc)

    @pl.when(step < half)
    def _():
        acc[...] += dot_t(g[...], sd[...])

    @pl.when(step == half - 1)
    def _():
        to, i = grid_ids(128, 128)
        kx, kz = to >> 5, (to >> 3) & 3
        from_x = jnp.where(i == (kz * 4 + kx) * 8 + (to & 7), 1.0, 0.0)
        x, z = (at[1] // 4 - kx) & 3, (at[1] - kz) & 3
        from_g = jnp.where(i == (x * 4 + z) * 8 + (to & 7), 1.0, 0.0)
        silu, prime = silu_parts(gate[...])
        grad = turn(from_g, acc[...])
        dg[...] = (grad * turn(from_x, up[...] * prime)).astype(BF16)
        du[...] = (grad * turn(from_x, silu)).astype(BF16)

    @pl.when(step >= half)
    def _():
        total = (dot_t(dg[...], sg[...]) + dot_t(du[...], su[...])).astype(BF16)
        o0[...] = total[:32]
        o1[...] = total[32:64]
        o2[...] = total[64:96]
        o3[...] = total[96:]


def local(
    tokens,
    routes,
    weights_q,
    cotangent,
    expert_gate,
    expert_up,
    expert_down,
    shared_gate,
    shared_up,
    shared_down,
):
    width = tokens.shape[1]
    hidden = expert_gate.shape[2]
    part = shared_gate.shape[1]
    steps = width // BLK
    tail = width // INFO
    grp, exp = lax.axis_index("grp"), lax.axis_index("exp")
    at = jnp.stack([grp, exp]).astype(I32)
    info = jnp.pad(jnp.concatenate([routes, weights_q], axis=1).astype(BF16), ((0, 0), (0, INFO - 2 * TOP)))
    first = lambda i: (0, jnp.minimum(i, steps - 1))
    later = lambda i: (0, jnp.maximum(i - steps, 0))
    info_at = lambda i: (0, tail)
    SM = lambda a: (a, "smem", None)

    x_wide = jnp.concatenate([tokens, info], axis=1)
    g_wide = jnp.concatenate([cotangent, info], axis=1)
    with jax.named_scope("tok_gather"):
        x_line = jnp.concatenate(ring(move_x, x_wide), axis=0)
        x_blocks = ring(move_z, x_line)
    with jax.named_scope("cot_gather"):
        g_line = jnp.concatenate(ring(move_y, g_wide), axis=0)
        g_blocks = [g_line, swap_core(g_line)]
        cot_plane = lax.all_gather(cotangent, "exp", axis=0, tiled=True)

    with jax.named_scope("cot_pick"):
        g_sent, g_mix = call(
            cot_pick_kernel,
            steps,
            [SM(at)] + [(b, (32, BLK), COL) for b in g_blocks] + [(b, (32, INFO), info_at) for b in g_blocks],
            [((256, width), BF16, (256, BLK), COL), ((256, 64), BF16, (256, 64), FIX)],
            [pltpu.VMEM((256, 64), BF16)],
            2 * 256 * 64 * width,
            2 * 320 * width,
        )
    with jax.named_scope("cot_route"):
        g_rows = lax.all_to_all(g_sent.reshape(16, 16, width), "exp", split_axis=0, concat_axis=0, tiled=True)
        g_rows = g_rows.reshape(256, width)

    with jax.named_scope("tok_pick"):
        *x_sent, x_mix, s_gate, s_up = call(
            tok_pick_kernel,
            steps,
            [SM(at), (g_mix, "any", None)]
            + [(b, (32, BLK), COL) for b in x_blocks]
            + [(b, (32, INFO), info_at) for b in x_blocks]
            + [(shared_gate, (BLK, part), lambda i: (i, 0)), (shared_up, (BLK, part), lambda i: (i, 0))],
            [((32, width), BF16, (32, BLK), COL)] * 8
            + [((256, 128), BF16, (256, 128), FIX), ((128, part), F32, (128, part), FIX), ((128, part), F32, (128, part), FIX)],
            [pltpu.VMEM((256, 128), BF16), pltpu.VMEM((128, 2 * part), F32)],
            2 * 256 * 128 * width,
            2 * 500 * width,
        )
    with jax.named_scope("tok_route"):
        over = [x_sent[1]] + [move_y(x_sent[2 * k + 1], k) for k in (1, 2, 3)]
        x_rows = [x_sent[0]] + [move_y(x_sent[2 * k], k) for k in (1, 2, 3)]
        x_rows = x_rows + [swap_core(v) for v in over]

    with jax.named_scope("expert_grad_hidden"):
        (grad_hidden,) = call(
            grad_hidden_kernel,
            steps,
            [(g_rows, (256, BLK), COL), (expert_down, (1, hidden, BLK), lambda i: (0, 0, i))],
            [((256, hidden), F32, (256, hidden), FIX)],
            [],
            2 * 256 * hidden * width,
            2 * (256 + hidden) * width,
        )
    with jax.named_scope("expert_forward"):
        up_to = lambda i: (0, jnp.minimum(i, steps - 1), 0)
        *y_rows, act, slope = call(
            forward_kernel,
            2 * steps,
            [(x, (32, BLK), first) for x in x_rows]
            + [
                (expert_gate, (1, BLK, hidden), up_to),
                (expert_up, (1, BLK, hidden), up_to),
                (expert_down, (1, hidden, BLK), lambda i: (0, 0, jnp.maximum(i - steps, 0))),
            ],
            [((32, width), BF16, (32, BLK), later)] * 8 + [((256, hidden), F32, (256, hidden), FIX)] * 2,
            [pltpu.VMEM((256, hidden), F32), pltpu.VMEM((256, hidden), F32), pltpu.VMEM((256, hidden), BF16)],
            6 * 256 * hidden * width,
            2 * (512 + 3 * hidden) * width,
        )
    with jax.named_scope("expert_backward"):
        (dx_rows,) = call(
            backward_kernel,
            steps,
            [
                SM(at),
                (grad_hidden, (256, hidden), FIX),
                (act, (256, hidden), FIX),
                (slope, (256, hidden), FIX),
                (expert_gate, (1, BLK, hidden), lambda i: (0, i, 0)),
                (expert_up, (1, BLK, hidden), lambda i: (0, i, 0)),
            ],
            [((256, width), BF16, (256, BLK), COL)],
            [pltpu.VMEM((256, hidden), BF16), pltpu.VMEM((256, hidden), BF16)],
            4 * 256 * hidden * width,
            2 * (256 + 2 * hidden) * width,
        )
    with jax.named_scope("back_route"):
        dx_home = lax.all_to_all(dx_rows.reshape(16, 16, width), "exp", split_axis=0, concat_axis=0, tiled=True)
        dx_home = dx_home.reshape(256, width)

    with jax.named_scope("out_route"):
        y_other = [swap_core(v) for v in y_rows[4:]]
        y_home = [y_rows[0], y_other[0]]
        for k in (1, 2, 3):
            y_home += [move_y(y_rows[k], -k), move_y(y_other[k], -k)]
        parts = call(
            out_sum_kernel,
            steps,
            [(v, (32, BLK), COL) for v in y_home]
            + [
                (x_mix, (256, 128), FIX),
                (s_gate, (128, part), FIX),
                (s_up, (128, part), FIX),
                (shared_down, (part, BLK), COL),
            ],
            [((32, width), BF16, (32, BLK), COL)] * 4,
            [pltpu.VMEM((128, part), BF16)],
            2 * 256 * 128 * width,
            2 * 400 * width,
        )
        line = ring_sum(move_z, parts).astype(BF16).reshape(4, 8, width)
        mixed = ring_sum(move_x, [line[k] for k in range(4)]).astype(BF16)

    with jax.named_scope("shared_back"):
        twice = lambda i: (0, jnp.where(i < steps, i, 0))
        s_parts = call(
            shared_back_kernel,
            2 * steps,
            [
                SM(at),
                (cot_plane, (128, BLK), first),
                (s_gate, (128, part), FIX),
                (s_up, (128, part), FIX),
                (shared_down, (part, BLK), first),
                (shared_gate, (BLK, part), lambda i: (jnp.maximum(i - steps, 0), 0)),
                (shared_up, (BLK, part), lambda i: (jnp.maximum(i - steps, 0), 0)),
            ],
            [((32, width), BF16, (32, BLK), later)] * 4,
            [pltpu.VMEM((128, part), F32), pltpu.VMEM((128, part), BF16), pltpu.VMEM((128, part), BF16)],
            6 * 128 * part * width,
            2 * 500 * width,
        )
        s_line = ring_sum(move_x, s_parts).astype(BF16).reshape(4, 8, width)
        s_grad = ring_sum(move_z, [s_line[k] for k in range(4)])

    with jax.named_scope("back_sum"):
        mine, other = call(
            back_sum_kernel,
            steps,
            [(dx_home, (256, BLK), COL), (g_mix, (256, 64), FIX)],
            [((32, width), F32, (32, BLK), COL), ((32, width), BF16, (32, BLK), COL)],
            [],
            2 * 256 * 64 * width,
            2 * 352 * width,
        )
        line = (mine + swap_core(other).astype(F32)).reshape(4, 8, width)
        line = [line[0]] + [line[k].astype(BF16) for k in (1, 2, 3)]
        token_grad = (ring_sum(move_y, line) + s_grad).astype(BF16)
    return (mixed, token_grad)


def solution(mesh):
    in_specs = (
        P(("grp", "exp"), None),
        P(("grp", "exp"), None),
        P(("grp", "exp"), None),
        P(("grp", "exp"), None),
        P(("grp", "exp"), None, None),
        P(("grp", "exp"), None, None),
        P(("grp", "exp"), None, None),
        P(None, "exp"),
        P(None, "exp"),
        P("exp", None),
    )
    out_specs = (P(("grp", "exp"), None), P(("grp", "exp"), None))
    return jax.shard_map(local, mesh=mesh, in_specs=in_specs, out_specs=out_specs, check_vma=False)
```

profile of v0, /device:TPU:0, one launch (start us, length us, event | category | flops | bytes accessed | tf_op | source)
XLA Modules:
  0.0 378.4 jit_solution(14209692844431238598)
XLA Ops:
  9.6 2.9 collective-permute-start.6
  14.2 3.0 collective-permute-start.2
  17.8 1.2 collective-permute-start
  19.9 1.2 collective-permute-done.4
  21.5 2.4 collective-permute-done.1
  23.8 1.2 collective-permute-done
  25.0 1.0 fusion.5
  26.2 1.7 collective-permute-done.3.g1.i1
  28.0 3.7 cot_pick.1
  31.7 1.9 copy-done.8
  33.5 7.8 %all-to-all-start = ((bf16[16,16,7168]{2,1,0:T(8,128)(2,1)}), bf16[16,16,7168]{2,1,0:T(8,128)(2,1)}, u32[]{:S(2)}, u32[]{:S(2)}) async-start(bf16[16,16,7168]{2,1,0:T(8,128)(2,1)} %bitcast.7), calls=%async_computation | async-start | bytes 7340032 | tf_op jit(solution)/shard_map/cot_route/all_to_all | solution.py:306
  41.4 3.2 collective-permute-start.9
  46.3 2.0 copy.12.sg
  48.2 2.6 copy.13.su
  50.8 43.5 %collective-permute-done.9.b3.i3 = bf16[32,7296]{1,0:T(8,128)(2,1)S(1)} collective-permute-done((bf16[32,7296]{1,0:T(8,128)(2,1)S(1)}, bf16[32,7296]{1,0:T(8,128)(2,1)S(1)}, u32[]{:S(2)}, u32[]{:S(2)}) %collective-permute-start.9) | collective-permute-done | bytes 466976 | tf_op jit(solution)/shard_map/tok_gather/ppermute | solution.py:58
  94.3 3.2 collective-permute-done.8.b2.i2
  97.5 7.5 %collective-permute-done.7.b1.i1 = bf16[32,7296]{1,0:T(8,128)(2,1)} collective-permute-done((bf16[32,7296]{1,0:T(8,128)(2,1)S(1)}, bf16[32,7296]{1,0:T(8,128)(2,1)}, u32[]{:S(2)}, u32[]{:S(2)}) %collective-permute-start.7) | collective-permute-done | bytes 466976 | tf_op jit(solution)/shard_map/tok_gather/ppermute | solution.py:58
  105.0 1.5 copy-done.5
  106.5 7.1 %tok_pick.1 = (bf16[32,7168]{1,0:T(8,128)(2,1)S(1)}, bf16[32,7168]{1,0:T(8,128)(2,1)}, bf16[32,7168]{1,0:T(8,128)(2,1)S(1)}, bf16[32,7168]{1,0:T(8,128)(2,1)S(1)...) custom-call(s32[2]{0:T(128)S(1)} %pad_add_fusion.at, ...), custom_call_target="tpu_custom_call" | custom-call | flops 469762048 | bytes 7168000 | tf_op jit(solution)/shard_map/tok_pick/pallas_call | solution.py:81
  114.4 3.0 collective-permute-start.11
  117.4 1.1 collective-permute-start.14
  118.5 1.7 collective-permute-start.16
  121.1 17.7 %collective-permute-done.10.refs_1_ = bf16[32,7168]{1,0:T(8,128)(2,1)S(1)} collective-permute-done((bf16[32,7168]{1,0:T(8,128)(2,1)S(1)}, bf16[32,7168]{1,0:T(8,128)(2,1)S(1)}, u32[]{:S(2)}, u32[]{:S(2)}) %collective-permute-start.10) | collective-permute-done | bytes 458784 | tf_op jit(solution)/shard_map/tok_route/ppermute | solution.py:46
  140.4 16.4 %collective-permute-done.14 = bf16[32,7168]{1,0:T(8,128)(2,1)} collective-permute-done((bf16[32,7168]{1,0:T(8,128)(2,1)S(1)}, bf16[32,7168]{1,0:T(8,128)(2,1)}, u32[]{:S(2)}, u32[]{:S(2)}) %collective-permute-start.14) | collective-permute-done | bytes 458784 | tf_op jit(solution)/shard_map/tok_route/ppermute | solution.py:46
  160.3 3.1 copy-done.1
  163.4 3.1 copy-done.3
  167.5 1.0 copy-done.16
  169.6 1.0 copy-done.20
  170.6 1.0 copy-done.22
  172.6 13.9 %expert_forward.1 = (bf16[32,7168]{1,0:T(8,128)(2,1)S(1)}, bf16[32,7168]{1,0:T(8,128)(2,1)S(1)}, bf16[32,7168]{1,0:T(8,128)(2,1)S(1)}, bf16[32,7168]{1,0:T(8,128...) custom-call(bf16[32,7168]{1,0:T(8,128)(2,1)S(1)} %copy-done.14, ...), custom_call_target="tpu_custom_call" | custom-call | flops 5637144576 | bytes 29360128 | tf_op jit(solution)/shard_map/expert_forward/pallas_call | solution.py:81
  187.5 1.9 collective-permute-start.21
  190.7 18.8 %collective-permute-done.21.refs_2_ = bf16[32,7168]{1,0:T(8,128)(2,1)S(1)} collective-permute-done((bf16[32,7168]{1,0:T(8,128)(2,1)S(1)}, bf16[32,7168]{1,0:T(8,128)(2,1)S(1)}, u32[]{:S(2)}, u32[]{:S(2)}) %collective-permute-start.21) | collective-permute-done | bytes 458784 | tf_op jit(solution)/shard_map/out_route/ppermute | solution.py:46
  209.5 3.8 %collective-permute-start.23 = (bf16[32,7168]{1,0:T(8,128)(2,1)S(1)}, bf16[32,7168]{1,0:T(8,128)(2,1)S(1)}, u32[]{:S(2)}, u32[]{:S(2)}) collective-permute-start(bf16[32,7168]{1,0:T(8,128)(2,1)S(1)} %collective-permute-done.22), channel_id=1, source_target_pairs={{0,96},{16,112},{32,0},{48,16},{64,32},{80,48},{96,64},{112,80},{1... | collective-permute-start | bytes 1376264 | tf_op jit(solution)/shard_map/out_route/ppermute | solution.py:46
  213.4 1.5 collective-permute-start.26
  214.9 1.3 collective-permute-start.29
  216.3 16.8 %collective-permute-done.27.refs_6_ = bf16[32,7168]{1,0:T(8,128)(2,1)S(1)} collective-permute-done((bf16[32,7168]{1,0:T(8,128)(2,1)S(1)}, bf16[32,7168]{1,0:T(8,128)(2,1)S(1)}, u32[]{:S(2)}, u32[]{:S(2)}) %collective-permute-start.27) | collective-permute-done | bytes 458784 | tf_op jit(solution)/shard_map/out_route/ppermute | solution.py:46
  233.1 3.0 collective-permute-done.26.refs_5_
  236.1 6.9 %collective-permute-done.29.refs_7_ = bf16[32,7168]{1,0:T(8,128)(2,1)S(1)} collective-permute-done((bf16[32,7168]{1,0:T(8,128)(2,1)S(1)}, bf16[32,7168]{1,0:T(8,128)(2,1)S(1)}, u32[]{:S(2)}, u32[]{:S(2)}) %collective-permute-start.29) | collective-permute-done | bytes 458784 | tf_op jit(solution)/shard_map/out_route/ppermute | solution.py:46
  243.0 4.4 %out_route.1 = (bf16[32,7168]{1,0:T(8,128)(2,1)S(1)}, bf16[32,7168]{1,0:T(8,128)(2,1)}, bf16[32,7168]{1,0:T(8,128)(2,1)}, bf16[32,7168]{1,0:T(8,128)(2,1)}) custom-call(bf16[32,7168]{1,0:T(8,128)(2,1)S(1)} %get-tuple-element.44.refs_0_, bf16[32,7168]{1,0:T(8,128)(2,1)S(1)} %collective-permute-done.20.refs_1_, ...), custom_call_target="tpu_custom_call" | custom-call | flops 469762048 | bytes 5734400 | tf_op jit(solution)/shard_map/out_route/pallas_call | solution.py:81
  248.2 1.7 collective-permute-start.30
  249.9 2.9 collective-permute-start.31
  252.8 3.1 copy-done
  255.9 6.2 %expert_grad_hidden.1.grad = f32[256,512]{1,0:T(8,128)S(1)} custom-call(bf16[256,7168]{1,0:T(8,128)(2,1)} %bitcast.3.g, bf16[1,512,7168]{2,1,0:T(8,128)(2,1)S(1)} %copy-done), custom_call_target="tpu_custom_call" | custom-call | flops 1879048192 | bytes 11010048 | tf_op jit(solution)/shard_map/expert_grad_hidden/pallas_call | solution.py:81
  262.2 3.1 copy-done.2
  265.2 3.1 copy-done.4
  268.3 7.1 %expert_backward.1 = bf16[256,7168]{1,0:T(8,128)(2,1)S(1)} custom-call(s32[2]{0:T(128)S(1)} %pad_add_fusion.at, f32[256,512]{1,0:T(8,128)S(1)} %expert_grad_hidden.1.grad, f32[256,512]{1,0:T(8,128)S(1)} %get-tuple-element.60.act, f32[256,512]{1,0:T(8,128)S(1)} %copy-done.12, bf16[1,7168,512]{2,1,0:T(8,128)(2,1)S(1)} %copy-done.2, ...), custom_call_target="tpu_custom_call" | custom-call | flops 3758096384 | bytes 18350080 | tf_op jit(solution)/shard_map/expert_backward/pallas_call | solution.py:81
  275.4 1.9 copy-done.7
  277.3 9.5 %all-to-all-start.1 = ((bf16[16,16,7168]{2,1,0:T(8,128)(2,1)}), bf16[16,16,7168]{2,1,0:T(8,128)(2,1)}, u32[]{:S(2)}, u32[]{:S(2)}) async-start(bf16[16,16,7168]{2,1,0:T(8,128)(2,1)} %bitcast.6), calls=%async_computation.1 | async-start | bytes 7340032 | tf_op jit(solution)/shard_map/back_route/all_to_all | solution.py:372
  286.8 2.3 add_convert_fusion.1
  289.1 1.5 copy-done.6
  290.6 1.5 copy-done.10
  292.1 5.6 %shared_back.1 = (bf16[32,7168]{1,0:T(8,128)(2,1)S(1)}, bf16[32,7168]{1,0:T(8,128)(2,1)S(1)}, bf16[32,7168]{1,0:T(8,128)(2,1)S(1)}, bf16[32,7168]{1,0:T(8,128)(2,1)S(1)}) custom-call(s32[2]{0:T(128)S(1)} %pad_add_fusion.at, bf16[128,7168]{1,0:T(8,128)(2,1)S(1)} %copy-done.10, f32[128,64]{1,0:T(8,128)S(1)} %get-tuple-element.53.refs_9_.gate, ...), custom_call_target="tpu_custom_call" | custom-call | flops 352321536 | bytes 7168000 | tf_op jit(solution)/shard_map/shared_back/pallas_call | solution.py:81
  297.7 3.2 collective-permute-start.40
  302.6 2.4 collective-permute-start.33
  305.0 38.7 %collective-permute-done.40 = bf16[32,7168]{1,0:T(8,128)(2,1)S(1)} collective-permute-done((bf16[32,7168]{1,0:T(8,128)(2,1)S(1)}, bf16[32,7168]{1,0:T(8,128)(2,1)S(1)}, u32[]{:S(2)}, u32[]{:S(2)}) %collective-permute-start.40) | collective-permute-done | bytes 458784 | tf_op jit(solution)/shard_map/shared_back/ppermute | solution.py:54
  343.7 7.3 %collective-permute-start.34 = (bf16[8,7168]{1,0:T(8,128)(2,1)S(1)}, bf16[8,7168]{1,0:T(8,128)(2,1)S(1)}, u32[]{:S(2)}, u32[]{:S(2)}) collective-permute-start(bf16[8,7168]{1,0:T(8,128)(2,1)S(1)} %get-tuple-element.78), channel_id=1, source_target_pairs={{0,8},{1,9},{2,10},{3,11},{4,12},{5,13},{6,14},{7,15},{8,0},{9,1},... | collective-permute-start | bytes 344072 | tf_op jit(solution)/shard_map/out_route/ppermute | solution.py:54
  351.3 5.2 %back_sum.1 = (f32[32,7168]{1,0:T(8,128)S(1)}, bf16[32,7168]{1,0:T(8,128)(2,1)S(1)}) custom-call(bf16[256,7168]{1,0:T(8,128)(2,1)} %bitcast.5.rows, bf16[256,64]{1,0:T(8,128)(2,1)S(1)} %get-tuple-element.35._.mix), custom_call_target="tpu_custom_call" | custom-call | flops 234881024 | bytes 5046272 | tf_op jit(solution)/shard_map/back_sum/pallas_call | solution.py:81
  356.6 1.2 collective-permute-start.43
  358.4 1.3 collective-permute-start.45
  359.8 1.4 collective-permute-start.44
  361.2 1.5 collective-permute-start.37
  364.3 1.6 add_convert_fusion.2
  365.9 1.3 collective-permute-done.45
  367.2 3.5 collective-permute-done.39
  (115 shorter events, 25.8 us)
Async XLA Ops:
  9.6 8.2 %collective-permute-start.6 = (bf16[8,7296]{1,0:T(8,128)(2,1)S(1)}, bf16[8,7296]{1,0:T(8,128)(2,1)S(1)}, u32[]{:S(2)}, u32[]{:S(2)}) collective-permute-start(bf16[8,7296]{1,0:T(8,128)(2,1)S(1)} %get-tuple-element.81), channel_id=1, source_target_pairs={{0,12},{1,13},{2,14},{3,15},{4,0},{5,1},{6,2},{7,3},{8,4},{9,5},{1... | collective-permute-start | bytes 350216 | tf_op jit(solution)/shard_map/tok_gather/ppermute | solution.py:54
  12.5 7.4 %collective-permute-start.5 = (bf16[8,7296]{1,0:T(8,128)(2,1)S(1)}, bf16[8,7296]{1,0:T(8,128)(2,1)S(1)}, u32[]{:S(2)}, u32[]{:S(2)}) collective-permute-start(bf16[8,7296]{1,0:T(8,128)(2,1)S(1)} %get-tuple-element.81), channel_id=1, source_target_pairs={{0,8},{1,9},{2,10},{3,11},{4,12},{5,13},{6,14},{7,15},{8,0},{9,1},... | collective-permute-start | bytes 350216 | tf_op jit(solution)/shard_map/tok_gather/ppermute | solution.py:54
  13.3 7.9 %collective-permute-start.4 = (bf16[8,7296]{1,0:T(8,128)(2,1)S(1)}, bf16[8,7296]{1,0:T(8,128)(2,1)S(1)}, u32[]{:S(2)}, u32[]{:S(2)}) collective-permute-start(bf16[8,7296]{1,0:T(8,128)(2,1)S(1)} %get-tuple-element.81), channel_id=1, source_target_pairs={{0,4},{1,5},{2,6},{3,7},{4,8},{5,9},{6,10},{7,11},{8,12},{9,13},{1... | collective-permute-start | bytes 350216 | tf_op jit(solution)/shard_map/tok_gather/ppermute | solution.py:54
  14.2 7.3 %collective-permute-start.2 = (bf16[8,7296]{1,0:T(8,128)(2,1)S(1)}, bf16[8,7296]{1,0:T(8,128)(2,1)S(1)}, u32[]{:S(2)}, u32[]{:S(2)}) collective-permute-start(bf16[8,7296]{1,0:T(8,128)(2,1)S(1)} %get-tuple-element.82), channel_id=1, source_target_pairs={{0,96},{16,112},{32,0},{48,16},{64,32},{80,48},{96,64},{112,80},{1... | collective-permute-start | bytes 350216 | tf_op jit(solution)/shard_map/cot_gather/ppermute | solution.py:46
  17.2 6.6 %collective-permute-start.1 = (bf16[8,7296]{1,0:T(8,128)(2,1)S(1)}, bf16[8,7296]{1,0:T(8,128)(2,1)S(1)}, u32[]{:S(2)}, u32[]{:S(2)}) collective-permute-start(bf16[8,7296]{1,0:T(8,128)(2,1)S(1)} %get-tuple-element.82), channel_id=1, source_target_pairs={{0,64},{16,80},{32,96},{48,112},{64,0},{80,16},{96,32},{112,48},{1... | collective-permute-start | bytes 350216 | tf_op jit(solution)/shard_map/cot_gather/ppermute | solution.py:46
  17.8 7.2 %collective-permute-start = (bf16[8,7296]{1,0:T(8,128)(2,1)S(1)}, bf16[8,7296]{1,0:T(8,128)(2,1)S(1)}, u32[]{:S(2)}, u32[]{:S(2)}) collective-permute-start(bf16[8,7296]{1,0:T(8,128)(2,1)S(1)} %get-tuple-element.82), channel_id=1, source_target_pairs={{0,32},{16,48},{32,64},{48,80},{64,96},{80,112},{96,0},{112,16},{1... | collective-permute-start | bytes 350216 | tf_op jit(solution)/shard_map/cot_gather/ppermute | solution.py:46
  26.1 1.9 collective-permute-start.3
  31.6 1.9 copy-start.8
  33.5 219.3 %all-to-all-start = ((bf16[16,16,7168]{2,1,0:T(8,128)(2,1)}), bf16[16,16,7168]{2,1,0:T(8,128)(2,1)}, u32[]{:S(2)}, u32[]{:S(2)}) async-start(bf16[16,16,7168]{2,1,0:T(8,128)(2,1)} %bitcast.7), calls=%async_computation | async-start | bytes 7340032 | tf_op jit(solution)/shard_map/cot_route/all_to_all | solution.py:306
  41.3 247.7 %all-gather.2.cloned.1.call-start = ((), (), s32[]{:S(2)}) async-start(), calls=%async_computation.2 | async-start | bytes 1949696 | tf_op jit(solution)/shard_map/cot_gather/all_gather | solution.py:293
  41.4 52.9 %collective-permute-start.9 = (bf16[32,7296]{1,0:T(8,128)(2,1)S(1)}, bf16[32,7296]{1,0:T(8,128)(2,1)S(1)}, u32[]{:S(2)}, u32[]{:S(2)}) collective-permute-start(bf16[32,7296]{1,0:T(8,128)(2,1)S(1)} %get-tuple-element.79.b0.i0), channel_id=1, source_target_pairs={{0,3},{1,0},{2,1},{3,2},{4,7},{5,4},{6,5},{7,6},{8,11},{9,8},{10,9... | collective-permute-start | bytes 1400840 | tf_op jit(solution)/shard_map/tok_gather/ppermute | solution.py:58
  44.5 53.0 %collective-permute-start.8 = (bf16[32,7296]{1,0:T(8,128)(2,1)S(1)}, bf16[32,7296]{1,0:T(8,128)(2,1)S(1)}, u32[]{:S(2)}, u32[]{:S(2)}) collective-permute-start(bf16[32,7296]{1,0:T(8,128)(2,1)S(1)} %get-tuple-element.79.b0.i0), channel_id=1, source_target_pairs={{0,2},{1,3},{2,0},{3,1},{4,6},{5,7},{6,4},{7,5},{8,10},{9,11},{10,... | collective-permute-start | bytes 1400840 | tf_op jit(solution)/shard_map/tok_gather/ppermute | solution.py:58
  45.4 59.6 %collective-permute-start.7 = (bf16[32,7296]{1,0:T(8,128)(2,1)S(1)}, bf16[32,7296]{1,0:T(8,128)(2,1)}, u32[]{:S(2)}, u32[]{:S(2)}) collective-permute-start(bf16[32,7296]{1,0:T(8,128)(2,1)S(1)} %get-tuple-element.79.b0.i0), channel_id=1, source_target_pairs={{0,1},{1,2},{2,3},{3,0},{4,5},{5,6},{6,7},{7,4},{8,9},{9,10},{10,1... | collective-permute-start | bytes 1400840 | tf_op jit(solution)/shard_map/tok_gather/ppermute | solution.py:58
  105.0 1.5 copy-start.5
  114.4 24.5 %collective-permute-start.10 = (bf16[32,7168]{1,0:T(8,128)(2,1)S(1)}, bf16[32,7168]{1,0:T(8,128)(2,1)S(1)}, u32[]{:S(2)}, u32[]{:S(2)}) collective-permute-start(bf16[32,7168]{1,0:T(8,128)(2,1)S(1)} %get-tuple-element.37), channel_id=1, source_target_pairs={{0,32},{16,48},{32,64},{48,80},{64,96},{80,112},{96,0},{112,16},{1... | collective-permute-start | bytes 1376264 | tf_op jit(solution)/shard_map/tok_route/ppermute | solution.py:46
  114.4 25.3 %collective-permute-start.11 = (bf16[32,7168]{1,0:T(8,128)(2,1)S(1)}, bf16[32,7168]{1,0:T(8,128)(2,1)S(1)}, u32[]{:S(2)}, u32[]{:S(2)}) collective-permute-start(bf16[32,7168]{1,0:T(8,128)(2,1)S(1)} %get-tuple-element.38), channel_id=1, source_target_pairs={{0,64},{16,80},{32,96},{48,112},{64,0},{80,16},{96,32},{112,48},{1... | collective-permute-start | bytes 1376264 | tf_op jit(solution)/shard_map/tok_route/ppermute | solution.py:46
  117.4 39.5 %collective-permute-start.14 = (bf16[32,7168]{1,0:T(8,128)(2,1)S(1)}, bf16[32,7168]{1,0:T(8,128)(2,1)}, u32[]{:S(2)}, u32[]{:S(2)}) collective-permute-start(bf16[32,7168]{1,0:T(8,128)(2,1)S(1)} %get-tuple-element.41), channel_id=1, source_target_pairs={{0,32},{16,48},{32,64},{48,80},{64,96},{80,112},{96,0},{112,16},{1... | collective-permute-start | bytes 1376264 | tf_op jit(solution)/shard_map/tok_route/ppermute | solution.py:46
  118.5 38.4 %collective-permute-start.16 = (bf16[32,7168]{1,0:T(8,128)(2,1)S(1)}, bf16[32,7168]{1,0:T(8,128)(2,1)}, u32[]{:S(2)}, u32[]{:S(2)}) collective-permute-start(bf16[32,7168]{1,0:T(8,128)(2,1)S(1)} %get-tuple-element.42), channel_id=1, source_target_pairs={{0,64},{16,80},{32,96},{48,112},{64,0},{80,16},{96,32},{112,48},{1... | collective-permute-start | bytes 1376264 | tf_op jit(solution)/shard_map/tok_route/ppermute | solution.py:46
  120.2 37.2 %collective-permute-start.18 = (bf16[32,7168]{1,0:T(8,128)(2,1)S(1)}, bf16[32,7168]{1,0:T(8,128)(2,1)}, u32[]{:S(2)}, u32[]{:S(2)}) collective-permute-start(bf16[32,7168]{1,0:T(8,128)(2,1)S(1)} %get-tuple-element.43), channel_id=1, source_target_pairs={{0,96},{16,112},{32,0},{48,16},{64,32},{80,48},{96,64},{112,80},{1... | collective-permute-start | bytes 1376264 | tf_op jit(solution)/shard_map/tok_route/ppermute | solution.py:46
  139.7 17.8 %collective-permute-start.12 = (bf16[32,7168]{1,0:T(8,128)(2,1)}, bf16[32,7168]{1,0:T(8,128)(2,1)S(1)}, u32[]{:S(2)}, u32[]{:S(2)}) collective-permute-start(bf16[32,7168]{1,0:T(8,128)(2,1)} %get-tuple-element.39), channel_id=1, source_target_pairs={{0,96},{16,112},{32,0},{48,16},{64,32},{80,48},{96,64},{112,80},{1... | collective-permute-start | bytes 1376264 | tf_op jit(solution)/shard_map/tok_route/ppermute | solution.py:46
  140.4 17.9 %collective-permute-start.13 = (bf16[32,7168]{1,0:T(8,128)(2,1)}, bf16[32,7168]{1,0:T(8,128)(2,1)S(1)}, u32[]{:S(2)}, u32[]{:S(2)}) collective-permute-start(bf16[32,7168]{1,0:T(8,128)(2,1)} %get-tuple-element.40), channel_id=1, source_target_pairs={{0,16},{16,0},{32,48},{48,32},{64,80},{80,64},{96,112},{112,96},{1... | collective-permute-start | bytes 1376264 | tf_op jit(solution)/shard_map/tok_route/ppermute | solution.py:50
  156.9 2.6 collective-permute-start.15
  156.9 3.4 collective-permute-start.17
  157.4 3.0 collective-permute-start.19
  160.3 3.1 copy-start.1
  163.4 3.1 copy-start.3
  170.6 1.0 copy-start.22
  172.6 70.4 %copy-start.9 = (bf16[64,7168]{1,0:T(8,128)(2,1)S(1)}, bf16[64,7168]{1,0:T(8,128)(2,1)}, u32[]{:S(2)}) copy-start(bf16[64,7168]{1,0:T(8,128)(2,1)} %sd.1) | copy-start | bytes 2752516
  187.4 2.8 collective-permute-start.20
  187.5 22.0 %collective-permute-start.21 = (bf16[32,7168]{1,0:T(8,128)(2,1)S(1)}, bf16[32,7168]{1,0:T(8,128)(2,1)S(1)}, u32[]{:S(2)}, u32[]{:S(2)}) collective-permute-start(bf16[32,7168]{1,0:T(8,128)(2,1)S(1)} %get-tuple-element.46), channel_id=1, source_target_pairs={{0,96},{16,112},{32,0},{48,16},{64,32},{80,48},{96,64},{112,80},{1... | collective-permute-start | bytes 1376264 | tf_op jit(solution)/shard_map/out_route/ppermute | solution.py:46
  189.4 20.1 %collective-permute-start.22 = (bf16[32,7168]{1,0:T(8,128)(2,1)S(1)}, bf16[32,7168]{1,0:T(8,128)(2,1)S(1)}, u32[]{:S(2)}, u32[]{:S(2)}) collective-permute-start(bf16[32,7168]{1,0:T(8,128)(2,1)S(1)} %get-tuple-element.47), channel_id=1, source_target_pairs={{0,16},{16,0},{32,48},{48,32},{64,80},{80,64},{96,112},{112,96},{1... | collective-permute-start | bytes 1376264 | tf_op jit(solution)/shard_map/out_route/ppermute | solution.py:50
  189.6 23.7 %collective-permute-start.25 = (bf16[32,7168]{1,0:T(8,128)(2,1)S(1)}, bf16[32,7168]{1,0:T(8,128)(2,1)S(1)}, u32[]{:S(2)}, u32[]{:S(2)}) collective-permute-start(bf16[32,7168]{1,0:T(8,128)(2,1)S(1)} %get-tuple-element.49), channel_id=1, source_target_pairs={{0,16},{16,0},{32,48},{48,32},{64,80},{80,64},{96,112},{112,96},{1... | collective-permute-start | bytes 1376264 | tf_op jit(solution)/shard_map/out_route/ppermute | solution.py:50
  189.9 25.0 %collective-permute-start.28 = (bf16[32,7168]{1,0:T(8,128)(2,1)S(1)}, bf16[32,7168]{1,0:T(8,128)(2,1)S(1)}, u32[]{:S(2)}, u32[]{:S(2)}) collective-permute-start(bf16[32,7168]{1,0:T(8,128)(2,1)S(1)} %get-tuple-element.51), channel_id=1, source_target_pairs={{0,16},{16,0},{32,48},{48,32},{64,80},{80,64},{96,112},{112,96},{1... | collective-permute-start | bytes 1376264 | tf_op jit(solution)/shard_map/out_route/ppermute | solution.py:50
  190.2 26.1 %collective-permute-start.24 = (bf16[32,7168]{1,0:T(8,128)(2,1)S(1)}, bf16[32,7168]{1,0:T(8,128)(2,1)S(1)}, u32[]{:S(2)}, u32[]{:S(2)}) collective-permute-start(bf16[32,7168]{1,0:T(8,128)(2,1)S(1)} %get-tuple-element.48), channel_id=1, source_target_pairs={{0,64},{16,80},{32,96},{48,112},{64,0},{80,16},{96,32},{112,48},{1... | collective-permute-start | bytes 1376264 | tf_op jit(solution)/shard_map/out_route/ppermute | solution.py:46
  209.5 23.6 %collective-permute-start.27 = (bf16[32,7168]{1,0:T(8,128)(2,1)S(1)}, bf16[32,7168]{1,0:T(8,128)(2,1)S(1)}, u32[]{:S(2)}, u32[]{:S(2)}) collective-permute-start(bf16[32,7168]{1,0:T(8,128)(2,1)S(1)} %get-tuple-element.50), channel_id=1, source_target_pairs={{0,32},{16,48},{32,64},{48,80},{64,96},{80,112},{96,0},{112,16},{1... | collective-permute-start | bytes 1376264 | tf_op jit(solution)/shard_map/out_route/ppermute | solution.py:46
  209.5 23.6 %collective-permute-start.23 = (bf16[32,7168]{1,0:T(8,128)(2,1)S(1)}, bf16[32,7168]{1,0:T(8,128)(2,1)S(1)}, u32[]{:S(2)}, u32[]{:S(2)}) collective-permute-start(bf16[32,7168]{1,0:T(8,128)(2,1)S(1)} %collective-permute-done.22), channel_id=1, source_target_pairs={{0,96},{16,112},{32,0},{48,16},{64,32},{80,48},{96,64},{112,80},{1... | collective-permute-start | bytes 1376264 | tf_op jit(solution)/shard_map/out_route/ppermute | solution.py:46
  213.4 22.8 %collective-permute-start.26 = (bf16[32,7168]{1,0:T(8,128)(2,1)S(1)}, bf16[32,7168]{1,0:T(8,128)(2,1)S(1)}, u32[]{:S(2)}, u32[]{:S(2)}) collective-permute-start(bf16[32,7168]{1,0:T(8,128)(2,1)S(1)} %collective-permute-done.25), channel_id=1, source_target_pairs={{0,64},{16,80},{32,96},{48,112},{64,0},{80,16},{96,32},{112,48},{1... | collective-permute-start | bytes 1376264 | tf_op jit(solution)/shard_map/out_route/ppermute | solution.py:46
  214.9 28.1 %collective-permute-start.29 = (bf16[32,7168]{1,0:T(8,128)(2,1)S(1)}, bf16[32,7168]{1,0:T(8,128)(2,1)S(1)}, u32[]{:S(2)}, u32[]{:S(2)}) collective-permute-start(bf16[32,7168]{1,0:T(8,128)(2,1)S(1)} %collective-permute-done.28), channel_id=1, source_target_pairs={{0,32},{16,48},{32,64},{48,80},{64,96},{80,112},{96,0},{112,16},{1... | collective-permute-start | bytes 1376264 | tf_op jit(solution)/shard_map/out_route/ppermute | solution.py:46
  248.2 38.6 %collective-permute-start.30 = (bf16[32,7168]{1,0:T(8,128)(2,1)}, bf16[32,7168]{1,0:T(8,128)(2,1)}, u32[]{:S(2)}, u32[]{:S(2)}) collective-permute-start(bf16[32,7168]{1,0:T(8,128)(2,1)} %get-tuple-element.56), channel_id=1, source_target_pairs={{0,3},{1,0},{2,1},{3,2},{4,7},{5,4},{6,5},{7,6},{8,11},{9,8},{10,9... | collective-permute-start | bytes 1376264 | tf_op jit(solution)/shard_map/out_route/ppermute | solution.py:58
  249.9 36.8 %collective-permute-start.31 = (bf16[32,7168]{1,0:T(8,128)(2,1)}, bf16[32,7168]{1,0:T(8,128)(2,1)}, u32[]{:S(2)}, u32[]{:S(2)}) collective-permute-start(bf16[32,7168]{1,0:T(8,128)(2,1)} %get-tuple-element.57), channel_id=1, source_target_pairs={{0,2},{1,3},{2,0},{3,1},{4,6},{5,7},{6,4},{7,5},{8,10},{9,11},{10,... | collective-permute-start | bytes 1376264 | tf_op jit(solution)/shard_map/out_route/ppermute | solution.py:58
  252.8 34.0 %collective-permute-start.32 = (bf16[32,7168]{1,0:T(8,128)(2,1)}, bf16[32,7168]{1,0:T(8,128)(2,1)}, u32[]{:S(2)}, u32[]{:S(2)}) collective-permute-start(bf16[32,7168]{1,0:T(8,128)(2,1)} %get-tuple-element.58), channel_id=1, source_target_pairs={{0,1},{1,2},{2,3},{3,0},{4,5},{5,6},{6,7},{7,4},{8,9},{9,10},{10,1... | collective-permute-start | bytes 1376264 | tf_op jit(solution)/shard_map/out_route/ppermute | solution.py:58
  252.8 3.1 copy-start
  255.9 6.3 %copy-start.12 = (f32[256,512]{1,0:T(8,128)S(1)}, f32[256,512]{1,0:T(8,128)}, u32[]{:S(2)}) copy-start(f32[256,512]{1,0:T(8,128)} %copy-done.11) | copy-start | bytes 1572868
  262.1 3.1 copy-start.2
  265.2 3.1 copy-start.4
  275.4 1.9 copy-start.7
  277.3 9.5 %copy-start.26 = (bf16[32,7168]{1,0:T(8,128)(2,1)S(1)}, bf16[32,7168]{1,0:T(8,128)(2,1)}, u32[]{:S(2)}) copy-start(bf16[32,7168]{1,0:T(8,128)(2,1)} %copy-done.25) | copy-start | bytes 1376260
  277.3 74.0 %all-to-all-start.1 = ((bf16[16,16,7168]{2,1,0:T(8,128)(2,1)}), bf16[16,16,7168]{2,1,0:T(8,128)(2,1)}, u32[]{:S(2)}, u32[]{:S(2)}) async-start(bf16[16,16,7168]{2,1,0:T(8,128)(2,1)} %bitcast.6), calls=%async_computation.1 | async-start | bytes 7340032 | tf_op jit(solution)/shard_map/back_route/all_to_all | solution.py:372
  289.1 1.5 copy-start.6
  290.6 1.5 copy-start.10
  292.1 10.5 %copy-start.27 = (bf16[32,7168]{1,0:T(8,128)(2,1)S(1)}, bf16[32,7168]{1,0:T(8,128)(2,1)}, u32[]{:S(2)}) copy-start(bf16[32,7168]{1,0:T(8,128)(2,1)} %add_convert_fusion.1) | copy-start | bytes 1376260
  297.7 46.1 %collective-permute-start.40 = (bf16[32,7168]{1,0:T(8,128)(2,1)S(1)}, bf16[32,7168]{1,0:T(8,128)(2,1)S(1)}, u32[]{:S(2)}, u32[]{:S(2)}) collective-permute-start(bf16[32,7168]{1,0:T(8,128)(2,1)S(1)} %get-tuple-element.65), channel_id=1, source_target_pairs={{0,12},{1,13},{2,14},{3,15},{4,0},{5,1},{6,2},{7,3},{8,4},{9,5},{1... | collective-permute-start | bytes 1376264 | tf_op jit(solution)/shard_map/shared_back/ppermute | solution.py:54
  300.9 50.2 %collective-permute-start.41 = (bf16[32,7168]{1,0:T(8,128)(2,1)S(1)}, bf16[32,7168]{1,0:T(8,128)(2,1)S(1)}, u32[]{:S(2)}, u32[]{:S(2)}) collective-permute-start(bf16[32,7168]{1,0:T(8,128)(2,1)S(1)} %get-tuple-element.66), channel_id=1, source_target_pairs={{0,8},{1,9},{2,10},{3,11},{4,12},{5,13},{6,14},{7,15},{8,0},{9,1},... | collective-permute-start | bytes 1376264 | tf_op jit(solution)/shard_map/shared_back/ppermute | solution.py:54
  301.7 49.3 %collective-permute-start.42 = (bf16[32,7168]{1,0:T(8,128)(2,1)S(1)}, bf16[32,7168]{1,0:T(8,128)(2,1)S(1)}, u32[]{:S(2)}, u32[]{:S(2)}) collective-permute-start(bf16[32,7168]{1,0:T(8,128)(2,1)S(1)} %get-tuple-element.67), channel_id=1, source_target_pairs={{0,4},{1,5},{2,6},{3,7},{4,8},{5,9},{6,10},{7,11},{8,12},{9,13},{1... | collective-permute-start | bytes 1376264 | tf_op jit(solution)/shard_map/shared_back/ppermute | solution.py:54
  302.6 57.2 %collective-permute-start.33 = (bf16[8,7168]{1,0:T(8,128)(2,1)S(1)}, bf16[8,7168]{1,0:T(8,128)(2,1)S(1)}, u32[]{:S(2)}, u32[]{:S(2)}) collective-permute-start(bf16[8,7168]{1,0:T(8,128)(2,1)S(1)} %get-tuple-element.76), channel_id=1, source_target_pairs={{0,12},{1,13},{2,14},{3,15},{4,0},{5,1},{6,2},{7,3},{8,4},{9,5},{1... | collective-permute-start | bytes 344072 | tf_op jit(solution)/shard_map/out_route/ppermute | solution.py:54
  305.0 56.2 %collective-permute-start.35 = (bf16[8,7168]{1,0:T(8,128)(2,1)S(1)}, bf16[8,7168]{1,0:T(8,128)(2,1)S(1)}, u32[]{:S(2)}, u32[]{:S(2)}) collective-permute-start(bf16[8,7168]{1,0:T(8,128)(2,1)S(1)} %get-tuple-element.77), channel_id=1, source_target_pairs={{0,4},{1,5},{2,6},{3,7},{4,8},{5,9},{6,10},{7,11},{8,12},{9,13},{1... | collective-permute-start | bytes 344072 | tf_op jit(solution)/shard_map/out_route/ppermute | solution.py:54
  343.7 19.0 %collective-permute-start.34 = (bf16[8,7168]{1,0:T(8,128)(2,1)S(1)}, bf16[8,7168]{1,0:T(8,128)(2,1)S(1)}, u32[]{:S(2)}, u32[]{:S(2)}) collective-permute-start(bf16[8,7168]{1,0:T(8,128)(2,1)S(1)} %get-tuple-element.78), channel_id=1, source_target_pairs={{0,8},{1,9},{2,10},{3,11},{4,12},{5,13},{6,14},{7,15},{8,0},{9,1},... | collective-permute-start | bytes 344072 | tf_op jit(solution)/shard_map/out_route/ppermute | solution.py:54
  356.5 1.9 collective-permute-start.36
  356.6 6.7 %collective-permute-start.43 = (bf16[8,7168]{1,0:T(8,128)(2,1)S(1)}, bf16[8,7168]{1,0:T(8,128)(2,1)S(1)}, u32[]{:S(2)}, u32[]{:S(2)}) collective-permute-start(bf16[8,7168]{1,0:T(8,128)(2,1)S(1)} %get-tuple-element.73), channel_id=1, source_target_pairs={{0,3},{1,0},{2,1},{3,2},{4,7},{5,4},{6,5},{7,6},{8,11},{9,8},{10,9... | collective-permute-start | bytes 344072 | tf_op jit(solution)/shard_map/shared_back/ppermute | solution.py:58
  358.4 8.9 %collective-permute-start.45 = (bf16[8,7168]{1,0:T(8,128)(2,1)S(1)}, bf16[8,7168]{1,0:T(8,128)(2,1)S(1)}, u32[]{:S(2)}, u32[]{:S(2)}) collective-permute-start(bf16[8,7168]{1,0:T(8,128)(2,1)S(1)} %get-tuple-element.74), channel_id=1, source_target_pairs={{0,1},{1,2},{2,3},{3,0},{4,5},{5,6},{6,7},{7,4},{8,9},{9,10},{10,1... | collective-permute-start | bytes 344072 | tf_op jit(solution)/shard_map/shared_back/ppermute | solution.py:58
  359.8 7.4 %collective-permute-start.44 = (bf16[8,7168]{1,0:T(8,128)(2,1)S(1)}, bf16[8,7168]{1,0:T(8,128)(2,1)S(1)}, u32[]{:S(2)}, u32[]{:S(2)}) collective-permute-start(bf16[8,7168]{1,0:T(8,128)(2,1)S(1)} %get-tuple-element.75), channel_id=1, source_target_pairs={{0,2},{1,3},{2,0},{3,1},{4,6},{5,7},{6,4},{7,5},{8,10},{9,11},{10,... | collective-permute-start | bytes 344072 | tf_op jit(solution)/shard_map/shared_back/ppermute | solution.py:58
  361.2 6.0 %collective-permute-start.37 = (bf16[8,7168]{1,0:T(8,128)(2,1)S(1)}, bf16[8,7168]{1,0:T(8,128)(2,1)S(1)}, u32[]{:S(2)}, u32[]{:S(2)}) collective-permute-start(bf16[8,7168]{1,0:T(8,128)(2,1)S(1)} %get-tuple-element.70), channel_id=1, source_target_pairs={{0,96},{16,112},{32,0},{48,16},{64,32},{80,48},{96,64},{112,80},{1... | collective-permute-start | bytes 344072 | tf_op jit(solution)/shard_map/back_sum/ppermute | solution.py:46
  362.7 8.0 %collective-permute-start.39 = (bf16[8,7168]{1,0:T(8,128)(2,1)S(1)}, bf16[8,7168]{1,0:T(8,128)(2,1)S(1)}, u32[]{:S(2)}, u32[]{:S(2)}) collective-permute-start(bf16[8,7168]{1,0:T(8,128)(2,1)S(1)} %get-tuple-element.71), channel_id=1, source_target_pairs={{0,32},{16,48},{32,64},{48,80},{64,96},{80,112},{96,0},{112,16},{1... | collective-permute-start | bytes 344072 | tf_op jit(solution)/shard_map/back_sum/ppermute | solution.py:46
  363.3 7.5 %collective-permute-start.38 = (bf16[8,7168]{1,0:T(8,128)(2,1)S(1)}, bf16[8,7168]{1,0:T(8,128)(2,1)S(1)}, u32[]{:S(2)}, u32[]{:S(2)}) collective-permute-start(bf16[8,7168]{1,0:T(8,128)(2,1)S(1)} %get-tuple-element.72), channel_id=1, source_target_pairs={{0,64},{16,80},{32,96},{48,112},{64,0},{80,16},{96,32},{112,48},{1... | collective-permute-start | bytes 344072 | tf_op jit(solution)/shard_map/back_sum/ppermute | solution.py:46
  (13 other events, 11.3 us)
Sparse Core Ops, SparseCore 0:
  157.6 47.8 all-gather.1
where the time goes:
time: 381 us; the launch traced here: 378 us
  waiting for transfers between devices  186 us (49%)
  starting transfers between devices  75.5 us (20%)
  Pallas kernels  53.1 us (14%)
  local copies, waits for them, and re-layouts  40.6 us (11%)
  between operations  14.3 us (4%)
  other arithmetic  8.53 us (2%)
    ppermute x18, waiting for transfers between devices, move_y(): lax.ppermute(v, 'grp', [(y * 2 + c, (y + k) % N_Y * 2 + c) for y in range...  87.2 us
    ppermute x9, waiting for transfers between devices, move_z(): lax.ppermute(v, 'exp', [(x * 4 + z, x * 4 + (z + k) % N_Z) for x in range...  55.5 us
    pallas_call x8, Pallas kernels, call(): pl.pallas_call(kernel, grid=(grid,), in_specs=in_specs, out_specs=[pl.Blo...  53.1 us
    ppermute x9, waiting for transfers between devices, move_x(): lax.ppermute(v, 'exp', [(x * 4 + z, (x + k) % N_X * 4 + z) for x in range...  40.8 us
    unnamed x58, local copies, waits for them, and re-layouts  40.6 us
    ppermute x18, starting transfers between devices, move_y(): lax.ppermute(v, 'grp', [(y * 2 + c, (y + k) % N_Y * 2 + c) for y in range...  23.9 us
    ppermute x9, starting transfers between devices, move_x(): lax.ppermute(v, 'exp', [(x * 4 + z, (x + k) % N_X * 4 + z) for x in range...  19.2 us
    ppermute x9, starting transfers between devices, move_z(): lax.ppermute(v, 'exp', [(x * 4 + z, x * 4 + (z + k) % N_Z) for x in range...  13.5 us
  transfers between devices with their start and end apart: 49, of which 21 were waited for; matrix products, arithmetic and copies ran while one was open for 2% of the time, Pallas kernels for 13%

commit v1 on v0

v1 whole, which is shorter than its diff:
```python
import functools

import jax
import jax.numpy as jnp
from jax import lax
from jax.experimental import pallas as pl
from jax.experimental.pallas import tpu as pltpu
from jax.sharding import PartitionSpec as P

SPLIT = 2
TOP = 8
CAP = 2
N_Y, N_X, N_Z = 4, 4, 4
INFO = 128
BLK = 1792

F32, BF16, I32 = jnp.float32, jnp.bfloat16, jnp.int32


def silu_parts(values):
    logistic = 1.0 / (1.0 + jnp.exp(-values))
    return values * logistic, logistic * (1.0 + values * (1.0 - logistic))


def dot(a, b):
    return jnp.dot(a, b, preferred_element_type=F32)


def dot_t(a, b):
    return lax.dot_general(a, b, (((1,), (1,)), ((), ())), preferred_element_type=F32)


def dot_a(a, b):
    return lax.dot_general(a, b, (((0,), (0,)), ((), ())), preferred_element_type=F32)


def turn(order, v):
    return jnp.dot(order, v, precision=lax.Precision.HIGHEST, preferred_element_type=F32)


def grid_ids(rows, cols):
    return lax.broadcasted_iota(I32, (rows, cols), 0), lax.broadcasted_iota(I32, (rows, cols), 1)


def move_y(v, k):
    return lax.ppermute(v, "grp", [(y * 2 + c, (y + k) % N_Y * 2 + c) for y in range(N_Y) for c in range(2)])


def swap_core(v):
    return lax.ppermute(v, "grp", [(g, g ^ 1) for g in range(N_Y * 2)])


def move_plane(v, k, turned):
    pairs = []
    for grp in range(N_Y * 2):
        for x in range(N_X):
            for z in range(N_Z):
                along_x = (grp % 2 == 0) != turned
                to = (x + k) % N_X * 4 + z if along_x else x * 4 + (z + k) % N_Z
                pairs.append((grp * 16 + x * 4 + z, grp * 16 + to))
    return lax.ppermute(v, ("grp", "exp"), pairs)


def move_a(v, k):
    return move_plane(v, k, False)


def move_b(v, k):
    return move_plane(v, k, True)


def ring(move, v):
    return [v] + [move(v, k) for k in (1, 2, 3)]


def ring_sum(move, parts):
    total = parts[0].astype(F32)
    for k in (1, 2, 3):
        total = total + move(parts[k], -k).astype(F32)
    return total


def call(kernel, grid, ins, outs, scratch, flops, moved, after=()):
    in_specs = [pl.BlockSpec(memory_space=pl.ANY)] * len(after) + [
        pl.BlockSpec(memory_space=pltpu.SMEM) if block == "smem" else pl.BlockSpec(block, at) for _, block, at in ins
    ]
    skip = len(after)
    return pl.pallas_call(
        lambda *refs: kernel(*refs[skip:]),
        grid=(grid,),
        in_specs=in_specs,
        out_specs=[pl.BlockSpec(block, at) for _, _, block, at in outs],
        out_shape=[jax.ShapeDtypeStruct(shape, dtype) for shape, dtype, _, _ in outs],
        scratch_shapes=scratch,
        compiler_params=pltpu.CompilerParams(vmem_limit_bytes=60 * 1024 * 1024),
        cost_estimate=pl.CostEstimate(flops=flops, bytes_accessed=moved, transcendentals=0),
    )(*after, *[a for a, _, _ in ins])


COL = lambda i: (0, i)
FIX = lambda i: (0, 0)


def slots_of(info, expert, block, rank):
    rows = info.shape[0]
    a, b = grid_ids(2 * TOP, INFO)
    across = dot_t((a == b).astype(BF16), info)
    want = expert.astype(F32)
    named = jnp.zeros(expert.shape, F32)
    scale = jnp.zeros(expert.shape, F32)
    for k in range(TOP):
        hit = across[k : k + 1, :] == want
        named = named + jnp.where(hit, 1.0, 0.0)
        scale = scale + jnp.where(hit, across[TOP + k : TOP + k + 1, :], 0.0)
    a, b = grid_ids(rows, rows)
    earlier = jnp.where(((a >> 3) == (b >> 3)) & (a < b), 1.0, 0.0).astype(BF16)
    before = dot(named.astype(BF16), earlier)
    _, row = grid_ids(*expert.shape)
    taken = (named > 0.5) & (before == rank.astype(F32)) & ((row >> 3) == block)
    return jnp.where(taken, 1.0, 0.0).astype(BF16), jnp.where(taken, scale * (1.0 / 256.0), 0.0).astype(BF16)


def cot_pick_kernel(at, g0, g1, i0, i1, sent, mix, hot):
    @pl.when(pl.program_id(0) == 0)
    def _():
        slot, _ = grid_ids(256, 64)
        info = jnp.concatenate([i0[...], i1[...]], axis=0)
        one, scaled = slots_of(info, at[0] * 8 + (slot >> 5), (slot >> 1) & 7, slot & 1)
        hot[...] = one
        mix[...] = scaled

    sent[...] = dot(hot[...], jnp.concatenate([g0[...], g1[...]], axis=0)).astype(BF16)


def widen_kernel(tok, cot, routes, weights, all_, g):
    width = tok.shape[1]
    at, to = grid_ids(TOP, INFO)
    place = lambda v, n: dot(v.astype(F32).astype(BF16), jnp.where(to == at + n, 1.0, 0.0).astype(BF16))
    info = (place(routes[...], 0) + place(weights[...], TOP)).astype(BF16)
    all_[:, :width] = cot[...]
    all_[:, width : 2 * width] = tok[...]
    all_[:, 2 * width :] = info
    g[:, :width] = cot[...]
    g[:, width:] = info


def tok_pick_kernel(at, b0, b1, b2, b3, i0, i1, i2, i3, *rest):
    sent, (over, mix, hot) = rest[:4], rest[4:]

    @pl.when(pl.program_id(0) == 0)
    def _():
        slot, _ = grid_ids(256, 128)
        info = jnp.concatenate([i0[...], i1[...], i2[...], i3[...]], axis=0)
        y = (at[0] // 2 + (slot >> 5)) & 3
        c = (at[0] + (slot >> 7)) & 1
        one, scaled = slots_of(info, (y * 2 + c) * 8 + at[1] // SPLIT, (slot >> 1) & 15, slot & 1)
        hot[...] = one
        mix[...] = scaled

    picked = dot(hot[...], jnp.concatenate([b0[...], b1[...], b2[...], b3[...]], axis=0)).astype(BF16)
    for n in range(4):
        sent[n][...] = picked[n * 32 : n * 32 + 32]
    over[...] = picked[128:]


def order_of(at):
    to, i = grid_ids(256, 256)
    from_1 = ((at[0] + (i >> 7)) & 1) == 1
    inner, outer = (i >> 1) & 3, (i >> 3) & 3
    x = (at[1] // 4 - jnp.where(from_1, outer, inner)) & 3
    z = (at[1] - jnp.where(from_1, inner, outer)) & 3
    return jnp.where(to == ((x * 4 + z) * 8 + (i >> 5)) * 2 + (i & 1), 1.0, 0.0)


def forward_kernel(at, *refs):
    xs, (gw, uw, hid, act, slope, acc_g, acc_u) = refs[:8], refs[8:]
    step = pl.program_id(0)

    @pl.when(step == 0)
    def _():
        acc_g[...] = jnp.zeros_like(acc_g)
        acc_u[...] = jnp.zeros_like(acc_u)

    rows = jnp.concatenate([x[...] for x in xs], axis=0)
    acc_g[...] += dot(rows, gw[0])
    acc_u[...] += dot(rows, uw[0])

    @pl.when(step == pl.num_programs(0) - 1)
    def _():
        silu, prime = silu_parts(acc_g[...])
        act[...] = silu
        slope[...] = acc_u[...] * prime
        hid[...] = dot(order_of(at).astype(BF16), (silu * acc_u[...]).astype(BF16)).astype(BF16)


def grad_kernel(at, g, dw, act, slope, dg, du, acc):
    step = pl.program_id(0)

    @pl.when(step == 0)
    def _():
        acc[...] = jnp.zeros_like(acc)

    acc[...] += dot_t(g[...], dw[0])

    @pl.when(step == pl.num_programs(0) - 1)
    def _():
        grad = lax.dot_general(
            order_of(at), acc[...], (((0,), (0,)), ((), ())), precision=lax.Precision.HIGHEST, preferred_element_type=F32
        )
        dg[...] = (grad * slope[...]).astype(BF16)
        du[...] = (grad * act[...]).astype(BF16)


def backward_kernel(dg, du, hid, gw, uw, dw, *outs):
    dx = (dot_t(dg[...], gw[0]) + dot_t(du[...], uw[0])).astype(BF16)
    for n in range(4):
        outs[n][...] = dx[n * 32 : n * 32 + 32]
    outs[4][...] = dx[128:]
    outs[5][...] = dot(hid[...], dw[0]).astype(BF16)


def back_sum_kernel(*refs):
    blocks, (mix, hid, grads, sg, su, sd), outs = refs[:8], refs[8:14], refs[14:]
    step = pl.program_id(0)
    half = pl.num_programs(0) // 2

    def put(total):
        for n in range(4):
            outs[n][...] = total[n * 32 : n * 32 + 32].astype(BF16)

    @pl.when(step < half)
    def _():
        rows = jnp.concatenate([v[...] for v in blocks], axis=0)
        put(dot_a(mix[...], rows) + dot(grads[...], jnp.concatenate([sg[...], su[...]], axis=0)))

    @pl.when(step >= half)
    def _():
        put(dot(hid[...], sd[...]))


def out_sum_kernel(rows, mix, mine, other):
    total = dot_a(mix[...], rows[...])
    mine[...] = total[:32]
    other[...] = total[32:].astype(BF16)


def shared_kernel(*refs):
    xs, gs, (sg, su, sd), (hid, grads, acc, acc_g) = refs[:4], refs[4:8], refs[8:11], refs[11:]
    step = pl.program_id(0)
    part = sg.shape[0]

    @pl.when(step == 0)
    def _():
        acc[...] = jnp.zeros_like(acc)
        acc_g[...] = jnp.zeros_like(acc_g)

    rows = jnp.concatenate([x[...] for x in xs], axis=0)
    acc[...] += dot_t(rows, jnp.concatenate([sg[...], su[...]], axis=0))
    acc_g[...] += dot_t(jnp.concatenate([g[...] for g in gs], axis=0), sd[...])

    @pl.when(step == pl.num_programs(0) - 1)
    def _():
        up = acc[:, part:]
        silu, prime = silu_parts(acc[:, :part])
        hid[...] = (silu * up).astype(BF16)
        grads[:, :part] = (acc_g[...] * up * prime).astype(BF16)
        grads[:, part:] = (acc_g[...] * silu).astype(BF16)


def local(
    tokens,
    routes,
    weights_q,
    cotangent,
    expert_gate,
    expert_up,
    expert_down,
    shared_gate,
    shared_up,
    shared_down,
):
    width = tokens.shape[1]
    hidden = expert_gate.shape[2]
    part = shared_gate.shape[1]
    steps = width // BLK
    tail = width // INFO
    grp, exp = lax.axis_index("grp"), lax.axis_index("exp")
    at = jnp.stack([grp, exp]).astype(I32)
    info = jnp.pad(jnp.concatenate([routes, weights_q], axis=1).astype(BF16), ((0, 0), (0, INFO - 2 * TOP)))
    first = lambda i: (0, jnp.minimum(i, steps - 1))
    later = lambda i: (0, jnp.maximum(i - steps, 0))
    info_at = lambda i: (0, tail)
    SM = lambda a: (a, "smem", None)

    with jax.named_scope("widen"):
        whole = lambda v: (v, v.shape, FIX)
        made = lambda rows, cols: ((rows, cols), BF16, (rows, cols), FIX)
        all_wide, g_wide = call(
            widen_kernel,
            1,
            [whole(v) for v in (tokens, cotangent, routes, weights_q)],
            [made(8, 2 * width + INFO), made(8, width + INFO)],
            [],
            0,
            4 * width * 16,
        )
    with jax.named_scope("gather_line"):
        all_line = ring(move_a, all_wide)
    with jax.named_scope("gather_plane"):
        plane = ring(move_b, jnp.concatenate(all_line, axis=0))
    with jax.named_scope("cot_gather"):
        g_line = jnp.concatenate(ring(move_y, g_wide), axis=0)
        g_blocks = [g_line, swap_core(g_line)]

    with jax.named_scope("cot_pick"):
        g_sent, g_mix = call(
            cot_pick_kernel,
            steps,
            [SM(at)] + [(b, (32, BLK), COL) for b in g_blocks] + [(b, (32, INFO), info_at) for b in g_blocks],
            [((256, width), BF16, (256, BLK), COL), ((256, 64), BF16, (256, 64), FIX)],
            [pltpu.VMEM((256, 64), BF16)],
            2 * 256 * 64 * width,
            2 * 320 * width,
        )
    with jax.named_scope("cot_route"):
        g_rows = lax.all_to_all(g_sent.reshape(16, 16, width), "exp", split_axis=0, concat_axis=0, tiled=True)
        g_rows = g_rows.reshape(256, width)

    with jax.named_scope("tok_pick"):
        *x_sent, x_over, x_mix = call(
            tok_pick_kernel,
            steps,
            [SM(at)]
            + [(b, (32, BLK), lambda i: (0, steps + i)) for b in plane]
            + [(b, (32, INFO), lambda i: (0, 2 * tail)) for b in plane],
            [((32, width), BF16, (32, BLK), COL)] * 4
            + [((128, width), BF16, (128, BLK), COL), ((256, 128), BF16, (256, 128), FIX)],
            [pltpu.VMEM((256, 128), BF16)],
            2 * 256 * 128 * width,
            2 * 400 * width,
            after=[g_mix],
        )
    with jax.named_scope("tok_route"):
        x_rows = [x_sent[0]] + [move_y(x_sent[k], k) for k in (1, 2, 3)]
        x_over = swap_core(x_over)
        x_over = [x_over[k * 32 : k * 32 + 32] for k in range(4)]
        x_rows += [x_over[0]] + [move_y(x_over[k], k) for k in (1, 2, 3)]

    with jax.named_scope("shared"):
        s_hid, s_grads = call(
            shared_kernel,
            steps,
            [(v, (32, BLK), lambda i: (0, steps + i)) for v in plane]
            + [(v, (32, BLK), COL) for v in plane]
            + [(shared_gate.T, (part, BLK), COL), (shared_up.T, (part, BLK), COL), (shared_down, (part, BLK), COL)],
            [((128, part), BF16, (128, part), FIX), ((128, 2 * part), BF16, (128, 2 * part), FIX)],
            [pltpu.VMEM((128, 2 * part), F32), pltpu.VMEM((128, part), F32)],
            6 * 128 * part * width,
            2 * 450 * width,
            after=[x_mix],
        )

    row_at = lambda i: (0, i, 0)
    col_at = lambda i: (0, 0, i)
    pre = ((256, hidden), F32, (256, hidden), FIX)
    mid = ((256, hidden), BF16, (256, hidden), FIX)
    with jax.named_scope("expert_forward"):
        hid, act, slope = call(
            forward_kernel,
            steps,
            [SM(at)]
            + [(x, (32, BLK), COL) for x in x_rows]
            + [(expert_gate, (1, BLK, hidden), row_at), (expert_up, (1, BLK, hidden), row_at)],
            [mid, pre, pre],
            [pltpu.VMEM((256, hidden), F32), pltpu.VMEM((256, hidden), F32)],
            4 * 256 * hidden * width,
            2 * (256 + 2 * hidden) * width,
            after=[s_hid],
        )
    with jax.named_scope("expert_grad"):
        dg, du = call(
            grad_kernel,
            steps,
            [
                SM(at),
                (g_rows, (256, BLK), COL),
                (expert_down, (1, hidden, BLK), col_at),
                (act, (256, hidden), FIX),
                (slope, (256, hidden), FIX),
            ],
            [mid, mid],
            [pltpu.VMEM((256, hidden), F32)],
            2 * 256 * hidden * width,
            2 * (256 + hidden) * width,
        )
    with jax.named_scope("expert_backward"):
        *dx_rows, dx_over, y_rows = call(
            backward_kernel,
            steps,
            [
                (dg, (256, hidden), FIX),
                (du, (256, hidden), FIX),
                (hid, (256, hidden), FIX),
                (expert_gate, (1, BLK, hidden), row_at),
                (expert_up, (1, BLK, hidden), row_at),
                (expert_down, (1, hidden, BLK), col_at),
            ],
            [((32, width), BF16, (32, BLK), COL)] * 4
            + [((128, width), BF16, (128, BLK), COL), ((256, width), BF16, (256, BLK), COL)],
            [],
            6 * 256 * hidden * width,
            2 * (512 + 3 * hidden) * width,
        )
    with jax.named_scope("out_route"):
        y_home = lax.all_to_all(y_rows.reshape(16, 16, width), "exp", split_axis=0, concat_axis=0, tiled=True)
        y_home = y_home.reshape(256, width)

    with jax.named_scope("back_route"):
        dx_home = [dx_rows[0]] + [move_y(dx_rows[k], -k) for k in (1, 2, 3)]
        dx_over = swap_core(dx_over)
        dx_over = [dx_over[k * 32 : k * 32 + 32] for k in range(4)]
        dx_home += [dx_over[0]] + [move_y(dx_over[k], -k) for k in (1, 2, 3)]
        parts = call(
            back_sum_kernel,
            2 * steps,
            [(v, (32, BLK), first) for v in dx_home]
            + [
                (x_mix, (256, 128), FIX),
                (s_hid, (128, part), FIX),
                (s_grads, (128, 2 * part), FIX),
                (shared_gate.T, (part, BLK), first),
                (shared_up.T, (part, BLK), first),
                (shared_down, (part, BLK), later),
            ],
            [((32, 2 * width), BF16, (32, BLK), COL)] * 4,
            [],
            2 * 256 * 128 * width,
            2 * 400 * width,
            after=[y_home],
        )
        line = ring_sum(move_b, parts).astype(BF16).reshape(4, 8, 2 * width)
        both = ring_sum(move_a, [line[k] for k in range(4)])
        token_grad, s_out = both[:, :width].astype(BF16), both[:, width:]
    with jax.named_scope("out_sum"):
        mine, other = call(
            out_sum_kernel,
            steps,
            [(y_home, (256, BLK), COL), (g_mix, (256, 64), FIX)],
            [((32, width), F32, (32, BLK), COL), ((32, width), BF16, (32, BLK), COL)],
            [],
            2 * 256 * 64 * width,
            2 * 352 * width,
        )
        line = (mine + swap_core(other).astype(F32)).reshape(4, 8, width)
        line = [line[0]] + [line[k].astype(BF16) for k in (1, 2, 3)]
        mixed = (ring_sum(move_y, line) + s_out).astype(BF16)
    return (mixed, token_grad)


def solution(mesh):
    in_specs = (
        P(("grp", "exp"), None),
        P(("grp", "exp"), None),
        P(("grp", "exp"), None),
        P(("grp", "exp"), None),
        P(("grp", "exp"), None, None),
        P(("grp", "exp"), None, None),
        P(("grp", "exp"), None, None),
        P(None, "exp"),
        P(None, "exp"),
        P("exp", None),
    )
    out_specs = (P(("grp", "exp"), None), P(("grp", "exp"), None))
    return jax.shard_map(local, mesh=mesh, in_specs=in_specs, out_specs=out_specs, check_vma=False)
```

time: 381 us -> 252 us (0.66)
  waiting for transfers between devices: 186 us -> 113 us
  local copies, waits for them, and re-layouts: 40.6 us -> 8 us
  between operations: 14.3 us -> 0.89 us
  starting transfers between devices: 75.5 us -> 66.1 us
  Pallas kernels: 53.1 us -> 61.5 us
  other arithmetic: 8.53 us -> 2.04 us
    ppermute x18 -> x12, waiting for transfers between devices: 96.3 us -> 37.3 us  [move_plane(): return lax.ppermute(v, ('grp', 'exp'), pairs)]
    ppermute x18, waiting for transfers between devices: 87.2 us -> 49.1 us  [move_y(): lax.ppermute(v, 'grp', [(y * 2 + c, (y + k) % N_Y * 2 + c) for y in range...]
    unnamed x58 -> x32, local copies, waits for them, and re-layouts: 40.6 us -> 5.43 us
    all_to_all x1, waiting for transfers between devices: 0.01 us -> 25.4 us  [local(): lax.all_to_all(y_rows.reshape(16, 16, width), 'exp', split_axis=0, concat...]
    pallas_call x8 -> x9, Pallas kernels: 53.1 us -> 61.5 us  [call(): pl.pallas_call(lambda *refs: kernel(*refs[skip:]), grid=(grid,), in_specs...]
    ppermute x18 -> x12, starting transfers between devices: 32.7 us -> 28.3 us  [move_plane(): return lax.ppermute(v, ('grp', 'exp'), pairs)]
  transfers between devices with their start and end apart: 49 -> 36, of which waited for: 21 -> 15; matrix products, arithmetic and copies ran while one was open for 2% -> 2% of each run, Pallas kernels for 13% -> 13%
where the time goes in v1:
time: 252 us
  waiting for transfers between devices  113 us (45%)
  starting transfers between devices  66.1 us (26%)
  Pallas kernels  61.5 us (24%)
  local copies, waits for them, and re-layouts  8 us (3%)
    pallas_call x9, Pallas kernels, call(): pl.pallas_call(lambda *refs: kernel(*refs[skip:]), grid=(grid,), in_specs...  61.5 us
    ppermute x18, waiting for transfers between devices, move_y(): lax.ppermute(v, 'grp', [(y * 2 + c, (y + k) % N_Y * 2 + c) for y in range...  49.1 us
    ppermute x12, waiting for transfers between devices, move_plane(): return lax.ppermute(v, ('grp', 'exp'), pairs)  37.3 us
    ppermute x12, starting transfers between devices, move_plane(): return lax.ppermute(v, ('grp', 'exp'), pairs)  28.3 us
    ppermute x18, starting transfers between devices, move_y(): lax.ppermute(v, 'grp', [(y * 2 + c, (y + k) % N_Y * 2 + c) for y in range...  25.5 us
    all_to_all x1, waiting for transfers between devices, local(): lax.all_to_all(y_rows.reshape(16, 16, width), 'exp', split_axis=0, concat...  25.4 us
    all_to_all x1, starting transfers between devices, local(): lax.all_to_all(y_rows.reshape(16, 16, width), 'exp', split_axis=0, concat...  6.87 us
    unnamed x32, local copies, waits for them, and re-layouts  5.43 us
  transfers between devices with their start and end apart: 36, of which 15 were waited for; matrix products, arithmetic and copies ran while one was open for 2% of the time, Pallas kernels for 13%

profile of v1, /device:TPU:0, one launch (start us, length us, event | category | flops | bytes accessed | tf_op | source)
XLA Modules:
  0.0 251.7 jit_solution(8829660702888504223)
XLA Ops:
  0.6 1.8 widen.1
  2.5 1.7 collective-permute-start
  4.1 2.9 %collective-permute-start.1 = (bf16[8,7296]{1,0:T(8,128)(2,1)}, bf16[8,7296]{1,0:T(8,128)(2,1)S(1)}, u32[]{:S(2)}, u32[]{:S(2)}) collective-permute-start(bf16[8,7296]{1,0:T(8,128)(2,1)} %get-tuple-element.31), channel_id=1, source_target_pairs={{0,64},{16,80},{32,96},{48,112},{64,0},{80,16},{96,32},{112,48},{1... | collective-permute-start | bytes 350216 | tf_op jit(solution)/shard_map/cot_gather/ppermute | solution.py:46
  7.0 1.3 collective-permute-start.2
  8.4 1.5 collective-permute-start.4
  9.9 2.7 %collective-permute-start.5 = (bf16[8,14464]{1,0:T(8,128)(2,1)}, bf16[8,14464]{1,0:T(8,128)(2,1)S(1)}, u32[]{:S(2)}, u32[]{:S(2)}) collective-permute-start(bf16[8,14464]{1,0:T(8,128)(2,1)} %get-tuple-element.34), channel_id=1, source_target_pairs={{0,8},{1,9},{2,10},{3,11},{4,12},{5,13},{6,14},{7,15},{8,0},{9,1},... | collective-permute-start | bytes 694280 | tf_op jit(solution)/shard_map/gather_line/ppermute | solution.py:61
  12.6 1.0 constant_dynamic-update-slice_fusion.7
  13.6 0.9 constant_dynamic-update-slice_fusion.3
  14.5 1.5 collective-permute-start.6
  16.1 3.2 %collective-permute-done.5 = bf16[8,14464]{1,0:T(8,128)(2,1)S(1)} collective-permute-done((bf16[8,14464]{1,0:T(8,128)(2,1)}, bf16[8,14464]{1,0:T(8,128)(2,1)S(1)}, u32[]{:S(2)}, u32[]{:S(2)}) %collective-permute-start.5) | collective-permute-done | bytes 231456 | tf_op jit(solution)/shard_map/gather_line/ppermute | solution.py:61
  19.3 1.5 collective-permute-done.6
  20.8 2.0 collective-permute-start.7
  22.8 3.6 %collective-permute-start.8 = (bf16[32,14464]{1,0:T(8,128)(2,1)S(1)}, bf16[32,14464]{1,0:T(8,128)(2,1)S(1)}, u32[]{:S(2)}, u32[]{:S(2)}) collective-permute-start(bf16[32,14464]{1,0:T(8,128)(2,1)S(1)} %constant_dynamic-update-slice_fusion.4.refs_2_.refs_6_.refs_1_.refs_5_), channel_id=1, source_target_pairs={{0,2},{1,3},{2,0},{3,1},{4,6},{5,7},{6,4},{7,5},{8,10},{9,11},{10,... | collective-permute-start | bytes 2777096 | tf_op jit(solution)/shard_map/gather_plane/ppermute | solution.py:61
  26.4 1.0 collective-permute-start.9
  27.6 0.7 pad_add_fusion.refs_0_.refs_1_
  28.2 1.3 collective-permute-done.3.refs_2_.refs_4_
  29.5 5.1 %cot_pick.1 = (bf16[256,7168]{1,0:T(8,128)(2,1)}, bf16[256,64]{1,0:T(8,128)(2,1)}) custom-call(s32[2]{0:T(128)} %pad_add_fusion.refs_0_.refs_1_, bf16[32,7296]{1,0:T(8,128)(2,1)} %copy-done.3, bf16[32,7296]{1,0:T(8,128)(2,1)} %collective-permute-done.3.refs_2_.refs_4_, bf16[32,7296]{1,0:T(8,128)(2,1)} %copy-done.3, ...), custom_call_target="tpu_custom_call" | custom-call | flops 234881024 | bytes 4587520 | tf_op jit(solution)/shard_map/cot_pick/pallas_call | solution.py:88
  34.6 1.9 collective-permute-done.7.refs_3_.refs_7_.refs_2_.refs_6_
  36.4 11.4 %collective-permute-done.8.refs_4_.refs_8_.refs_3_.refs_7_ = bf16[32,14464]{1,0:T(8,128)(2,1)S(1)} collective-permute-done((bf16[32,14464]{1,0:T(8,128)(2,1)S(1)}, bf16[32,14464]{1,0:T(8,128)(2,1)S(1)}, u32[]{:S(2)}, u32[]{:S(2)}) %collective-permute-start.8) | collective-permute-done | bytes 925728 | tf_op jit(solution)/shard_map/gather_plane/ppermute | solution.py:61
  47.8 1.0 copy-done.2
  48.8 5.2 %tok_pick.1 = (bf16[32,7168]{1,0:T(8,128)(2,1)}, bf16[32,7168]{1,0:T(8,128)(2,1)}, bf16[32,7168]{1,0:T(8,128)(2,1)}, bf16[32,7168]{1,0:T(8,128)(2,1)}, bf16[128,...) custom-call(bf16[256,64]{1,0:T(8,128)(2,1)} %get-tuple-element.33.refs_0_.refs_1_, s32[2]{0:T(128)} %pad_add_fusion.refs_0_.refs_1_, ...), custom_call_target="tpu_custom_call" | custom-call | flops 469762048 | bytes 5734400 | tf_op jit(solution)/shard_map/tok_pick/pallas_call | solution.py:88
  54.1 5.2 %all-to-all-start = ((bf16[16,16,7168]{2,1,0:T(8,128)(2,1)}), bf16[16,16,7168]{2,1,0:T(8,128)(2,1)}, u32[]{:S(2)}, u32[]{:S(2)}) async-start(bf16[16,16,7168]{2,1,0:T(8,128)(2,1)} %bitcast.12), calls=%async_computation | async-start | bytes 7340032 | tf_op jit(solution)/shard_map/cot_route/all_to_all | solution.py:326
  59.3 0.7 collective-permute-start.10
  60.0 0.8 collective-permute-start.11
  60.8 2.0 collective-permute-start.12
  62.8 0.9 fusion.5
  63.7 0.7 collective-permute-start.14
  64.3 2.1 collective-permute-start.15
  66.5 17.5 %collective-permute-done.10.refs_3_ = bf16[32,7168]{1,0:T(8,128)(2,1)S(1)} collective-permute-done((bf16[32,7168]{1,0:T(8,128)(2,1)}, bf16[32,7168]{1,0:T(8,128)(2,1)S(1)}, u32[]{:S(2)}, u32[]{:S(2)}) %collective-permute-start.10) | collective-permute-done | bytes 458784 | tf_op jit(solution)/shard_map/tok_route/ppermute | solution.py:46
  84.0 5.3 %shared.1 = (bf16[128,64]{1,0:T(8,128)(2,1)}, bf16[128,128]{1,0:T(8,128)(2,1)}) custom-call(bf16[256,128]{1,0:T(8,128)(2,1)} %get-tuple-element.35.refs_0_.refs_9_, bf16[32,14464]{1,0:T(8,128)(2,1)} %copy-done, bf16[32,14464]{1,0:T(8,128)(2,1)} %copy-done.1, bf16[32,14464]{1,0:T(8,128)(2,1)} %copy-done.2, ...), custom_call_target="tpu_custom_call" | custom-call | flops 352321536 | bytes 6451200 | tf_op jit(solution)/shard_map/shared/pallas_call | solution.py:88
  89.2 13.6 %collective-permute-done.14.refs_7_ = bf16[32,7168]{1,0:T(8,128)(2,1)S(1)} collective-permute-done((bf16[32,7168]{1,0:T(8,128)(2,1)S(1)}, bf16[32,7168]{1,0:T(8,128)(2,1)S(1)}, u32[]{:S(2)}, u32[]{:S(2)}) %collective-permute-start.14) | collective-permute-done | bytes 458784 | tf_op jit(solution)/shard_map/tok_route/ppermute | solution.py:46
  102.9 0.7 collective-permute-done.16.refs_9_
  103.8 0.5 copy-done.12
  104.3 10.3 %expert_forward.1 = (bf16[256,512]{1,0:T(8,128)(2,1)}, f32[256,512]{1,0:T(8,128)}, f32[256,512]{1,0:T(8,128)}) custom-call(bf16[128,64]{1,0:T(8,128)(2,1)} %get-tuple-element.36.refs_0_.refs_10_, s32[2]{0:T(128)} %pad_add_fusion.refs_0_.refs_1_, bf16[32,7168]{1,0:T(8,128)(2,1)} %get-tuple-element.37.refs_2_, bf16[32,7168]{1,0:T(8,128)(2,1)} %copy-done.7, ...), custom_call_target="tpu_custom_call" | custom-call | flops 3758096384 | bytes 18350080 | tf_op jit(solution)/shard_map/expert_forward/pallas_call | solution.py:88
  114.6 7.8 %expert_grad.1 = (bf16[256,512]{1,0:T(8,128)(2,1)}, bf16[256,512]{1,0:T(8,128)(2,1)}) custom-call(s32[2]{0:T(128)} %pad_add_fusion.refs_0_.refs_1_, bf16[256,7168]{1,0:T(8,128)(2,1)} %bitcast.3.refs_1_, bf16[1,512,7168]{2,1,0:T(8,128)(2,1)} %refs_5_.1, f32[256,512]{1,0:T(8,128)} %get-tuple-element.42.refs_3_, f32[256,512]{1,0:T(8,128)} %get-tuple-element.43.refs_4_), custom_call_target="tpu_custom_call" | custom-call | flops 1879048192 | bytes 11010048 | tf_op jit(solution)/shard_map/expert_grad/pallas_call | solution.py:88
  122.5 12.9 %expert_backward.1 = (bf16[32,7168]{1,0:T(8,128)(2,1)}, bf16[32,7168]{1,0:T(8,128)(2,1)}, bf16[32,7168]{1,0:T(8,128)(2,1)}, bf16[32,7168]{1,0:T(8,128)(2,1)}, bf...) custom-call(bf16[256,512]{1,0:T(8,128)(2,1)} %get-tuple-element.44.refs_0_, ...), custom_call_target="tpu_custom_call" | custom-call | flops 5637144576 | bytes 29360128 | tf_op jit(solution)/shard_map/expert_backward/pallas_call | solution.py:88
  135.4 6.9 %all-to-all-start.1 = ((bf16[16,16,7168]{2,1,0:T(8,128)(2,1)}), bf16[16,16,7168]{2,1,0:T(8,128)(2,1)}, u32[]{:S(2)}, u32[]{:S(2)}) async-start(bf16[16,16,7168]{2,1,0:T(8,128)(2,1)} %bitcast.13), calls=%async_computation.1 | async-start | bytes 7340032 | tf_op jit(solution)/shard_map/out_route/all_to_all | solution.py:415
  142.3 2.6 %collective-permute-start.21 = (bf16[32,7168]{1,0:T(8,128)(2,1)}, bf16[32,7168]{1,0:T(8,128)(2,1)S(1)}, u32[]{:S(2)}, u32[]{:S(2)}) collective-permute-start(bf16[32,7168]{1,0:T(8,128)(2,1)} %get-tuple-element.51), channel_id=1, source_target_pairs={{0,96},{16,112},{32,0},{48,16},{64,32},{80,48},{96,64},{112,80},{1... | collective-permute-start | bytes 1376264 | tf_op jit(solution)/shard_map/back_route/ppermute | solution.py:46
  144.9 0.9 collective-permute-start.23
  145.8 0.9 fusion.4
  146.7 2.4 collective-permute-start.25
  149.1 2.2 collective-permute-start.26
  151.3 14.4 %collective-permute-done.21.refs_2_ = bf16[32,7168]{1,0:T(8,128)(2,1)S(1)} collective-permute-done((bf16[32,7168]{1,0:T(8,128)(2,1)}, bf16[32,7168]{1,0:T(8,128)(2,1)S(1)}, u32[]{:S(2)}, u32[]{:S(2)}) %collective-permute-start.21) | collective-permute-done | bytes 458784 | tf_op jit(solution)/shard_map/back_route/ppermute | solution.py:46
  165.7 0.8 copy-done.6
  166.5 25.4 %all-to-all-done.1 = bf16[16,16,7168]{2,1,0:T(8,128)(2,1)} async-done(((bf16[16,16,7168]{2,1,0:T(8,128)(2,1)}), bf16[16,16,7168]{2,1,0:T(8,128)(2,1)}, u32[]{:S(2)}, u32[]{:S(2)}) %all-to-all-start.1) | async-done | bytes 3670048 | tf_op jit(solution)/shard_map/out_route/all_to_all | solution.py:415
  191.9 4.5 %out_sum.1 = (f32[32,7168]{1,0:T(8,128)}, bf16[32,7168]{1,0:T(8,128)(2,1)}) custom-call(bf16[256,7168]{1,0:T(8,128)(2,1)} %bitcast.7.refs_0_, bf16[256,64]{1,0:T(8,128)(2,1)} %get-tuple-element.33.refs_0_.refs_1_), custom_call_target="tpu_custom_call" | custom-call | flops 234881024 | bytes 5046272 | tf_op jit(solution)/shard_map/out_sum/pallas_call | solution.py:88
  196.6 0.8 copy-done.8
  197.5 8.6 %back_route.1 = (bf16[32,14336]{1,0:T(8,128)(2,1)}, bf16[32,14336]{1,0:T(8,128)(2,1)}, bf16[32,14336]{1,0:T(8,128)(2,1)}, bf16[32,14336]{1,0:T(8,128)(2,1)}) custom-call(bf16[256,7168]{1,0:T(8,128)(2,1)} %bitcast.7.refs_0_, bf16[32,7168]{1,0:T(8,128)(2,1)} %get-tuple-element.50.refs_1_, bf16[32,7168]{1,0:T(8,128)(2,1)} %copy-done.6, ...), custom_call_target="tpu_custom_call" | custom-call | flops 469762048 | bytes 5734400 | tf_op jit(solution)/shard_map/back_route/pallas_call | solution.py:88
  206.1 0.3 collective-permute-start.30
  206.4 4.6 %collective-permute-start.29 = (bf16[32,14336]{1,0:T(8,128)(2,1)}, bf16[32,14336]{1,0:T(8,128)(2,1)S(1)}, u32[]{:S(2)}, u32[]{:S(2)}) collective-permute-start(bf16[32,14336]{1,0:T(8,128)(2,1)} %get-tuple-element.58), channel_id=1, source_target_pairs={{0,2},{1,3},{2,0},{3,1},{4,6},{5,7},{6,4},{7,5},{8,10},{9,11},{10,... | collective-permute-start | bytes 2752520 | tf_op jit(solution)/shard_map/back_route/ppermute | solution.py:61
  211.0 1.9 collective-permute-start.28
  213.1 8.1 %collective-permute-done.30 = bf16[32,14336]{1,0:T(8,128)(2,1)S(1)} collective-permute-done((bf16[32,14336]{1,0:T(8,128)(2,1)}, bf16[32,14336]{1,0:T(8,128)(2,1)S(1)}, u32[]{:S(2)}, u32[]{:S(2)}) %collective-permute-start.30) | collective-permute-done | bytes 917536 | tf_op jit(solution)/shard_map/back_route/ppermute | solution.py:61
  221.1 11.3 %collective-permute-done.29 = bf16[32,14336]{1,0:T(8,128)(2,1)S(1)} collective-permute-done((bf16[32,14336]{1,0:T(8,128)(2,1)}, bf16[32,14336]{1,0:T(8,128)(2,1)S(1)}, u32[]{:S(2)}, u32[]{:S(2)}) %collective-permute-start.29) | collective-permute-done | bytes 917536 | tf_op jit(solution)/shard_map/back_route/ppermute | solution.py:61
  232.4 0.4 add_convert_fusion
  232.9 0.5 collective-permute-start.33
  233.5 6.1 %collective-permute-start.32 = (bf16[8,14336]{1,0:T(8,128)(2,1)S(1)}, bf16[8,14336]{1,0:T(8,128)(2,1)S(1)}, u32[]{:S(2)}, u32[]{:S(2)}) collective-permute-start(bf16[8,14336]{1,0:T(8,128)(2,1)S(1)} %get-tuple-element.72), channel_id=1, source_target_pairs={{0,8},{1,9},{2,10},{3,11},{4,12},{5,13},{6,14},{7,15},{8,0},{9,1},... | collective-permute-start | bytes 688136 | tf_op jit(solution)/shard_map/back_route/ppermute | solution.py:61
  239.6 2.5 %collective-permute-start.31 = (bf16[8,14336]{1,0:T(8,128)(2,1)S(1)}, bf16[8,14336]{1,0:T(8,128)(2,1)S(1)}, u32[]{:S(2)}, u32[]{:S(2)}) collective-permute-start(bf16[8,14336]{1,0:T(8,128)(2,1)S(1)} %get-tuple-element.70), channel_id=1, source_target_pairs={{0,12},{1,13},{2,14},{3,15},{4,0},{5,1},{6,2},{7,3},{8,4},{9,5},{1... | collective-permute-start | bytes 688136 | tf_op jit(solution)/shard_map/back_route/ppermute | solution.py:61
  242.1 2.4 collective-permute-start.20
  244.5 1.6 collective-permute-start.19
  246.2 1.1 collective-permute-start.18
  247.4 0.7 slice.114
  248.1 1.0 collective-permute-done.20
  249.0 1.8 collective-permute-done.19
  251.0 0.7 fusion
  (61 shorter events, 1.4 us)
Async XLA Ops:
  2.5 12.0 %collective-permute-start = (bf16[8,7296]{1,0:T(8,128)(2,1)}, bf16[8,7296]{1,0:T(8,128)(2,1)S(1)}, u32[]{:S(2)}, u32[]{:S(2)}) collective-permute-start(bf16[8,7296]{1,0:T(8,128)(2,1)} %get-tuple-element.31), channel_id=1, source_target_pairs={{0,32},{16,48},{32,64},{48,80},{64,96},{80,112},{96,0},{112,16},{1... | collective-permute-start | bytes 350216 | tf_op jit(solution)/shard_map/cot_gather/ppermute | solution.py:46
  4.1 11.9 %collective-permute-start.1 = (bf16[8,7296]{1,0:T(8,128)(2,1)}, bf16[8,7296]{1,0:T(8,128)(2,1)S(1)}, u32[]{:S(2)}, u32[]{:S(2)}) collective-permute-start(bf16[8,7296]{1,0:T(8,128)(2,1)} %get-tuple-element.31), channel_id=1, source_target_pairs={{0,64},{16,80},{32,96},{48,112},{64,0},{80,16},{96,32},{112,48},{1... | collective-permute-start | bytes 350216 | tf_op jit(solution)/shard_map/cot_gather/ppermute | solution.py:46
  7.0 20.4 %collective-permute-start.2 = (bf16[8,7296]{1,0:T(8,128)(2,1)}, bf16[8,7296]{1,0:T(8,128)(2,1)S(1)}, u32[]{:S(2)}, u32[]{:S(2)}) collective-permute-start(bf16[8,7296]{1,0:T(8,128)(2,1)} %get-tuple-element.31), channel_id=1, source_target_pairs={{0,96},{16,112},{32,0},{48,16},{64,32},{80,48},{96,64},{112,80},{1... | collective-permute-start | bytes 350216 | tf_op jit(solution)/shard_map/cot_gather/ppermute | solution.py:46
  8.4 7.7 %collective-permute-start.4 = (bf16[8,14464]{1,0:T(8,128)(2,1)}, bf16[8,14464]{1,0:T(8,128)(2,1)S(1)}, u32[]{:S(2)}, u32[]{:S(2)}) collective-permute-start(bf16[8,14464]{1,0:T(8,128)(2,1)} %get-tuple-element.34), channel_id=1, source_target_pairs={{0,4},{1,5},{2,6},{3,7},{4,8},{5,9},{6,10},{7,11},{8,12},{9,13},{1... | collective-permute-start | bytes 694280 | tf_op jit(solution)/shard_map/gather_line/ppermute | solution.py:61
  9.9 9.4 %collective-permute-start.5 = (bf16[8,14464]{1,0:T(8,128)(2,1)}, bf16[8,14464]{1,0:T(8,128)(2,1)S(1)}, u32[]{:S(2)}, u32[]{:S(2)}) collective-permute-start(bf16[8,14464]{1,0:T(8,128)(2,1)} %get-tuple-element.34), channel_id=1, source_target_pairs={{0,8},{1,9},{2,10},{3,11},{4,12},{5,13},{6,14},{7,15},{8,0},{9,1},... | collective-permute-start | bytes 694280 | tf_op jit(solution)/shard_map/gather_line/ppermute | solution.py:61
  14.5 6.3 %collective-permute-start.6 = (bf16[8,14464]{1,0:T(8,128)(2,1)}, bf16[8,14464]{1,0:T(8,128)(2,1)S(1)}, u32[]{:S(2)}, u32[]{:S(2)}) collective-permute-start(bf16[8,14464]{1,0:T(8,128)(2,1)} %get-tuple-element.34), channel_id=1, source_target_pairs={{0,12},{1,13},{2,14},{3,15},{4,0},{5,1},{6,2},{7,3},{8,4},{9,5},{1... | collective-permute-start | bytes 694280 | tf_op jit(solution)/shard_map/gather_line/ppermute | solution.py:61
  20.8 27.0 %copy-start = (bf16[32,14464]{1,0:T(8,128)(2,1)}, bf16[32,14464]{1,0:T(8,128)(2,1)S(1)}, u32[]{:S(2)}) copy-start(bf16[32,14464]{1,0:T(8,128)(2,1)S(1)} %constant_dynamic-update-slice_fusion.4.refs_2_.refs_6_.refs_1_.refs_5_) | copy-start | bytes 2777092
  20.8 15.6 %collective-permute-start.7 = (bf16[32,14464]{1,0:T(8,128)(2,1)S(1)}, bf16[32,14464]{1,0:T(8,128)(2,1)S(1)}, u32[]{:S(2)}, u32[]{:S(2)}) collective-permute-start(bf16[32,14464]{1,0:T(8,128)(2,1)S(1)} %constant_dynamic-update-slice_fusion.4.refs_2_.refs_6_.refs_1_.refs_5_), channel_id=1, source_target_pairs={{0,1},{1,2},{2,3},{3,0},{4,5},{5,6},{6,7},{7,4},{8,9},{9,10},{10,1... | collective-permute-start | bytes 2777096 | tf_op jit(solution)/shard_map/gather_plane/ppermute | solution.py:61
  22.8 25.0 %collective-permute-start.8 = (bf16[32,14464]{1,0:T(8,128)(2,1)S(1)}, bf16[32,14464]{1,0:T(8,128)(2,1)S(1)}, u32[]{:S(2)}, u32[]{:S(2)}) collective-permute-start(bf16[32,14464]{1,0:T(8,128)(2,1)S(1)} %constant_dynamic-update-slice_fusion.4.refs_2_.refs_6_.refs_1_.refs_5_), channel_id=1, source_target_pairs={{0,2},{1,3},{2,0},{3,1},{4,6},{5,7},{6,4},{7,5},{8,10},{9,11},{10,... | collective-permute-start | bytes 2777096 | tf_op jit(solution)/shard_map/gather_plane/ppermute | solution.py:61
  26.4 21.4 %collective-permute-start.9 = (bf16[32,14464]{1,0:T(8,128)(2,1)S(1)}, bf16[32,14464]{1,0:T(8,128)(2,1)}, u32[]{:S(2)}, u32[]{:S(2)}) collective-permute-start(bf16[32,14464]{1,0:T(8,128)(2,1)S(1)} %constant_dynamic-update-slice_fusion.4.refs_2_.refs_6_.refs_1_.refs_5_), channel_id=1, source_target_pairs={{0,3},{1,0},{2,1},{3,2},{4,7},{5,4},{6,5},{7,6},{8,11},{9,8},{10,9... | collective-permute-start | bytes 2777096 | tf_op jit(solution)/shard_map/gather_plane/ppermute | solution.py:61
  27.4 2.1 copy-start.3
  27.5 2.0 collective-permute-start.3
  36.4 11.4 %copy-start.1 = (bf16[32,14464]{1,0:T(8,128)(2,1)}, bf16[32,14464]{1,0:T(8,128)(2,1)S(1)}, u32[]{:S(2)}) copy-start(bf16[32,14464]{1,0:T(8,128)(2,1)S(1)} %collective-permute-done.7.refs_3_.refs_7_.refs_2_.refs_6_) | copy-start | bytes 2777092
  47.8 1.0 copy-start.2
  54.0 8.8 %collective-permute-start.13 = (bf16[128,7168]{1,0:T(8,128)(2,1)}, bf16[128,7168]{1,0:T(8,128)(2,1)S(1)}, u32[]{:S(2)}, u32[]{:S(2)}) collective-permute-start(bf16[128,7168]{1,0:T(8,128)(2,1)} %get-tuple-element.41), channel_id=1, source_target_pairs={{0,16},{16,0},{32,48},{48,32},{64,80},{80,64},{96,112},{112,96},{1... | collective-permute-start | bytes 5505032 | tf_op jit(solution)/shard_map/tok_route/ppermute | solution.py:50
  54.1 60.6 %all-to-all-start = ((bf16[16,16,7168]{2,1,0:T(8,128)(2,1)}), bf16[16,16,7168]{2,1,0:T(8,128)(2,1)}, u32[]{:S(2)}, u32[]{:S(2)}) async-start(bf16[16,16,7168]{2,1,0:T(8,128)(2,1)} %bitcast.12), calls=%async_computation | async-start | bytes 7340032 | tf_op jit(solution)/shard_map/cot_route/all_to_all | solution.py:326
  59.3 24.7 %collective-permute-start.10 = (bf16[32,7168]{1,0:T(8,128)(2,1)}, bf16[32,7168]{1,0:T(8,128)(2,1)S(1)}, u32[]{:S(2)}, u32[]{:S(2)}) collective-permute-start(bf16[32,7168]{1,0:T(8,128)(2,1)} %get-tuple-element.38), channel_id=1, source_target_pairs={{0,32},{16,48},{32,64},{48,80},{64,96},{80,112},{96,0},{112,16},{1... | collective-permute-start | bytes 1376264 | tf_op jit(solution)/shard_map/tok_route/ppermute | solution.py:46
  60.0 29.2 %collective-permute-start.11 = (bf16[32,7168]{1,0:T(8,128)(2,1)}, bf16[32,7168]{1,0:T(8,128)(2,1)}, u32[]{:S(2)}, u32[]{:S(2)}) collective-permute-start(bf16[32,7168]{1,0:T(8,128)(2,1)} %get-tuple-element.39), channel_id=1, source_target_pairs={{0,64},{16,80},{32,96},{48,112},{64,0},{80,16},{96,32},{112,48},{1... | collective-permute-start | bytes 1376264 | tf_op jit(solution)/shard_map/tok_route/ppermute | solution.py:46
  60.8 28.4 %collective-permute-start.12 = (bf16[32,7168]{1,0:T(8,128)(2,1)}, bf16[32,7168]{1,0:T(8,128)(2,1)}, u32[]{:S(2)}, u32[]{:S(2)}) collective-permute-start(bf16[32,7168]{1,0:T(8,128)(2,1)} %get-tuple-element.40), channel_id=1, source_target_pairs={{0,96},{16,112},{32,0},{48,16},{64,32},{80,48},{96,64},{112,80},{1... | collective-permute-start | bytes 1376264 | tf_op jit(solution)/shard_map/tok_route/ppermute | solution.py:46
  63.7 39.2 %collective-permute-start.14 = (bf16[32,7168]{1,0:T(8,128)(2,1)S(1)}, bf16[32,7168]{1,0:T(8,128)(2,1)S(1)}, u32[]{:S(2)}, u32[]{:S(2)}) collective-permute-start(bf16[32,7168]{1,0:T(8,128)(2,1)S(1)} %get-tuple-element.68), channel_id=1, source_target_pairs={{0,32},{16,48},{32,64},{48,80},{64,96},{80,112},{96,0},{112,16},{1... | collective-permute-start | bytes 1376264 | tf_op jit(solution)/shard_map/tok_route/ppermute | solution.py:46
  64.3 38.6 %collective-permute-start.15 = (bf16[32,7168]{1,0:T(8,128)(2,1)S(1)}, bf16[32,7168]{1,0:T(8,128)(2,1)S(1)}, u32[]{:S(2)}, u32[]{:S(2)}) collective-permute-start(bf16[32,7168]{1,0:T(8,128)(2,1)S(1)} %get-tuple-element.67), channel_id=1, source_target_pairs={{0,64},{16,80},{32,96},{48,112},{64,0},{80,16},{96,32},{112,48},{1... | collective-permute-start | bytes 1376264 | tf_op jit(solution)/shard_map/tok_route/ppermute | solution.py:46
  84.0 5.3 %copy-start.7 = (bf16[32,7168]{1,0:T(8,128)(2,1)}, bf16[32,7168]{1,0:T(8,128)(2,1)S(1)}, u32[]{:S(2)}) copy-start(bf16[32,7168]{1,0:T(8,128)(2,1)S(1)} %collective-permute-done.10.refs_3_) | copy-start | bytes 1376260
  84.0 19.6 %collective-permute-start.16 = (bf16[32,7168]{1,0:T(8,128)(2,1)S(1)}, bf16[32,7168]{1,0:T(8,128)(2,1)S(1)}, u32[]{:S(2)}, u32[]{:S(2)}) collective-permute-start(bf16[32,7168]{1,0:T(8,128)(2,1)S(1)} %get-tuple-element.66), channel_id=1, source_target_pairs={{0,96},{16,112},{32,0},{48,16},{64,32},{80,48},{96,64},{112,80},{1... | collective-permute-start | bytes 1376264 | tf_op jit(solution)/shard_map/tok_route/ppermute | solution.py:46
  102.9 0.8 copy-start.10
  102.9 0.9 copy-start.11
  103.6 0.8 copy-start.12
  135.3 10.5 %collective-permute-start.24 = (bf16[128,7168]{1,0:T(8,128)(2,1)}, bf16[128,7168]{1,0:T(8,128)(2,1)S(1)}, u32[]{:S(2)}, u32[]{:S(2)}) collective-permute-start(bf16[128,7168]{1,0:T(8,128)(2,1)} %get-tuple-element.54), channel_id=1, source_target_pairs={{0,16},{16,0},{32,48},{48,32},{64,80},{80,64},{96,112},{112,96},{1... | collective-permute-start | bytes 5505032 | tf_op jit(solution)/shard_map/back_route/ppermute | solution.py:50
  135.4 56.5 %all-to-all-start.1 = ((bf16[16,16,7168]{2,1,0:T(8,128)(2,1)}), bf16[16,16,7168]{2,1,0:T(8,128)(2,1)}, u32[]{:S(2)}, u32[]{:S(2)}) async-start(bf16[16,16,7168]{2,1,0:T(8,128)(2,1)} %bitcast.13), calls=%async_computation.1 | async-start | bytes 7340032 | tf_op jit(solution)/shard_map/out_route/all_to_all | solution.py:415
  142.3 23.4 %collective-permute-start.21 = (bf16[32,7168]{1,0:T(8,128)(2,1)}, bf16[32,7168]{1,0:T(8,128)(2,1)S(1)}, u32[]{:S(2)}, u32[]{:S(2)}) collective-permute-start(bf16[32,7168]{1,0:T(8,128)(2,1)} %get-tuple-element.51), channel_id=1, source_target_pairs={{0,96},{16,112},{32,0},{48,16},{64,32},{80,48},{96,64},{112,80},{1... | collective-permute-start | bytes 1376264 | tf_op jit(solution)/shard_map/back_route/ppermute | solution.py:46
  144.9 51.6 %collective-permute-start.22 = (bf16[32,7168]{1,0:T(8,128)(2,1)}, bf16[32,7168]{1,0:T(8,128)(2,1)}, u32[]{:S(2)}, u32[]{:S(2)}) collective-permute-start(bf16[32,7168]{1,0:T(8,128)(2,1)} %get-tuple-element.52), channel_id=1, source_target_pairs={{0,64},{16,80},{32,96},{48,112},{64,0},{80,16},{96,32},{112,48},{1... | collective-permute-start | bytes 1376264 | tf_op jit(solution)/shard_map/back_route/ppermute | solution.py:46
  144.9 51.6 %collective-permute-start.23 = (bf16[32,7168]{1,0:T(8,128)(2,1)}, bf16[32,7168]{1,0:T(8,128)(2,1)}, u32[]{:S(2)}, u32[]{:S(2)}) collective-permute-start(bf16[32,7168]{1,0:T(8,128)(2,1)} %get-tuple-element.53), channel_id=1, source_target_pairs={{0,32},{16,48},{32,64},{48,80},{64,96},{80,112},{96,0},{112,16},{1... | collective-permute-start | bytes 1376264 | tf_op jit(solution)/shard_map/back_route/ppermute | solution.py:46
  146.7 49.8 %collective-permute-start.25 = (bf16[32,7168]{1,0:T(8,128)(2,1)S(1)}, bf16[32,7168]{1,0:T(8,128)(2,1)S(1)}, u32[]{:S(2)}, u32[]{:S(2)}) collective-permute-start(bf16[32,7168]{1,0:T(8,128)(2,1)S(1)} %get-tuple-element.64), channel_id=1, source_target_pairs={{0,96},{16,112},{32,0},{48,16},{64,32},{80,48},{96,64},{112,80},{1... | collective-permute-start | bytes 1376264 | tf_op jit(solution)/shard_map/back_route/ppermute | solution.py:46
  149.1 47.5 %collective-permute-start.26 = (bf16[32,7168]{1,0:T(8,128)(2,1)S(1)}, bf16[32,7168]{1,0:T(8,128)(2,1)S(1)}, u32[]{:S(2)}, u32[]{:S(2)}) collective-permute-start(bf16[32,7168]{1,0:T(8,128)(2,1)S(1)} %get-tuple-element.63), channel_id=1, source_target_pairs={{0,64},{16,80},{32,96},{48,112},{64,0},{80,16},{96,32},{112,48},{1... | collective-permute-start | bytes 1376264 | tf_op jit(solution)/shard_map/back_route/ppermute | solution.py:46
  165.7 0.8 copy-start.6
  166.5 30.1 %collective-permute-start.27 = (bf16[32,7168]{1,0:T(8,128)(2,1)S(1)}, bf16[32,7168]{1,0:T(8,128)(2,1)}, u32[]{:S(2)}, u32[]{:S(2)}) collective-permute-start(bf16[32,7168]{1,0:T(8,128)(2,1)S(1)} %get-tuple-element.62), channel_id=1, source_target_pairs={{0,32},{16,48},{32,64},{48,80},{64,96},{80,112},{96,0},{112,16},{1... | collective-permute-start | bytes 1376264 | tf_op jit(solution)/shard_map/back_route/ppermute | solution.py:46
  196.5 16.5 %collective-permute-start.17 = (bf16[32,7168]{1,0:T(8,128)(2,1)}, bf16[32,7168]{1,0:T(8,128)(2,1)S(1)}, u32[]{:S(2)}, u32[]{:S(2)}) collective-permute-start(bf16[32,7168]{1,0:T(8,128)(2,1)} %get-tuple-element.49), channel_id=1, source_target_pairs={{0,16},{16,0},{32,48},{48,32},{64,80},{80,64},{96,112},{112,96},{1... | collective-permute-start | bytes 1376264 | tf_op jit(solution)/shard_map/out_sum/ppermute | solution.py:50
  196.5 0.8 copy-start.8
  196.5 1.0 copy-start.9
  197.5 15.4 %copy-start.4 = (f32[32,7168]{1,0:T(8,128)S(1)}, f32[32,7168]{1,0:T(8,128)}, u32[]{:S(2)}) copy-start(f32[32,7168]{1,0:T(8,128)} %get-tuple-element.48) | copy-start | bytes 2752516
  206.1 26.3 %copy-start.5 = (bf16[32,14336]{1,0:T(8,128)(2,1)S(1)}, bf16[32,14336]{1,0:T(8,128)(2,1)}, u32[]{:S(2)}) copy-start(bf16[32,14336]{1,0:T(8,128)(2,1)} %get-tuple-element.56) | copy-start | bytes 2752516
  206.1 15.0 %collective-permute-start.30 = (bf16[32,14336]{1,0:T(8,128)(2,1)}, bf16[32,14336]{1,0:T(8,128)(2,1)S(1)}, u32[]{:S(2)}, u32[]{:S(2)}) collective-permute-start(bf16[32,14336]{1,0:T(8,128)(2,1)} %get-tuple-element.59), channel_id=1, source_target_pairs={{0,1},{1,2},{2,3},{3,0},{4,5},{5,6},{6,7},{7,4},{8,9},{9,10},{10,1... | collective-permute-start | bytes 2752520 | tf_op jit(solution)/shard_map/back_route/ppermute | solution.py:61
  206.4 26.0 %collective-permute-start.29 = (bf16[32,14336]{1,0:T(8,128)(2,1)}, bf16[32,14336]{1,0:T(8,128)(2,1)S(1)}, u32[]{:S(2)}, u32[]{:S(2)}) collective-permute-start(bf16[32,14336]{1,0:T(8,128)(2,1)} %get-tuple-element.58), channel_id=1, source_target_pairs={{0,2},{1,3},{2,0},{3,1},{4,6},{5,7},{6,4},{7,5},{8,10},{9,11},{10,... | collective-permute-start | bytes 2752520 | tf_op jit(solution)/shard_map/back_route/ppermute | solution.py:61
  211.0 21.4 %collective-permute-start.28 = (bf16[32,14336]{1,0:T(8,128)(2,1)}, bf16[32,14336]{1,0:T(8,128)(2,1)S(1)}, u32[]{:S(2)}, u32[]{:S(2)}) collective-permute-start(bf16[32,14336]{1,0:T(8,128)(2,1)} %get-tuple-element.57), channel_id=1, source_target_pairs={{0,3},{1,0},{2,1},{3,2},{4,7},{5,4},{6,5},{7,6},{8,11},{9,8},{10,9... | collective-permute-start | bytes 2752520 | tf_op jit(solution)/shard_map/back_route/ppermute | solution.py:61
  232.9 13.2 %collective-permute-start.33 = (bf16[8,14336]{1,0:T(8,128)(2,1)S(1)}, bf16[8,14336]{1,0:T(8,128)(2,1)S(1)}, u32[]{:S(2)}, u32[]{:S(2)}) collective-permute-start(bf16[8,14336]{1,0:T(8,128)(2,1)S(1)} %get-tuple-element.71), channel_id=1, source_target_pairs={{0,4},{1,5},{2,6},{3,7},{4,8},{5,9},{6,10},{7,11},{8,12},{9,13},{1... | collective-permute-start | bytes 688136 | tf_op jit(solution)/shard_map/back_route/ppermute | solution.py:61
  233.5 13.8 %collective-permute-start.32 = (bf16[8,14336]{1,0:T(8,128)(2,1)S(1)}, bf16[8,14336]{1,0:T(8,128)(2,1)S(1)}, u32[]{:S(2)}, u32[]{:S(2)}) collective-permute-start(bf16[8,14336]{1,0:T(8,128)(2,1)S(1)} %get-tuple-element.72), channel_id=1, source_target_pairs={{0,8},{1,9},{2,10},{3,11},{4,12},{5,13},{6,14},{7,15},{8,0},{9,1},... | collective-permute-start | bytes 688136 | tf_op jit(solution)/shard_map/back_route/ppermute | solution.py:61
  239.6 7.7 %collective-permute-start.31 = (bf16[8,14336]{1,0:T(8,128)(2,1)S(1)}, bf16[8,14336]{1,0:T(8,128)(2,1)S(1)}, u32[]{:S(2)}, u32[]{:S(2)}) collective-permute-start(bf16[8,14336]{1,0:T(8,128)(2,1)S(1)} %get-tuple-element.70), channel_id=1, source_target_pairs={{0,12},{1,13},{2,14},{3,15},{4,0},{5,1},{6,2},{7,3},{8,4},{9,5},{1... | collective-permute-start | bytes 688136 | tf_op jit(solution)/shard_map/back_route/ppermute | solution.py:61
  242.1 6.9 %collective-permute-start.20 = (bf16[8,7168]{1,0:T(8,128)(2,1)S(1)}, bf16[8,7168]{1,0:T(8,128)(2,1)S(1)}, u32[]{:S(2)}, u32[]{:S(2)}) collective-permute-start(bf16[8,7168]{1,0:T(8,128)(2,1)S(1)} %get-tuple-element.74), channel_id=1, source_target_pairs={{0,32},{16,48},{32,64},{48,80},{64,96},{80,112},{96,0},{112,16},{1... | collective-permute-start | bytes 344072 | tf_op jit(solution)/shard_map/out_sum/ppermute | solution.py:46
  244.5 6.3 %collective-permute-start.19 = (bf16[8,7168]{1,0:T(8,128)(2,1)S(1)}, bf16[8,7168]{1,0:T(8,128)(2,1)S(1)}, u32[]{:S(2)}, u32[]{:S(2)}) collective-permute-start(bf16[8,7168]{1,0:T(8,128)(2,1)S(1)} %get-tuple-element.75), channel_id=1, source_target_pairs={{0,64},{16,80},{32,96},{48,112},{64,0},{80,16},{96,32},{112,48},{1... | collective-permute-start | bytes 344072 | tf_op jit(solution)/shard_map/out_sum/ppermute | solution.py:46
  246.2 4.8 %collective-permute-start.18 = (bf16[8,7168]{1,0:T(8,128)(2,1)S(1)}, bf16[8,7168]{1,0:T(8,128)(2,1)S(1)}, u32[]{:S(2)}, u32[]{:S(2)}) collective-permute-start(bf16[8,7168]{1,0:T(8,128)(2,1)S(1)} %get-tuple-element.73), channel_id=1, source_target_pairs={{0,96},{16,112},{32,0},{48,16},{64,32},{80,48},{96,64},{112,80},{1... | collective-permute-start | bytes 344072 | tf_op jit(solution)/shard_map/out_sum/ppermute | solution.py:46

commit v2 on v1

--- a/solution.py
+++ b/solution.py
@@ -12,7 +12,8 @@
 CAP = 2
 N_Y, N_X, N_Z = 4, 4, 4
 INFO = 128
-BLK = 1792
+BLK = 3584
+CHUNK = 1792
 
 F32, BF16, I32 = jnp.float32, jnp.bfloat16, jnp.int32
 
@@ -44,6 +45,10 @@
 
 def move_y(v, k):
     return lax.ppermute(v, "grp", [(y * 2 + c, (y + k) % N_Y * 2 + c) for y in range(N_Y) for c in range(2)])
+
+
+def move_y_apart(v):
+    return lax.ppermute(v, "grp", [(y * 2 + c, (y + 1 - 2 * c) % N_Y * 2 + c) for y in range(N_Y) for c in range(2)])
 
 
 def swap_core(v):
@@ -120,16 +125,23 @@
     return jnp.where(taken, 1.0, 0.0).astype(BF16), jnp.where(taken, scale * (1.0 / 256.0), 0.0).astype(BF16)
 
 
-def cot_pick_kernel(at, g0, g1, i0, i1, sent, mix, hot):
+def cot_pick_kernel(at, g0, g1, g2, i0, i1, i2, sent, mix, hot):
     @pl.when(pl.program_id(0) == 0)
     def _():
         slot, _ = grid_ids(256, 64)
-        info = jnp.concatenate([i0[...], i1[...]], axis=0)
-        one, scaled = slots_of(info, at[0] * 8 + (slot >> 5), (slot >> 1) & 7, slot & 1)
-        hot[...] = one
+        to, i = grid_ids(64, 64)
+        near = 1 + 2 * (at[0] & 1)
+        far_near = 4 - near
+        came = jnp.zeros((64, 64), I32)
+        for n, block in enumerate((0, 4, near, 4 + near, 2, 4 + far_near, far_near, 6)):
+            came = jnp.where((i >> 3) == n, block, came)
+        order = jnp.where(((to >> 3) == came) & ((to & 7) == (i & 7)), 1.0, 0.0).astype(BF16)
+        info = jnp.concatenate([i0[...], i1[...], i2[...]], axis=0)
+        one, scaled = slots_of(dot(order, info).astype(BF16), at[0] * 8 + (slot >> 5), (slot >> 1) & 7, slot & 1)
+        hot[...] = dot(one, order).astype(BF16)
         mix[...] = scaled
 
-    sent[...] = dot(hot[...], jnp.concatenate([g0[...], g1[...]], axis=0)).astype(BF16)
+    sent[...] = dot(hot[...], jnp.concatenate([g0[...], g1[...], g2[...]], axis=0)).astype(BF16)
 
 
 def widen_kernel(tok, cot, routes, weights, all_, g):
@@ -172,51 +184,71 @@
     return jnp.where(to == ((x * 4 + z) * 8 + (i >> 5)) * 2 + (i & 1), 1.0, 0.0)
 
 
-def forward_kernel(at, *refs):
-    xs, (gw, uw, hid, act, slope, acc_g, acc_u) = refs[:8], refs[8:]
-    step = pl.program_id(0)
-
-    @pl.when(step == 0)
-    def _():
-        acc_g[...] = jnp.zeros_like(acc_g)
-        acc_u[...] = jnp.zeros_like(acc_u)
-
-    rows = jnp.concatenate([x[...] for x in xs], axis=0)
-    acc_g[...] += dot(rows, gw[0])
-    acc_u[...] += dot(rows, uw[0])
-
-    @pl.when(step == pl.num_programs(0) - 1)
-    def _():
-        silu, prime = silu_parts(acc_g[...])
-        act[...] = silu
-        slope[...] = acc_u[...] * prime
-        hid[...] = dot(order_of(at).astype(BF16), (silu * acc_u[...]).astype(BF16)).astype(BF16)
-
-
-def grad_kernel(at, g, dw, act, slope, dg, du, acc):
-    step = pl.program_id(0)
-
-    @pl.when(step == 0)
-    def _():
-        acc[...] = jnp.zeros_like(acc)
-
-    acc[...] += dot_t(g[...], dw[0])
-
-    @pl.when(step == pl.num_programs(0) - 1)
-    def _():
-        grad = lax.dot_general(
-            order_of(at), acc[...], (((0,), (0,)), ((), ())), precision=lax.Precision.HIGHEST, preferred_element_type=F32
-        )
-        dg[...] = (grad * slope[...]).astype(BF16)
-        du[...] = (grad * act[...]).astype(BF16)
-
-
-def backward_kernel(dg, du, hid, gw, uw, dw, *outs):
-    dx = (dot_t(dg[...], gw[0]) + dot_t(du[...], uw[0])).astype(BF16)
-    for n in range(4):
-        outs[n][...] = dx[n * 32 : n * 32 + 32]
-    outs[4][...] = dx[128:]
-    outs[5][...] = dot(hid[...], dw[0]).astype(BF16)
+def expert_kernel(at, *refs):
+    xs, (g_hbm, gw, uw, dw), dxs, (y_hbm,), (x, g, wg, wu, wd, y, dx, sem, sem_w, sem_o) = (
+        refs[:8],
+        refs[8:12],
+        refs[12:17],
+        refs[17:18],
+        refs[18:],
+    )
+    chunks, blk, hidden = wg.shape
+    cols = lambda c: pl.ds(pl.multiple_of(c * blk, blk), blk)
+    load_x = [pltpu.make_async_copy(v, x.at[pl.ds(n * 32, 32)], sem.at[n]) for n, v in enumerate(xs)]
+    load_g = pltpu.make_async_copy(g_hbm, g, sem.at[8])
+    load_1 = lambda c: pltpu.make_async_copy(gw.at[0, pl.ds(c * blk, blk)], wg.at[c], sem_w.at[0, c])
+    load_2 = lambda c: pltpu.make_async_copy(uw.at[0, pl.ds(c * blk, blk)], wu.at[c], sem_w.at[1, c])
+    load_3 = lambda c: pltpu.make_async_copy(dw.at[0, :, cols(c)], wd.at[c], sem_w.at[2, c])
+    send_y = lambda c: pltpu.make_async_copy(y.at[:, cols(c)], y_hbm.at[:, cols(c)], sem_o.at[0, c])
+    send_dx = [pltpu.make_async_copy(dx.at[pl.ds(n * 32, 32)], v, sem.at[9 + n]) for n, v in enumerate(dxs[:4])]
+    send_dx.append(pltpu.make_async_copy(dx.at[pl.ds(128, 128)], dxs[4], sem.at[13]))
+
+    for copy in load_x:
+        copy.start()
+    for c in range(chunks):
+        load_1(c).start()
+        load_2(c).start()
+    load_g.start()
+    for c in range(chunks):
+        load_3(c).start()
+    for copy in load_x:
+        copy.wait()
+
+    def pre(c, accs):
+        load_1(c).wait()
+        load_2(c).wait()
+        rows = x[:, cols(c)]
+        return accs[0] + dot(rows, wg[c]), accs[1] + dot(rows, wu[c])
+
+    zero = jnp.zeros((256, hidden), F32)
+    gate, up = lax.fori_loop(0, chunks, pre, (zero, zero))
+    silu, prime = silu_parts(gate)
+    order = order_of(at)
+    hid = dot(order.astype(BF16), (silu * up).astype(BF16)).astype(BF16)
+    load_g.wait()
+
+    def mid(c, acc):
+        load_3(c).wait()
+        y[:, cols(c)] = dot(hid, wd[c]).astype(BF16)
+        send_y(c).start()
+        return acc + dot_t(g[:, cols(c)], wd[c])
+
+    grad = lax.fori_loop(0, chunks, mid, zero)
+    grad = lax.dot_general(order, grad, (((0,), (0,)), ((), ())), precision=lax.Precision.HIGHEST, preferred_element_type=F32)
+    dg = (grad * (up * prime)).astype(BF16)
+    du = (grad * silu).astype(BF16)
+
+    def back(c, _):
+        dx[:, cols(c)] = (dot_t(dg, wg[c]) + dot_t(du, wu[c])).astype(BF16)
+        return 0
+
+    lax.fori_loop(0, chunks, back, 0)
+    for copy in send_dx:
+        copy.start()
+    for c in range(chunks):
+        send_y(c).wait()
+    for copy in send_dx:
+        copy.wait()
 
 
 def back_sum_kernel(*refs):
@@ -230,12 +262,12 @@
 
     @pl.when(step < half)
     def _():
+        put(dot(hid[...], sd[...]))
+
+    @pl.when(step >= half)
+    def _():
         rows = jnp.concatenate([v[...] for v in blocks], axis=0)
         put(dot_a(mix[...], rows) + dot(grads[...], jnp.concatenate([sg[...], su[...]], axis=0)))
-
-    @pl.when(step >= half)
-    def _():
-        put(dot(hid[...], sd[...]))
 
 
 def out_sum_kernel(rows, mix, mine, other):
@@ -309,14 +341,17 @@
     with jax.named_scope("gather_plane"):
         plane = ring(move_b, jnp.concatenate(all_line, axis=0))
     with jax.named_scope("cot_gather"):
-        g_line = jnp.concatenate(ring(move_y, g_wide), axis=0)
-        g_blocks = [g_line, swap_core(g_line)]
+        g_chip = jnp.concatenate([g_wide, swap_core(g_wide)], axis=0)
+        g_half = jnp.concatenate([move_y_apart(g_chip), move_y(g_wide, 2)], axis=0)
+        g_blocks = [g_chip, g_half, swap_core(g_half)]
 
     with jax.named_scope("cot_pick"):
         g_sent, g_mix = call(
             cot_pick_kernel,
             steps,
-            [SM(at)] + [(b, (32, BLK), COL) for b in g_blocks] + [(b, (32, INFO), info_at) for b in g_blocks],
+            [SM(at)]
+            + [(b, (b.shape[0], BLK), COL) for b in g_blocks]
+            + [(b, (b.shape[0], INFO), info_at) for b in g_blocks],
             [((256, width), BF16, (256, BLK), COL), ((256, 64), BF16, (256, 64), FIX)],
             [pltpu.VMEM((256, 64), BF16)],
             2 * 256 * 64 * width,
@@ -360,57 +395,29 @@
             after=[x_mix],
         )
 
-    row_at = lambda i: (0, i, 0)
-    col_at = lambda i: (0, 0, i)
-    pre = ((256, hidden), F32, (256, hidden), FIX)
-    mid = ((256, hidden), BF16, (256, hidden), FIX)
-    with jax.named_scope("expert_forward"):
-        hid, act, slope = call(
-            forward_kernel,
-            steps,
-            [SM(at)]
-            + [(x, (32, BLK), COL) for x in x_rows]
-            + [(expert_gate, (1, BLK, hidden), row_at), (expert_up, (1, BLK, hidden), row_at)],
-            [mid, pre, pre],
-            [pltpu.VMEM((256, hidden), F32), pltpu.VMEM((256, hidden), F32)],
-            4 * 256 * hidden * width,
-            2 * (256 + 2 * hidden) * width,
-            after=[s_hid],
-        )
-    with jax.named_scope("expert_grad"):
-        dg, du = call(
-            grad_kernel,
-            steps,
-            [
-                SM(at),
-                (g_rows, (256, BLK), COL),
-                (expert_down, (1, hidden, BLK), col_at),
-                (act, (256, hidden), FIX),
-                (slope, (256, hidden), FIX),
+    with jax.named_scope("expert"):
+        chunks = width // CHUNK
+        here = pl.BlockSpec(memory_space=pl.ANY)
+        *dx_rows, dx_over, y_rows = pl.pallas_call(
+            expert_kernel,
+            in_specs=[pl.BlockSpec(memory_space=pltpu.SMEM)] + [here] * 12,
+            out_specs=[here] * 6,
+            out_shape=[jax.ShapeDtypeStruct((32, width), BF16)] * 4
+            + [jax.ShapeDtypeStruct((128, width), BF16), jax.ShapeDtypeStruct((256, width), BF16)],
+            scratch_shapes=[
+                pltpu.VMEM((256, width), BF16),
+                pltpu.VMEM((256, width), BF16),
+                pltpu.VMEM((chunks, CHUNK, hidden), BF16),
+                pltpu.VMEM((chunks, CHUNK, hidden), BF16),
+                pltpu.VMEM((chunks, hidden, CHUNK), BF16),
+                pltpu.VMEM((256, width), BF16),
+                pltpu.VMEM((256, width), BF16),
+                pltpu.SemaphoreType.DMA((14,)),
+                pltpu.SemaphoreType.DMA((3, chunks)),
+                pltpu.SemaphoreType.DMA((1, chunks)),
             ],
-            [mid, mid],
-            [pltpu.VMEM((256, hidden), F32)],
-            2 * 256 * hidden * width,
-            2 * (256 + hidden) * width,
-        )
-    with jax.named_scope("expert_backward"):
-        *dx_rows, dx_over, y_rows = call(
-            backward_kernel,
-            steps,
-            [
-                (dg, (256, hidden), FIX),
-                (du, (256, hidden), FIX),
-                (hid, (256, hidden), FIX),
-                (expert_gate, (1, BLK, hidden), row_at),
-                (expert_up, (1, BLK, hidden), row_at),
-                (expert_down, (1, hidden, BLK), col_at),
-            ],
-            [((32, width), BF16, (32, BLK), COL)] * 4
-            + [((128, width), BF16, (128, BLK), COL), ((256, width), BF16, (256, BLK), COL)],
-            [],
-            6 * 256 * hidden * width,
-            2 * (512 + 3 * hidden) * width,
-        )
+            compiler_params=pltpu.CompilerParams(vmem_limit_bytes=60 * 1024 * 1024),
+        )(at, *x_rows, g_rows, expert_gate, expert_up, expert_down)
     with jax.named_scope("out_route"):
         y_home = lax.all_to_all(y_rows.reshape(16, 16, width), "exp", split_axis=0, concat_axis=0, tiled=True)
         y_home = y_home.reshape(256, width)
@@ -423,14 +430,14 @@
         parts = call(
             back_sum_kernel,
             2 * steps,
-            [(v, (32, BLK), first) for v in dx_home]
+            [(v, (32, BLK), later) for v in dx_home]
             + [
                 (x_mix, (256, 128), FIX),
                 (s_hid, (128, part), FIX),
                 (s_grads, (128, 2 * part), FIX),
-                (shared_gate.T, (part, BLK), first),
-                (shared_up.T, (part, BLK), first),
-                (shared_down, (part, BLK), later),
+                (shared_gate.T, (part, BLK), later),
+                (shared_up.T, (part, BLK), later),
+                (shared_down, (part, BLK), first),
             ],
             [((32, 2 * width), BF16, (32, BLK), COL)] * 4,
             [],
@@ -440,7 +447,7 @@
         )
         line = ring_sum(move_b, parts).astype(BF16).reshape(4, 8, 2 * width)
         both = ring_sum(move_a, [line[k] for k in range(4)])
-        token_grad, s_out = both[:, :width].astype(BF16), both[:, width:]
+        s_out, token_grad = both[:, :width], both[:, width:].astype(BF16)
     with jax.named_scope("out_sum"):
         mine, other = call(
             out_sum_kernel,

time: 252 us -> 255 us (1.012)
  waiting for transfers between devices: 113 us -> 133 us
  Pallas kernels: 61.5 us -> 50.7 us
  starting transfers between devices: 66.1 us -> 62.2 us
    pallas_call x9 -> x6, Pallas kernels: 61.5 us -> 25.3 us  [call(): pl.pallas_call(lambda *refs: kernel(*refs[skip:]), grid=(grid,), in_specs...]
    pallas_call x0 -> x1, Pallas kernels: none -> 25.4 us  [local(): pl.pallas_call(expert_kernel, in_specs=[pl.BlockSpec(memory_space=pltpu.S...]
    ppermute x12, waiting for transfers between devices: 37.3 us -> 49.3 us  [move_plane(): return lax.ppermute(v, ('grp', 'exp'), pairs)]
    all_to_all x1, waiting for transfers between devices: 25.4 us -> 33.4 us  [local(): lax.all_to_all(y_rows.reshape(16, 16, width), 'exp', split_axis=0, concat...]
    ppermute x12, starting transfers between devices: 28.3 us -> 24.1 us  [move_plane(): return lax.ppermute(v, ('grp', 'exp'), pairs)]
    all_to_all x1, starting transfers between devices: 6.87 us -> 10.5 us  [local(): lax.all_to_all(y_rows.reshape(16, 16, width), 'exp', split_axis=0, concat...]
    ppermute x18 -> x16, starting transfers between devices: 25.5 us -> 22.2 us  [move_y(): lax.ppermute(v, 'grp', [(y * 2 + c, (y + k) % N_Y * 2 + c) for y in range...]
    ppermute x18 -> x16, waiting for transfers between devices: 49.1 us -> 46.1 us  [move_y(): lax.ppermute(v, 'grp', [(y * 2 + c, (y + k) % N_Y * 2 + c) for y in range...]
  transfers between devices with their start and end apart: 36 -> 36, of which waited for: 15 -> 14; matrix products, arithmetic and copies ran while one was open for 2% -> 2% of each run, Pallas kernels for 13% -> 8%
where the time goes in v2:
time: 255 us
  waiting for transfers between devices  133 us (52%)
  starting transfers between devices  62.2 us (24%)
  Pallas kernels  50.7 us (20%)
  local copies, waits for them, and re-layouts  6.33 us (2%)
    ppermute x12, waiting for transfers between devices, move_plane(): return lax.ppermute(v, ('grp', 'exp'), pairs)  49.3 us
    ppermute x16, waiting for transfers between devices, move_y(): lax.ppermute(v, 'grp', [(y * 2 + c, (y + k) % N_Y * 2 + c) for y in range...  46.1 us
    all_to_all x1, waiting for transfers between devices, local(): lax.all_to_all(y_rows.reshape(16, 16, width), 'exp', split_axis=0, concat...  33.4 us
    pallas_call x1, Pallas kernels, local(): pl.pallas_call(expert_kernel, in_specs=[pl.BlockSpec(memory_space=pltpu.S...  25.4 us
    pallas_call x6, Pallas kernels, call(): pl.pallas_call(lambda *refs: kernel(*refs[skip:]), grid=(grid,), in_specs...  25.3 us
    ppermute x12, starting transfers between devices, move_plane(): return lax.ppermute(v, ('grp', 'exp'), pairs)  24.1 us
    ppermute x16, starting transfers between devices, move_y(): lax.ppermute(v, 'grp', [(y * 2 + c, (y + k) % N_Y * 2 + c) for y in range...  22.2 us
    all_to_all x1, starting transfers between devices, local(): lax.all_to_all(y_rows.reshape(16, 16, width), 'exp', split_axis=0, concat...  10.5 us
  transfers between devices with their start and end apart: 36, of which 14 were waited for; matrix products, arithmetic and copies ran while one was open for 2% of the time, Pallas kernels for 8%

profile of v2, /device:TPU:0, one launch (start us, length us, event | category | flops | bytes accessed | tf_op | source)
XLA Modules:
  0.0 254.9 jit_solution(9444568961310788558)
XLA Ops:
  0.6 1.8 widen.1
  2.5 3.3 %collective-permute-start.2 = (bf16[8,7296]{1,0:T(8,128)(2,1)}, bf16[8,7296]{1,0:T(8,128)(2,1)S(1)}, u32[]{:S(2)}, u32[]{:S(2)}) collective-permute-start(bf16[8,7296]{1,0:T(8,128)(2,1)} %get-tuple-element.26), channel_id=1, source_target_pairs={{0,64},{16,80},{32,96},{48,112},{64,0},{80,16},{96,32},{112,48},{1... | collective-permute-start | bytes 350216 | tf_op jit(solution)/shard_map/cot_gather/ppermute | solution.py:47
  5.7 2.8 %collective-permute-start.6 = (bf16[8,14464]{1,0:T(8,128)(2,1)}, bf16[8,14464]{1,0:T(8,128)(2,1)S(1)}, u32[]{:S(2)}, u32[]{:S(2)}) collective-permute-start(bf16[8,14464]{1,0:T(8,128)(2,1)} %get-tuple-element.28), channel_id=1, source_target_pairs={{0,12},{1,13},{2,14},{3,15},{4,0},{5,1},{6,2},{7,3},{8,4},{9,5},{1... | collective-permute-start | bytes 694280 | tf_op jit(solution)/shard_map/gather_line/ppermute | solution.py:66
  8.5 0.8 collective-permute-start.5
  9.3 0.9 collective-permute-start.4
  10.2 1.0 constant_dynamic-update-slice_fusion.7
  11.2 0.9 constant_dynamic-update-slice_fusion.1
  12.1 0.7 collective-permute-start.1
  12.9 5.9 %collective-permute-done.4 = bf16[8,14464]{1,0:T(8,128)(2,1)S(1)} collective-permute-done((bf16[8,14464]{1,0:T(8,128)(2,1)}, bf16[8,14464]{1,0:T(8,128)(2,1)S(1)}, u32[]{:S(2)}, u32[]{:S(2)}) %collective-permute-start.4) | collective-permute-done | bytes 231456 | tf_op jit(solution)/shard_map/gather_line/ppermute | solution.py:66
  18.8 4.1 %collective-permute-start.9 = (bf16[32,14464]{1,0:T(8,128)(2,1)S(1)}, bf16[32,14464]{1,0:T(8,128)(2,1)S(1)}, u32[]{:S(2)}, u32[]{:S(2)}) collective-permute-start(bf16[32,14464]{1,0:T(8,128)(2,1)S(1)} %constant_dynamic-update-slice_fusion.4.refs_2_.refs_6_.refs_1_.refs_5_), channel_id=1, source_target_pairs={{0,3},{1,0},{2,1},{3,2},{4,7},{5,4},{6,5},{7,6},{8,11},{9,8},{10,9... | collective-permute-start | bytes 2777096 | tf_op jit(solution)/shard_map/gather_plane/ppermute | solution.py:66
  22.9 1.3 collective-permute-start.7
  24.3 0.1 collective-permute-start.3
  24.4 0.7 pad_add_fusion.refs_0_.refs_1_.at
  25.0 1.1 collective-permute-done.3.refs_3_.refs_6_
  26.1 4.3 %cot_pick.1 = (bf16[256,7168]{1,0:T(8,128)(2,1)}, bf16[256,64]{1,0:T(8,128)(2,1)}) custom-call(s32[2]{0:T(128)} %pad_add_fusion.refs_0_.refs_1_.at, bf16[16,7296]{1,0:T(8,128)(2,1)} %copy-done.4, bf16[24,7296]{1,0:T(8,128)(2,1)} %copy-done.3, bf16[24,7296]{1,0:T(8,128)(2,1)} %collective-permute-done.3.refs_3_.refs_6_, bf16[16,7296]{1,0:T(8,128)(2,1)} %copy-done.4, ...), custom_call_target="tpu_custom_call" | custom-call | flops 234881024 | bytes 4587520 | tf_op jit(solution)/shard_map/cot_pick/pallas_call | solution.py:93
  30.4 13.4 %collective-permute-done.9.refs_5_.refs_9_.refs_4_.refs_8_ = bf16[32,14464]{1,0:T(8,128)(2,1)S(1)} collective-permute-done((bf16[32,14464]{1,0:T(8,128)(2,1)S(1)}, bf16[32,14464]{1,0:T(8,128)(2,1)S(1)}, u32[]{:S(2)}, u32[]{:S(2)}) %collective-permute-start.9) | collective-permute-done | bytes 925728 | tf_op jit(solution)/shard_map/gather_plane/ppermute | solution.py:66
  43.9 3.8 %collective-permute-done.7.refs_3_.refs_7_.refs_2_.refs_6_ = bf16[32,14464]{1,0:T(8,128)(2,1)} collective-permute-done((bf16[32,14464]{1,0:T(8,128)(2,1)S(1)}, bf16[32,14464]{1,0:T(8,128)(2,1)}, u32[]{:S(2)}, u32[]{:S(2)}) %collective-permute-start.7) | collective-permute-done | bytes 925728 | tf_op jit(solution)/shard_map/gather_plane/ppermute | solution.py:66
  47.7 4.3 %tok_pick.1 = (bf16[32,7168]{1,0:T(8,128)(2,1)}, bf16[32,7168]{1,0:T(8,128)(2,1)}, bf16[32,7168]{1,0:T(8,128)(2,1)}, bf16[32,7168]{1,0:T(8,128)(2,1)}, bf16[128,...) custom-call(bf16[256,64]{1,0:T(8,128)(2,1)} %get-tuple-element.27.refs_0_.refs_1_, s32[2]{0:T(128)} %pad_add_fusion.refs_0_.refs_1_.at, ...), custom_call_target="tpu_custom_call" | custom-call | flops 469762048 | bytes 5734400 | tf_op jit(solution)/shard_map/tok_pick/pallas_call | solution.py:93
  51.9 0.1 collective-permute-start.13
  52.0 4.5 %all-to-all-start = ((bf16[16,16,7168]{2,1,0:T(8,128)(2,1)}), bf16[16,16,7168]{2,1,0:T(8,128)(2,1)}, u32[]{:S(2)}, u32[]{:S(2)}) async-start(bf16[16,16,7168]{2,1,0:T(8,128)(2,1)} %bitcast.12), calls=%async_computation | async-start | bytes 7340032 | tf_op jit(solution)/shard_map/cot_route/all_to_all | solution.py:361
  56.6 0.7 collective-permute-start.10
  57.3 1.8 collective-permute-start.11
  59.1 0.9 collective-permute-start.12
  60.1 1.0 fusion.5
  61.0 1.3 collective-permute-start.16
  62.4 1.8 collective-permute-start.15
  64.2 26.4 %collective-permute-done.10.refs_1_ = bf16[32,7168]{1,0:T(8,128)(2,1)S(1)} collective-permute-done((bf16[32,7168]{1,0:T(8,128)(2,1)}, bf16[32,7168]{1,0:T(8,128)(2,1)S(1)}, u32[]{:S(2)}, u32[]{:S(2)}) %collective-permute-start.10) | collective-permute-done | bytes 458784 | tf_op jit(solution)/shard_map/tok_route/ppermute | solution.py:47
  90.7 1.3 collective-permute-done.16.refs_7_
  92.0 11.9 %collective-permute-done.14.refs_5_ = bf16[32,7168]{1,0:T(8,128)(2,1)S(1)} collective-permute-done((bf16[32,7168]{1,0:T(8,128)(2,1)S(1)}, bf16[32,7168]{1,0:T(8,128)(2,1)S(1)}, u32[]{:S(2)}, u32[]{:S(2)}) %collective-permute-start.14) | collective-permute-done | bytes 458784 | tf_op jit(solution)/shard_map/tok_route/ppermute | solution.py:47
  103.9 2.7 %all-to-all-done = bf16[16,16,7168]{2,1,0:T(8,128)(2,1)} async-done(((bf16[16,16,7168]{2,1,0:T(8,128)(2,1)}), bf16[16,16,7168]{2,1,0:T(8,128)(2,1)}, u32[]{:S(2)}, u32[]{:S(2)}) %all-to-all-start) | async-done | bytes 3670048 | tf_op jit(solution)/shard_map/cot_route/all_to_all | solution.py:361
  106.7 25.4 %expert.1 = (bf16[32,7168]{1,0:T(8,128)(2,1)}, bf16[32,7168]{1,0:T(8,128)(2,1)}, bf16[32,7168]{1,0:T(8,128)(2,1)}, bf16[32,7168]{1,0:T(8,128)(2,1)}, bf16[128,71...) custom-call(s32[2]{0:T(128)} %pad_add_fusion.refs_0_.refs_1_.at, bf16[32,7168]{1,0:T(8,128)(2,1)} %get-tuple-element.29.refs_0_, ...), custom_call_target="tpu_custom_call" | custom-call | tf_op jit(solution)/shard_map/expert/pallas_call | solution.py:401
  132.1 0.1 collective-permute-start.24
  132.2 10.5 %all-to-all-start.1 = ((bf16[16,16,7168]{2,1,0:T(8,128)(2,1)}), bf16[16,16,7168]{2,1,0:T(8,128)(2,1)}, u32[]{:S(2)}, u32[]{:S(2)}) async-start(bf16[16,16,7168]{2,1,0:T(8,128)(2,1)} %bitcast.13), calls=%async_computation.1 | async-start | bytes 7340032 | tf_op jit(solution)/shard_map/out_route/all_to_all | solution.py:422
  142.7 1.1 collective-permute-start.21
  143.8 1.7 collective-permute-start.22
  145.5 0.9 fusion.4
  146.4 1.8 collective-permute-start.27
  148.2 2.9 %collective-permute-start.26 = (bf16[32,7168]{1,0:T(8,128)(2,1)S(1)}, bf16[32,7168]{1,0:T(8,128)(2,1)S(1)}, u32[]{:S(2)}, u32[]{:S(2)}) collective-permute-start(bf16[32,7168]{1,0:T(8,128)(2,1)S(1)} %get-tuple-element.53), channel_id=1, source_target_pairs={{0,64},{16,80},{32,96},{48,112},{64,0},{80,16},{96,32},{112,48},{1... | collective-permute-start | bytes 1376264 | tf_op jit(solution)/shard_map/back_route/ppermute | solution.py:47
  151.1 5.2 %collective-permute-done.21.refs_2_ = bf16[32,7168]{1,0:T(8,128)(2,1)S(1)} collective-permute-done((bf16[32,7168]{1,0:T(8,128)(2,1)}, bf16[32,7168]{1,0:T(8,128)(2,1)S(1)}, u32[]{:S(2)}, u32[]{:S(2)}) %collective-permute-start.21) | collective-permute-done | bytes 458784 | tf_op jit(solution)/shard_map/back_route/ppermute | solution.py:47
  156.3 0.8 copy-done.13
  157.1 1.9 collective-permute-start.25
  159.0 33.4 %all-to-all-done.1 = bf16[16,16,7168]{2,1,0:T(8,128)(2,1)} async-done(((bf16[16,16,7168]{2,1,0:T(8,128)(2,1)}), bf16[16,16,7168]{2,1,0:T(8,128)(2,1)}, u32[]{:S(2)}, u32[]{:S(2)}) %all-to-all-start.1) | async-done | bytes 3670048 | tf_op jit(solution)/shard_map/out_route/all_to_all | solution.py:422
  192.3 3.4 %out_sum.1 = (f32[32,7168]{1,0:T(8,128)}, bf16[32,7168]{1,0:T(8,128)(2,1)}) custom-call(bf16[256,7168]{1,0:T(8,128)(2,1)} %bitcast.5.refs_0_, bf16[256,64]{1,0:T(8,128)(2,1)} %get-tuple-element.27.refs_0_.refs_1_), custom_call_target="tpu_custom_call" | custom-call | flops 234881024 | bytes 5046272 | tf_op jit(solution)/shard_map/out_sum/pallas_call | solution.py:93
  195.7 4.4 %shared.1 = (bf16[128,64]{1,0:T(8,128)(2,1)}, bf16[128,128]{1,0:T(8,128)(2,1)}) custom-call(bf16[256,128]{1,0:T(8,128)(2,1)} %get-tuple-element.43.refs_0_.refs_9_, bf16[32,14464]{1,0:T(8,128)(2,1)} %copy-done, bf16[32,14464]{1,0:T(8,128)(2,1)} %collective-permute-done.7.refs_3_.refs_7_.refs_2_.refs_6_, bf16[32,14464]{1,0:T(8,128)(2,1)} %copy-done.2, ...), custom_call_target="tpu_custom_call" | custom-call | flops 352321536 | bytes 6451200 | tf_op jit(solution)/shard_map/shared/pallas_call | solution.py:93
  200.2 0.7 copy-done.14
  200.9 0.2 copy-done.15
  201.0 7.2 %back_route.1 = (bf16[32,14336]{1,0:T(8,128)(2,1)}, bf16[32,14336]{1,0:T(8,128)(2,1)}, bf16[32,14336]{1,0:T(8,128)(2,1)}, bf16[32,14336]{1,0:T(8,128)(2,1)}) custom-call(bf16[256,7168]{1,0:T(8,128)(2,1)} %bitcast.5.refs_0_, bf16[32,7168]{1,0:T(8,128)(2,1)} %get-tuple-element.38.refs_1_, bf16[32,7168]{1,0:T(8,128)(2,1)} %copy-done.13, ...), custom_call_target="tpu_custom_call" | custom-call | flops 469762048 | bytes 5734400 | tf_op jit(solution)/shard_map/back_route/pallas_call | solution.py:93
  208.2 3.4 %collective-permute-start.28 = (bf16[32,14336]{1,0:T(8,128)(2,1)}, bf16[32,14336]{1,0:T(8,128)(2,1)S(1)}, u32[]{:S(2)}, u32[]{:S(2)}) collective-permute-start(bf16[32,14336]{1,0:T(8,128)(2,1)} %get-tuple-element.47), channel_id=1, source_target_pairs={{0,3},{1,0},{2,1},{3,2},{4,7},{5,4},{6,5},{7,6},{8,11},{9,8},{10,9... | collective-permute-start | bytes 2752520 | tf_op jit(solution)/shard_map/back_route/ppermute | solution.py:66
  211.7 0.9 collective-permute-start.29
  212.5 1.3 collective-permute-start.30
  213.9 0.1 fusion.3
  214.0 18.7 %collective-permute-done.28 = bf16[32,14336]{1,0:T(8,128)(2,1)S(1)} collective-permute-done((bf16[32,14336]{1,0:T(8,128)(2,1)}, bf16[32,14336]{1,0:T(8,128)(2,1)S(1)}, u32[]{:S(2)}, u32[]{:S(2)}) %collective-permute-start.28) | collective-permute-done | bytes 917536 | tf_op jit(solution)/shard_map/back_route/ppermute | solution.py:66
  232.7 3.9 %collective-permute-done.30 = bf16[32,14336]{1,0:T(8,128)(2,1)S(1)} collective-permute-done((bf16[32,14336]{1,0:T(8,128)(2,1)}, bf16[32,14336]{1,0:T(8,128)(2,1)S(1)}, u32[]{:S(2)}, u32[]{:S(2)}) %collective-permute-start.30) | collective-permute-done | bytes 917536 | tf_op jit(solution)/shard_map/back_route/ppermute | solution.py:66
  236.6 0.4 add_convert_fusion
  237.1 3.0 %collective-permute-start.31 = (bf16[8,14336]{1,0:T(8,128)(2,1)S(1)}, bf16[8,14336]{1,0:T(8,128)(2,1)S(1)}, u32[]{:S(2)}, u32[]{:S(2)}) collective-permute-start(bf16[8,14336]{1,0:T(8,128)(2,1)S(1)} %get-tuple-element.60), channel_id=1, source_target_pairs={{0,12},{1,13},{2,14},{3,15},{4,0},{5,1},{6,2},{7,3},{8,4},{9,5},{1... | collective-permute-start | bytes 688136 | tf_op jit(solution)/shard_map/back_route/ppermute | solution.py:66
  240.1 5.6 %collective-permute-start.32 = (bf16[8,14336]{1,0:T(8,128)(2,1)S(1)}, bf16[8,14336]{1,0:T(8,128)(2,1)S(1)}, u32[]{:S(2)}, u32[]{:S(2)}) collective-permute-start(bf16[8,14336]{1,0:T(8,128)(2,1)S(1)} %get-tuple-element.62), channel_id=1, source_target_pairs={{0,8},{1,9},{2,10},{3,11},{4,12},{5,13},{6,14},{7,15},{8,0},{9,1},... | collective-permute-start | bytes 688136 | tf_op jit(solution)/shard_map/back_route/ppermute | solution.py:66
  245.7 1.1 collective-permute-start.18
  246.9 1.0 collective-permute-start.20
  247.8 0.7 collective-permute-start.19
  248.6 3.6 %collective-permute-done.32 = bf16[8,14336]{1,0:T(8,128)(2,1)S(1)} collective-permute-done((bf16[8,14336]{1,0:T(8,128)(2,1)S(1)}, bf16[8,14336]{1,0:T(8,128)(2,1)S(1)}, u32[]{:S(2)}, u32[]{:S(2)}) %collective-permute-start.32) | collective-permute-done | bytes 229408 | tf_op jit(solution)/shard_map/back_route/ppermute | solution.py:66
  252.2 0.1 convert_add_fusion.1
  252.3 0.7 slice.114
  252.9 1.2 collective-permute-done.19
  254.1 0.7 fusion
  (65 shorter events, 0.3 us)
Async XLA Ops:
  2.5 21.8 %collective-permute-start.2 = (bf16[8,7296]{1,0:T(8,128)(2,1)}, bf16[8,7296]{1,0:T(8,128)(2,1)S(1)}, u32[]{:S(2)}, u32[]{:S(2)}) collective-permute-start(bf16[8,7296]{1,0:T(8,128)(2,1)} %get-tuple-element.26), channel_id=1, source_target_pairs={{0,64},{16,80},{32,96},{48,112},{64,0},{80,16},{96,32},{112,48},{1... | collective-permute-start | bytes 350216 | tf_op jit(solution)/shard_map/cot_gather/ppermute | solution.py:47
  5.7 6.4 %collective-permute-start = (bf16[8,7296]{1,0:T(8,128)(2,1)}, bf16[8,7296]{1,0:T(8,128)(2,1)S(1)}, u32[]{:S(2)}, u32[]{:S(2)}) collective-permute-start(bf16[8,7296]{1,0:T(8,128)(2,1)} %get-tuple-element.26), channel_id=1, source_target_pairs={{0,16},{16,0},{32,48},{48,32},{64,80},{80,64},{96,112},{112,96},{1... | collective-permute-start | bytes 350216 | tf_op jit(solution)/shard_map/cot_gather/ppermute | solution.py:55
  5.7 13.1 %collective-permute-start.6 = (bf16[8,14464]{1,0:T(8,128)(2,1)}, bf16[8,14464]{1,0:T(8,128)(2,1)S(1)}, u32[]{:S(2)}, u32[]{:S(2)}) collective-permute-start(bf16[8,14464]{1,0:T(8,128)(2,1)} %get-tuple-element.28), channel_id=1, source_target_pairs={{0,12},{1,13},{2,14},{3,15},{4,0},{5,1},{6,2},{7,3},{8,4},{9,5},{1... | collective-permute-start | bytes 694280 | tf_op jit(solution)/shard_map/gather_line/ppermute | solution.py:66
  8.5 10.3 %collective-permute-start.5 = (bf16[8,14464]{1,0:T(8,128)(2,1)}, bf16[8,14464]{1,0:T(8,128)(2,1)S(1)}, u32[]{:S(2)}, u32[]{:S(2)}) collective-permute-start(bf16[8,14464]{1,0:T(8,128)(2,1)} %get-tuple-element.28), channel_id=1, source_target_pairs={{0,8},{1,9},{2,10},{3,11},{4,12},{5,13},{6,14},{7,15},{8,0},{9,1},... | collective-permute-start | bytes 694280 | tf_op jit(solution)/shard_map/gather_line/ppermute | solution.py:66
  9.3 9.4 %collective-permute-start.4 = (bf16[8,14464]{1,0:T(8,128)(2,1)}, bf16[8,14464]{1,0:T(8,128)(2,1)S(1)}, u32[]{:S(2)}, u32[]{:S(2)}) collective-permute-start(bf16[8,14464]{1,0:T(8,128)(2,1)} %get-tuple-element.28), channel_id=1, source_target_pairs={{0,4},{1,5},{2,6},{3,7},{4,8},{5,9},{6,10},{7,11},{8,12},{9,13},{1... | collective-permute-start | bytes 694280 | tf_op jit(solution)/shard_map/gather_line/ppermute | solution.py:66
  12.1 14.0 %copy-start.4 = (bf16[16,7296]{1,0:T(8,128)(2,1)}, bf16[16,7296]{1,0:T(8,128)(2,1)S(1)}, u32[]{:S(2)}) copy-start(bf16[16,7296]{1,0:T(8,128)(2,1)S(1)} %constant_dynamic-update-slice_fusion.refs_1_.refs_4_) | copy-start | bytes 700420
  12.1 12.1 %collective-permute-start.1 = (bf16[16,7296]{1,0:T(8,128)(2,1)S(1)}, bf16[16,7296]{1,0:T(8,128)(2,1)S(1)}, u32[]{:S(2)}, u32[]{:S(2)}) collective-permute-start(bf16[16,7296]{1,0:T(8,128)(2,1)S(1)} %constant_dynamic-update-slice_fusion.refs_1_.refs_4_), channel_id=1, source_target_pairs={{0,32},{16,112},{32,64},{48,16},{64,96},{80,48},{96,0},{112,80},{1... | collective-permute-start | bytes 700424 | tf_op jit(solution)/shard_map/cot_gather/ppermute | solution.py:51
  18.8 28.8 %copy-start = (bf16[32,14464]{1,0:T(8,128)(2,1)}, bf16[32,14464]{1,0:T(8,128)(2,1)S(1)}, u32[]{:S(2)}) copy-start(bf16[32,14464]{1,0:T(8,128)(2,1)S(1)} %constant_dynamic-update-slice_fusion.4.refs_2_.refs_6_.refs_1_.refs_5_) | copy-start | bytes 2777092
  18.8 25.0 %collective-permute-start.9 = (bf16[32,14464]{1,0:T(8,128)(2,1)S(1)}, bf16[32,14464]{1,0:T(8,128)(2,1)S(1)}, u32[]{:S(2)}, u32[]{:S(2)}) collective-permute-start(bf16[32,14464]{1,0:T(8,128)(2,1)S(1)} %constant_dynamic-update-slice_fusion.4.refs_2_.refs_6_.refs_1_.refs_5_), channel_id=1, source_target_pairs={{0,3},{1,0},{2,1},{3,2},{4,7},{5,4},{6,5},{7,6},{8,11},{9,8},{10,9... | collective-permute-start | bytes 2777096 | tf_op jit(solution)/shard_map/gather_plane/ppermute | solution.py:66
  22.9 20.9 %collective-permute-start.8 = (bf16[32,14464]{1,0:T(8,128)(2,1)S(1)}, bf16[32,14464]{1,0:T(8,128)(2,1)S(1)}, u32[]{:S(2)}, u32[]{:S(2)}) collective-permute-start(bf16[32,14464]{1,0:T(8,128)(2,1)S(1)} %constant_dynamic-update-slice_fusion.4.refs_2_.refs_6_.refs_1_.refs_5_), channel_id=1, source_target_pairs={{0,2},{1,3},{2,0},{3,1},{4,6},{5,7},{6,4},{7,5},{8,10},{9,11},{10,... | collective-permute-start | bytes 2777096 | tf_op jit(solution)/shard_map/gather_plane/ppermute | solution.py:66
  22.9 24.7 %collective-permute-start.7 = (bf16[32,14464]{1,0:T(8,128)(2,1)S(1)}, bf16[32,14464]{1,0:T(8,128)(2,1)}, u32[]{:S(2)}, u32[]{:S(2)}) collective-permute-start(bf16[32,14464]{1,0:T(8,128)(2,1)S(1)} %constant_dynamic-update-slice_fusion.4.refs_2_.refs_6_.refs_1_.refs_5_), channel_id=1, source_target_pairs={{0,1},{1,2},{2,3},{3,0},{4,5},{5,6},{6,7},{7,4},{8,9},{9,10},{10,1... | collective-permute-start | bytes 2777096 | tf_op jit(solution)/shard_map/gather_plane/ppermute | solution.py:66
  24.3 1.9 copy-start.3
  24.3 1.9 collective-permute-start.3
  43.9 3.8 %copy-start.1 = (bf16[32,14464]{1,0:T(8,128)(2,1)}, bf16[32,14464]{1,0:T(8,128)(2,1)S(1)}, u32[]{:S(2)}) copy-start(bf16[32,14464]{1,0:T(8,128)(2,1)S(1)} %collective-permute-done.9.refs_5_.refs_9_.refs_4_.refs_8_) | copy-start | bytes 2777092
  43.9 3.8 %copy-start.2 = (bf16[32,14464]{1,0:T(8,128)(2,1)}, bf16[32,14464]{1,0:T(8,128)(2,1)S(1)}, u32[]{:S(2)}) copy-start(bf16[32,14464]{1,0:T(8,128)(2,1)S(1)} %collective-permute-done.8.refs_4_.refs_8_.refs_3_.refs_7_) | copy-start | bytes 2777092
  51.9 8.1 %collective-permute-start.13 = (bf16[128,7168]{1,0:T(8,128)(2,1)}, bf16[128,7168]{1,0:T(8,128)(2,1)S(1)}, u32[]{:S(2)}, u32[]{:S(2)}) collective-permute-start(bf16[128,7168]{1,0:T(8,128)(2,1)} %get-tuple-element.33), channel_id=1, source_target_pairs={{0,16},{16,0},{32,48},{48,32},{64,80},{80,64},{96,112},{112,96},{1... | collective-permute-start | bytes 5505032 | tf_op jit(solution)/shard_map/tok_route/ppermute | solution.py:55
  52.0 54.6 %all-to-all-start = ((bf16[16,16,7168]{2,1,0:T(8,128)(2,1)}), bf16[16,16,7168]{2,1,0:T(8,128)(2,1)}, u32[]{:S(2)}, u32[]{:S(2)}) async-start(bf16[16,16,7168]{2,1,0:T(8,128)(2,1)} %bitcast.12), calls=%async_computation | async-start | bytes 7340032 | tf_op jit(solution)/shard_map/cot_route/all_to_all | solution.py:361
  56.6 34.1 %collective-permute-start.10 = (bf16[32,7168]{1,0:T(8,128)(2,1)}, bf16[32,7168]{1,0:T(8,128)(2,1)S(1)}, u32[]{:S(2)}, u32[]{:S(2)}) collective-permute-start(bf16[32,7168]{1,0:T(8,128)(2,1)} %get-tuple-element.30), channel_id=1, source_target_pairs={{0,32},{16,48},{32,64},{48,80},{64,96},{80,112},{96,0},{112,16},{1... | collective-permute-start | bytes 1376264 | tf_op jit(solution)/shard_map/tok_route/ppermute | solution.py:47
  57.3 33.3 %collective-permute-start.11 = (bf16[32,7168]{1,0:T(8,128)(2,1)}, bf16[32,7168]{1,0:T(8,128)(2,1)S(1)}, u32[]{:S(2)}, u32[]{:S(2)}) collective-permute-start(bf16[32,7168]{1,0:T(8,128)(2,1)} %get-tuple-element.31), channel_id=1, source_target_pairs={{0,64},{16,80},{32,96},{48,112},{64,0},{80,16},{96,32},{112,48},{1... | collective-permute-start | bytes 1376264 | tf_op jit(solution)/shard_map/tok_route/ppermute | solution.py:47
  59.1 31.5 %collective-permute-start.12 = (bf16[32,7168]{1,0:T(8,128)(2,1)}, bf16[32,7168]{1,0:T(8,128)(2,1)S(1)}, u32[]{:S(2)}, u32[]{:S(2)}) collective-permute-start(bf16[32,7168]{1,0:T(8,128)(2,1)} %get-tuple-element.32), channel_id=1, source_target_pairs={{0,96},{16,112},{32,0},{48,16},{64,32},{80,48},{96,64},{112,80},{1... | collective-permute-start | bytes 1376264 | tf_op jit(solution)/shard_map/tok_route/ppermute | solution.py:47
  61.0 30.9 %collective-permute-start.16 = (bf16[32,7168]{1,0:T(8,128)(2,1)S(1)}, bf16[32,7168]{1,0:T(8,128)(2,1)S(1)}, u32[]{:S(2)}, u32[]{:S(2)}) collective-permute-start(bf16[32,7168]{1,0:T(8,128)(2,1)S(1)} %get-tuple-element.56), channel_id=1, source_target_pairs={{0,96},{16,112},{32,0},{48,16},{64,32},{80,48},{96,64},{112,80},{1... | collective-permute-start | bytes 1376264 | tf_op jit(solution)/shard_map/tok_route/ppermute | solution.py:47
  62.4 29.6 %collective-permute-start.15 = (bf16[32,7168]{1,0:T(8,128)(2,1)S(1)}, bf16[32,7168]{1,0:T(8,128)(2,1)S(1)}, u32[]{:S(2)}, u32[]{:S(2)}) collective-permute-start(bf16[32,7168]{1,0:T(8,128)(2,1)S(1)} %get-tuple-element.57), channel_id=1, source_target_pairs={{0,64},{16,80},{32,96},{48,112},{64,0},{80,16},{96,32},{112,48},{1... | collective-permute-start | bytes 1376264 | tf_op jit(solution)/shard_map/tok_route/ppermute | solution.py:47
  90.6 16.0 %copy-start.7 = (bf16[32,7168]{1,0:T(8,128)(2,1)}, bf16[32,7168]{1,0:T(8,128)(2,1)S(1)}, u32[]{:S(2)}) copy-start(bf16[32,7168]{1,0:T(8,128)(2,1)S(1)} %collective-permute-done.10.refs_1_) | copy-start | bytes 1376260
  90.6 13.3 %collective-permute-start.14 = (bf16[32,7168]{1,0:T(8,128)(2,1)S(1)}, bf16[32,7168]{1,0:T(8,128)(2,1)S(1)}, u32[]{:S(2)}, u32[]{:S(2)}) collective-permute-start(bf16[32,7168]{1,0:T(8,128)(2,1)S(1)} %get-tuple-element.58), channel_id=1, source_target_pairs={{0,32},{16,48},{32,64},{48,80},{64,96},{80,112},{96,0},{112,16},{1... | collective-permute-start | bytes 1376264 | tf_op jit(solution)/shard_map/tok_route/ppermute | solution.py:47
  90.6 16.0 %copy-start.8 = (bf16[32,7168]{1,0:T(8,128)(2,1)}, bf16[32,7168]{1,0:T(8,128)(2,1)S(1)}, u32[]{:S(2)}) copy-start(bf16[32,7168]{1,0:T(8,128)(2,1)S(1)} %collective-permute-done.11.refs_2_) | copy-start | bytes 1376260
  90.7 16.0 %copy-start.9 = (bf16[32,7168]{1,0:T(8,128)(2,1)}, bf16[32,7168]{1,0:T(8,128)(2,1)S(1)}, u32[]{:S(2)}) copy-start(bf16[32,7168]{1,0:T(8,128)(2,1)S(1)} %collective-permute-done.12.refs_3_) | copy-start | bytes 1376260
  92.0 14.7 %copy-start.10 = (bf16[32,7168]{1,0:T(8,128)(2,1)}, bf16[32,7168]{1,0:T(8,128)(2,1)S(1)}, u32[]{:S(2)}) copy-start(bf16[32,7168]{1,0:T(8,128)(2,1)S(1)} %collective-permute-done.16.refs_7_) | copy-start | bytes 1376260
  92.0 14.7 %copy-start.11 = (bf16[32,7168]{1,0:T(8,128)(2,1)}, bf16[32,7168]{1,0:T(8,128)(2,1)S(1)}, u32[]{:S(2)}) copy-start(bf16[32,7168]{1,0:T(8,128)(2,1)S(1)} %collective-permute-done.15.refs_6_) | copy-start | bytes 1376260
  103.9 2.8 %copy-start.12 = (bf16[32,7168]{1,0:T(8,128)(2,1)}, bf16[32,7168]{1,0:T(8,128)(2,1)S(1)}, u32[]{:S(2)}) copy-start(bf16[32,7168]{1,0:T(8,128)(2,1)S(1)} %collective-permute-done.14.refs_5_) | copy-start | bytes 1376260
  132.1 13.4 %collective-permute-start.24 = (bf16[128,7168]{1,0:T(8,128)(2,1)}, bf16[128,7168]{1,0:T(8,128)(2,1)S(1)}, u32[]{:S(2)}, u32[]{:S(2)}) collective-permute-start(bf16[128,7168]{1,0:T(8,128)(2,1)} %get-tuple-element.42), channel_id=1, source_target_pairs={{0,16},{16,0},{32,48},{48,32},{64,80},{80,64},{96,112},{112,96},{1... | collective-permute-start | bytes 5505032 | tf_op jit(solution)/shard_map/back_route/ppermute | solution.py:55
  132.2 60.1 %all-to-all-start.1 = ((bf16[16,16,7168]{2,1,0:T(8,128)(2,1)}), bf16[16,16,7168]{2,1,0:T(8,128)(2,1)}, u32[]{:S(2)}, u32[]{:S(2)}) async-start(bf16[16,16,7168]{2,1,0:T(8,128)(2,1)} %bitcast.13), calls=%async_computation.1 | async-start | bytes 7340032 | tf_op jit(solution)/shard_map/out_route/all_to_all | solution.py:422
  142.7 13.6 %collective-permute-start.21 = (bf16[32,7168]{1,0:T(8,128)(2,1)}, bf16[32,7168]{1,0:T(8,128)(2,1)S(1)}, u32[]{:S(2)}, u32[]{:S(2)}) collective-permute-start(bf16[32,7168]{1,0:T(8,128)(2,1)} %get-tuple-element.39), channel_id=1, source_target_pairs={{0,96},{16,112},{32,0},{48,16},{64,32},{80,48},{96,64},{112,80},{1... | collective-permute-start | bytes 1376264 | tf_op jit(solution)/shard_map/back_route/ppermute | solution.py:47
  143.8 51.9 %collective-permute-start.22 = (bf16[32,7168]{1,0:T(8,128)(2,1)}, bf16[32,7168]{1,0:T(8,128)(2,1)}, u32[]{:S(2)}, u32[]{:S(2)}) collective-permute-start(bf16[32,7168]{1,0:T(8,128)(2,1)} %get-tuple-element.40), channel_id=1, source_target_pairs={{0,64},{16,80},{32,96},{48,112},{64,0},{80,16},{96,32},{112,48},{1... | collective-permute-start | bytes 1376264 | tf_op jit(solution)/shard_map/back_route/ppermute | solution.py:47
  145.5 54.6 %collective-permute-start.23 = (bf16[32,7168]{1,0:T(8,128)(2,1)}, bf16[32,7168]{1,0:T(8,128)(2,1)}, u32[]{:S(2)}, u32[]{:S(2)}) collective-permute-start(bf16[32,7168]{1,0:T(8,128)(2,1)} %get-tuple-element.41), channel_id=1, source_target_pairs={{0,32},{16,48},{32,64},{48,80},{64,96},{80,112},{96,0},{112,16},{1... | collective-permute-start | bytes 1376264 | tf_op jit(solution)/shard_map/back_route/ppermute | solution.py:47
  146.4 53.7 %collective-permute-start.27 = (bf16[32,7168]{1,0:T(8,128)(2,1)S(1)}, bf16[32,7168]{1,0:T(8,128)(2,1)S(1)}, u32[]{:S(2)}, u32[]{:S(2)}) collective-permute-start(bf16[32,7168]{1,0:T(8,128)(2,1)S(1)} %get-tuple-element.52), channel_id=1, source_target_pairs={{0,32},{16,48},{32,64},{48,80},{64,96},{80,112},{96,0},{112,16},{1... | collective-permute-start | bytes 1376264 | tf_op jit(solution)/shard_map/back_route/ppermute | solution.py:47
  148.2 51.9 %collective-permute-start.26 = (bf16[32,7168]{1,0:T(8,128)(2,1)S(1)}, bf16[32,7168]{1,0:T(8,128)(2,1)S(1)}, u32[]{:S(2)}, u32[]{:S(2)}) collective-permute-start(bf16[32,7168]{1,0:T(8,128)(2,1)S(1)} %get-tuple-element.53), channel_id=1, source_target_pairs={{0,64},{16,80},{32,96},{48,112},{64,0},{80,16},{96,32},{112,48},{1... | collective-permute-start | bytes 1376264 | tf_op jit(solution)/shard_map/back_route/ppermute | solution.py:47
  156.3 0.8 copy-start.13
  157.1 43.0 %collective-permute-start.25 = (bf16[32,7168]{1,0:T(8,128)(2,1)S(1)}, bf16[32,7168]{1,0:T(8,128)(2,1)}, u32[]{:S(2)}, u32[]{:S(2)}) collective-permute-start(bf16[32,7168]{1,0:T(8,128)(2,1)S(1)} %get-tuple-element.54), channel_id=1, source_target_pairs={{0,96},{16,112},{32,0},{48,16},{64,32},{80,48},{96,64},{112,80},{1... | collective-permute-start | bytes 1376264 | tf_op jit(solution)/shard_map/back_route/ppermute | solution.py:47
  195.7 18.2 %collective-permute-start.17 = (bf16[32,7168]{1,0:T(8,128)(2,1)}, bf16[32,7168]{1,0:T(8,128)(2,1)S(1)}, u32[]{:S(2)}, u32[]{:S(2)}) collective-permute-start(bf16[32,7168]{1,0:T(8,128)(2,1)} %get-tuple-element.37), channel_id=1, source_target_pairs={{0,16},{16,0},{32,48},{48,32},{64,80},{80,64},{96,112},{112,96},{1... | collective-permute-start | bytes 1376264 | tf_op jit(solution)/shard_map/out_sum/ppermute | solution.py:55
  200.1 0.8 copy-start.14
  200.1 0.9 copy-start.15
  201.0 12.8 %copy-start.5 = (f32[32,7168]{1,0:T(8,128)S(1)}, f32[32,7168]{1,0:T(8,128)}, u32[]{:S(2)}) copy-start(f32[32,7168]{1,0:T(8,128)} %get-tuple-element.36) | copy-start | bytes 2752516
  208.2 28.4 %copy-start.6 = (bf16[32,14336]{1,0:T(8,128)(2,1)S(1)}, bf16[32,14336]{1,0:T(8,128)(2,1)}, u32[]{:S(2)}) copy-start(bf16[32,14336]{1,0:T(8,128)(2,1)} %get-tuple-element.46) | copy-start | bytes 2752516
  208.2 24.5 %collective-permute-start.28 = (bf16[32,14336]{1,0:T(8,128)(2,1)}, bf16[32,14336]{1,0:T(8,128)(2,1)S(1)}, u32[]{:S(2)}, u32[]{:S(2)}) collective-permute-start(bf16[32,14336]{1,0:T(8,128)(2,1)} %get-tuple-element.47), channel_id=1, source_target_pairs={{0,3},{1,0},{2,1},{3,2},{4,7},{5,4},{6,5},{7,6},{8,11},{9,8},{10,9... | collective-permute-start | bytes 2752520 | tf_op jit(solution)/shard_map/back_route/ppermute | solution.py:66
  211.7 21.1 %collective-permute-start.29 = (bf16[32,14336]{1,0:T(8,128)(2,1)}, bf16[32,14336]{1,0:T(8,128)(2,1)S(1)}, u32[]{:S(2)}, u32[]{:S(2)}) collective-permute-start(bf16[32,14336]{1,0:T(8,128)(2,1)} %get-tuple-element.48), channel_id=1, source_target_pairs={{0,2},{1,3},{2,0},{3,1},{4,6},{5,7},{6,4},{7,5},{8,10},{9,11},{10,... | collective-permute-start | bytes 2752520 | tf_op jit(solution)/shard_map/back_route/ppermute | solution.py:66
  212.5 24.0 %collective-permute-start.30 = (bf16[32,14336]{1,0:T(8,128)(2,1)}, bf16[32,14336]{1,0:T(8,128)(2,1)S(1)}, u32[]{:S(2)}, u32[]{:S(2)}) collective-permute-start(bf16[32,14336]{1,0:T(8,128)(2,1)} %get-tuple-element.49), channel_id=1, source_target_pairs={{0,1},{1,2},{2,3},{3,0},{4,5},{5,6},{6,7},{7,4},{8,9},{9,10},{10,1... | collective-permute-start | bytes 2752520 | tf_op jit(solution)/shard_map/back_route/ppermute | solution.py:66
  237.1 10.7 %collective-permute-start.31 = (bf16[8,14336]{1,0:T(8,128)(2,1)S(1)}, bf16[8,14336]{1,0:T(8,128)(2,1)S(1)}, u32[]{:S(2)}, u32[]{:S(2)}) collective-permute-start(bf16[8,14336]{1,0:T(8,128)(2,1)S(1)} %get-tuple-element.60), channel_id=1, source_target_pairs={{0,12},{1,13},{2,14},{3,15},{4,0},{5,1},{6,2},{7,3},{8,4},{9,5},{1... | collective-permute-start | bytes 688136 | tf_op jit(solution)/shard_map/back_route/ppermute | solution.py:66
  240.1 8.5 %collective-permute-start.33 = (bf16[8,14336]{1,0:T(8,128)(2,1)S(1)}, bf16[8,14336]{1,0:T(8,128)(2,1)S(1)}, u32[]{:S(2)}, u32[]{:S(2)}) collective-permute-start(bf16[8,14336]{1,0:T(8,128)(2,1)S(1)} %get-tuple-element.61), channel_id=1, source_target_pairs={{0,4},{1,5},{2,6},{3,7},{4,8},{5,9},{6,10},{7,11},{8,12},{9,13},{1... | collective-permute-start | bytes 688136 | tf_op jit(solution)/shard_map/back_route/ppermute | solution.py:66
  240.1 12.1 %collective-permute-start.32 = (bf16[8,14336]{1,0:T(8,128)(2,1)S(1)}, bf16[8,14336]{1,0:T(8,128)(2,1)S(1)}, u32[]{:S(2)}, u32[]{:S(2)}) collective-permute-start(bf16[8,14336]{1,0:T(8,128)(2,1)S(1)} %get-tuple-element.62), channel_id=1, source_target_pairs={{0,8},{1,9},{2,10},{3,11},{4,12},{5,13},{6,14},{7,15},{8,0},{9,1},... | collective-permute-start | bytes 688136 | tf_op jit(solution)/shard_map/back_route/ppermute | solution.py:66
  245.7 7.2 %collective-permute-start.18 = (bf16[8,7168]{1,0:T(8,128)(2,1)S(1)}, bf16[8,7168]{1,0:T(8,128)(2,1)S(1)}, u32[]{:S(2)}, u32[]{:S(2)}) collective-permute-start(bf16[8,7168]{1,0:T(8,128)(2,1)S(1)} %get-tuple-element.63), channel_id=1, source_target_pairs={{0,96},{16,112},{32,0},{48,16},{64,32},{80,48},{96,64},{112,80},{1... | collective-permute-start | bytes 344072 | tf_op jit(solution)/shard_map/out_sum/ppermute | solution.py:47
  246.9 6.1 %collective-permute-start.20 = (bf16[8,7168]{1,0:T(8,128)(2,1)S(1)}, bf16[8,7168]{1,0:T(8,128)(2,1)S(1)}, u32[]{:S(2)}, u32[]{:S(2)}) collective-permute-start(bf16[8,7168]{1,0:T(8,128)(2,1)S(1)} %get-tuple-element.64), channel_id=1, source_target_pairs={{0,32},{16,48},{32,64},{48,80},{64,96},{80,112},{96,0},{112,16},{1... | collective-permute-start | bytes 344072 | tf_op jit(solution)/shard_map/out_sum/ppermute | solution.py:47
  247.8 6.3 %collective-permute-start.19 = (bf16[8,7168]{1,0:T(8,128)(2,1)S(1)}, bf16[8,7168]{1,0:T(8,128)(2,1)S(1)}, u32[]{:S(2)}, u32[]{:S(2)}) collective-permute-start(bf16[8,7168]{1,0:T(8,128)(2,1)S(1)} %get-tuple-element.65), channel_id=1, source_target_pairs={{0,64},{16,80},{32,96},{48,112},{64,0},{80,16},{96,32},{112,48},{1... | collective-permute-start | bytes 344072 | tf_op jit(solution)/shard_map/out_sum/ppermute | solution.py:47

commit v3 on v2

--- a/solution.py
+++ b/solution.py
@@ -184,7 +184,7 @@
     return jnp.where(to == ((x * 4 + z) * 8 + (i >> 5)) * 2 + (i & 1), 1.0, 0.0)
 
 
-def expert_kernel(at, *refs):
+def expert_kernel(at, _, *refs):
     xs, (g_hbm, gw, uw, dw), dxs, (y_hbm,), (x, g, wg, wu, wd, y, dx, sem, sem_w, sem_o) = (
         refs[:8],
         refs[8:12],
@@ -252,22 +252,29 @@
 
 
 def back_sum_kernel(*refs):
-    blocks, (mix, hid, grads, sg, su, sd), outs = refs[:8], refs[8:14], refs[14:]
-    step = pl.program_id(0)
-    half = pl.num_programs(0) // 2
-
-    def put(total):
-        for n in range(4):
-            outs[n][...] = total[n * 32 : n * 32 + 32].astype(BF16)
-
-    @pl.when(step < half)
-    def _():
-        put(dot(hid[...], sd[...]))
-
-    @pl.when(step >= half)
-    def _():
-        rows = jnp.concatenate([v[...] for v in blocks], axis=0)
-        put(dot_a(mix[...], rows) + dot(grads[...], jnp.concatenate([sg[...], su[...]], axis=0)))
+    blocks, (mix, grads, sg, su), outs = refs[:8], refs[8:12], refs[12:]
+    rows = jnp.concatenate([v[...] for v in blocks], axis=0)
+    total = dot_a(mix[...], rows) + dot(grads[...], jnp.concatenate([sg[...], su[...]], axis=0))
+    for n in range(4):
+        outs[n][...] = total[n * 32 : n * 32 + 32].astype(BF16)
+
+
+def shared_out_kernel(hid, sd, *outs):
+    total = dot(hid[...], sd[...]).astype(BF16)
+    for n in range(4):
+        outs[n][...] = total[n * 32 : n * 32 + 32]
+
+
+def pass_on(v, after):
+    here = pl.BlockSpec(memory_space=pl.ANY)
+    return pl.pallas_call(
+        lambda *refs: None,
+        in_specs=[here] * (1 + len(after)),
+        out_specs=here,
+        out_shape=jax.ShapeDtypeStruct(v.shape, v.dtype),
+        input_output_aliases={0: 0},
+        compiler_params=pltpu.CompilerParams(vmem_limit_bytes=60 * 1024 * 1024),
+    )(v, *after)
 
 
 def out_sum_kernel(rows, mix, mine, other):
@@ -395,12 +402,25 @@
             after=[x_mix],
         )
 
+    with jax.named_scope("shared_out"):
+        s_parts = call(
+            shared_out_kernel,
+            steps,
+            [(s_hid, (128, part), FIX), (shared_down, (part, BLK), COL)],
+            [((32, width), BF16, (32, BLK), COL)] * 4,
+            [],
+            2 * 128 * part * width,
+            2 * 192 * width,
+            after=x_rows[1:4] + x_rows[5:],
+        )
+        s_line = ring_sum(move_b, s_parts)
+
     with jax.named_scope("expert"):
         chunks = width // CHUNK
         here = pl.BlockSpec(memory_space=pl.ANY)
         *dx_rows, dx_over, y_rows = pl.pallas_call(
             expert_kernel,
-            in_specs=[pl.BlockSpec(memory_space=pltpu.SMEM)] + [here] * 12,
+            in_specs=[pl.BlockSpec(memory_space=pltpu.SMEM)] + [here] * 13,
             out_specs=[here] * 6,
             out_shape=[jax.ShapeDtypeStruct((32, width), BF16)] * 4
             + [jax.ShapeDtypeStruct((128, width), BF16), jax.ShapeDtypeStruct((256, width), BF16)],
@@ -417,8 +437,9 @@
                 pltpu.SemaphoreType.DMA((1, chunks)),
             ],
             compiler_params=pltpu.CompilerParams(vmem_limit_bytes=60 * 1024 * 1024),
-        )(at, *x_rows, g_rows, expert_gate, expert_up, expert_down)
+        )(at, s_parts[0], *x_rows, g_rows, expert_gate, expert_up, expert_down)
     with jax.named_scope("out_route"):
+        y_rows = pass_on(y_rows, [s_line])
         y_home = lax.all_to_all(y_rows.reshape(16, 16, width), "exp", split_axis=0, concat_axis=0, tiled=True)
         y_home = y_home.reshape(256, width)
 
@@ -429,25 +450,23 @@
         dx_home += [dx_over[0]] + [move_y(dx_over[k], -k) for k in (1, 2, 3)]
         parts = call(
             back_sum_kernel,
-            2 * steps,
-            [(v, (32, BLK), later) for v in dx_home]
+            steps,
+            [(v, (32, BLK), COL) for v in dx_home]
             + [
                 (x_mix, (256, 128), FIX),
-                (s_hid, (128, part), FIX),
                 (s_grads, (128, 2 * part), FIX),
-                (shared_gate.T, (part, BLK), later),
-                (shared_up.T, (part, BLK), later),
-                (shared_down, (part, BLK), first),
+                (shared_gate.T, (part, BLK), COL),
+                (shared_up.T, (part, BLK), COL),
             ],
-            [((32, 2 * width), BF16, (32, BLK), COL)] * 4,
+            [((32, width), BF16, (32, BLK), COL)] * 4,
             [],
             2 * 256 * 128 * width,
             2 * 400 * width,
             after=[y_home],
         )
-        line = ring_sum(move_b, parts).astype(BF16).reshape(4, 8, 2 * width)
+        line = jnp.concatenate([ring_sum(move_b, parts), s_line], axis=1).astype(BF16).reshape(4, 8, 2 * width)
         both = ring_sum(move_a, [line[k] for k in range(4)])
-        s_out, token_grad = both[:, :width], both[:, width:].astype(BF16)
+        token_grad, s_out = both[:, :width].astype(BF16), both[:, width:]
     with jax.named_scope("out_sum"):
         mine, other = call(
             out_sum_kernel,
@@ -457,6 +476,7 @@
             [],
             2 * 256 * 64 * width,
             2 * 352 * width,
+            after=[parts[0]],
         )
         line = (mine + swap_core(other).astype(F32)).reshape(4, 8, width)
         line = [line[0]] + [line[k].astype(BF16) for k in (1, 2, 3)]

time: 255 us -> 237 us (0.929)
  waiting for transfers between devices: 133 us -> 113 us
    all_to_all x1, waiting for transfers between devices: 33.4 us -> 5.12 us  [local(): lax.all_to_all(y_rows.reshape(16, 16, width), 'exp', split_axis=0, concat...]
    ppermute x16, waiting for transfers between devices: 46.1 us -> 71 us  [move_y(): lax.ppermute(v, 'grp', [(y * 2 + c, (y + k) % N_Y * 2 + c) for y in range...]
    ppermute x12 -> x15, waiting for transfers between devices: 49.3 us -> 36.2 us  [move_plane(): return lax.ppermute(v, ('grp', 'exp'), pairs)]
    all_to_all x1, waiting for transfers between devices: 2.73 us -> 0.01 us  [local(): lax.all_to_all(g_sent.reshape(16, 16, width), 'exp', split_axis=0, concat...]
    ppermute x12 -> x15, starting transfers between devices: 24.1 us -> 26.1 us  [move_plane(): return lax.ppermute(v, ('grp', 'exp'), pairs)]
    pallas_call x6 -> x7, Pallas kernels: 25.3 us -> 25.4 us  [call(): pl.pallas_call(lambda *refs: kernel(*refs[skip:]), grid=(grid,), in_specs...]
  transfers between devices with their start and end apart: 36 -> 39, of which waited for: 14 -> 16; matrix products, arithmetic and copies ran while one was open for 2% -> 3% of each run, Pallas kernels for 8% -> 17%
where the time goes in v3:
time: 237 us
  waiting for transfers between devices  113 us (48%)
  starting transfers between devices  61.4 us (26%)
  Pallas kernels  51 us (22%)
  local copies, waits for them, and re-layouts  5.6 us (2%)
  other arithmetic  4.07 us (2%)
    ppermute x16, waiting for transfers between devices, move_y(): lax.ppermute(v, 'grp', [(y * 2 + c, (y + k) % N_Y * 2 + c) for y in range...  71 us
    ppermute x15, waiting for transfers between devices, move_plane(): return lax.ppermute(v, ('grp', 'exp'), pairs)  36.2 us
    ppermute x15, starting transfers between devices, move_plane(): return lax.ppermute(v, ('grp', 'exp'), pairs)  26.1 us
    pallas_call x1, Pallas kernels, local(): pl.pallas_call(expert_kernel, in_specs=[pl.BlockSpec(memory_space=pltpu.S...  25.6 us
    pallas_call x7, Pallas kernels, call(): pl.pallas_call(lambda *refs: kernel(*refs[skip:]), grid=(grid,), in_specs...  25.4 us
    ppermute x16, starting transfers between devices, move_y(): lax.ppermute(v, 'grp', [(y * 2 + c, (y + k) % N_Y * 2 + c) for y in range...  21.5 us
    all_to_all x1, starting transfers between devices, local(): lax.all_to_all(y_rows.reshape(16, 16, width), 'exp', split_axis=0, concat...  8.27 us
    all_to_all x1, waiting for transfers between devices, local(): lax.all_to_all(y_rows.reshape(16, 16, width), 'exp', split_axis=0, concat...  5.12 us
  transfers between devices with their start and end apart: 39, of which 16 were waited for; matrix products, arithmetic and copies ran while one was open for 3% of the time, Pallas kernels for 17%

profile of v3, /device:TPU:0, one launch (start us, length us, event | category | flops | bytes accessed | tf_op | source)
XLA Modules:
  0.0 236.5 jit_solution(15474749809136958395)
XLA Ops:
  0.6 1.9 widen.1
  2.5 3.3 %collective-permute-start.2 = (bf16[8,7296]{1,0:T(8,128)(2,1)}, bf16[8,7296]{1,0:T(8,128)(2,1)S(1)}, u32[]{:S(2)}, u32[]{:S(2)}) collective-permute-start(bf16[8,7296]{1,0:T(8,128)(2,1)} %get-tuple-element.30), channel_id=1, source_target_pairs={{0,64},{16,80},{32,96},{48,112},{64,0},{80,16},{96,32},{112,48},{1... | collective-permute-start | bytes 350216 | tf_op jit(solution)/shard_map/cot_gather/ppermute | solution.py:47
  5.8 2.8 %collective-permute-start.6 = (bf16[8,14464]{1,0:T(8,128)(2,1)}, bf16[8,14464]{1,0:T(8,128)(2,1)S(1)}, u32[]{:S(2)}, u32[]{:S(2)}) collective-permute-start(bf16[8,14464]{1,0:T(8,128)(2,1)} %get-tuple-element.32), channel_id=1, source_target_pairs={{0,12},{1,13},{2,14},{3,15},{4,0},{5,1},{6,2},{7,3},{8,4},{9,5},{1... | collective-permute-start | bytes 694280 | tf_op jit(solution)/shard_map/gather_line/ppermute | solution.py:66
  8.5 0.8 collective-permute-start.5
  9.3 0.9 collective-permute-start.4
  10.2 1.0 constant_dynamic-update-slice_fusion.7
  11.2 0.9 constant_dynamic-update-slice_fusion.1
  12.2 0.7 collective-permute-start.1
  12.9 5.9 %collective-permute-done.4 = bf16[8,14464]{1,0:T(8,128)(2,1)S(1)} collective-permute-done((bf16[8,14464]{1,0:T(8,128)(2,1)}, bf16[8,14464]{1,0:T(8,128)(2,1)S(1)}, u32[]{:S(2)}, u32[]{:S(2)}) %collective-permute-start.4) | collective-permute-done | bytes 231456 | tf_op jit(solution)/shard_map/gather_line/ppermute | solution.py:66
  18.9 4.1 %collective-permute-start.9 = (bf16[32,14464]{1,0:T(8,128)(2,1)S(1)}, bf16[32,14464]{1,0:T(8,128)(2,1)S(1)}, u32[]{:S(2)}, u32[]{:S(2)}) collective-permute-start(bf16[32,14464]{1,0:T(8,128)(2,1)S(1)} %constant_dynamic-update-slice_fusion.4.refs_2_.refs_6_.refs_1_.refs_5_), channel_id=1, source_target_pairs={{0,3},{1,0},{2,1},{3,2},{4,7},{5,4},{6,5},{7,6},{8,11},{9,8},{10,9... | collective-permute-start | bytes 2777096 | tf_op jit(solution)/shard_map/gather_plane/ppermute | solution.py:66
  23.0 1.3 collective-permute-start.7
  24.4 0.7 pad_add_fusion.refs_0_.refs_1_.at
  25.1 1.1 collective-permute-done.3.refs_3_.refs_6_
  26.2 4.3 %cot_pick.1 = (bf16[256,7168]{1,0:T(8,128)(2,1)}, bf16[256,64]{1,0:T(8,128)(2,1)}) custom-call(s32[2]{0:T(128)} %pad_add_fusion.refs_0_.refs_1_.at, bf16[16,7296]{1,0:T(8,128)(2,1)} %copy-done.12, bf16[24,7296]{1,0:T(8,128)(2,1)} %copy-done.3, bf16[24,7296]{1,0:T(8,128)(2,1)} %collective-permute-done.3.refs_3_.refs_6_, bf16[16,7296]{1,0:T(8,128)(2,1)} %copy-done.12, ...), custom_call_target="tpu_custom_call" | custom-call | flops 234881024 | bytes 4587520 | tf_op jit(solution)/shard_map/cot_pick/pallas_call | solution.py:93
  30.5 13.4 %collective-permute-done.9.refs_5_.refs_9_.refs_4_.refs_8_ = bf16[32,14464]{1,0:T(8,128)(2,1)S(1)} collective-permute-done((bf16[32,14464]{1,0:T(8,128)(2,1)S(1)}, bf16[32,14464]{1,0:T(8,128)(2,1)S(1)}, u32[]{:S(2)}, u32[]{:S(2)}) %collective-permute-start.9) | collective-permute-done | bytes 925728 | tf_op jit(solution)/shard_map/gather_plane/ppermute | solution.py:66
  43.9 3.8 %collective-permute-done.7.refs_3_.refs_7_.refs_2_.refs_6_ = bf16[32,14464]{1,0:T(8,128)(2,1)} collective-permute-done((bf16[32,14464]{1,0:T(8,128)(2,1)S(1)}, bf16[32,14464]{1,0:T(8,128)(2,1)}, u32[]{:S(2)}, u32[]{:S(2)}) %collective-permute-start.7) | collective-permute-done | bytes 925728 | tf_op jit(solution)/shard_map/gather_plane/ppermute | solution.py:66
  47.7 4.3 %tok_pick.1 = (bf16[32,7168]{1,0:T(8,128)(2,1)}, bf16[32,7168]{1,0:T(8,128)(2,1)}, bf16[32,7168]{1,0:T(8,128)(2,1)}, bf16[32,7168]{1,0:T(8,128)(2,1)}, bf16[128,...) custom-call(bf16[256,64]{1,0:T(8,128)(2,1)} %get-tuple-element.31.refs_0_.refs_2_, s32[2]{0:T(128)} %pad_add_fusion.refs_0_.refs_1_.at, ...), custom_call_target="tpu_custom_call" | custom-call | flops 469762048 | bytes 5734400 | tf_op jit(solution)/shard_map/tok_pick/pallas_call | solution.py:93
  52.1 4.5 %all-to-all-start = ((bf16[16,16,7168]{2,1,0:T(8,128)(2,1)}), bf16[16,16,7168]{2,1,0:T(8,128)(2,1)}, u32[]{:S(2)}, u32[]{:S(2)}) async-start(bf16[16,16,7168]{2,1,0:T(8,128)(2,1)} %bitcast.13), calls=%async_computation | async-start | bytes 7340032 | tf_op jit(solution)/shard_map/cot_route/all_to_all | solution.py:368
  56.6 0.7 collective-permute-start.10
  57.4 1.8 collective-permute-start.11
  59.2 0.9 collective-permute-start.12
  60.2 1.1 fusion.9
  61.3 1.3 collective-permute-start.16
  62.6 1.8 collective-permute-start.15
  64.5 26.3 %collective-permute-done.10.refs_0_.refs_1_ = bf16[32,7168]{1,0:T(8,128)(2,1)S(1)} collective-permute-done((bf16[32,7168]{1,0:T(8,128)(2,1)}, bf16[32,7168]{1,0:T(8,128)(2,1)S(1)}, u32[]{:S(2)}, u32[]{:S(2)}) %collective-permute-start.10) | collective-permute-done | bytes 458784 | tf_op jit(solution)/shard_map/tok_route/ppermute | solution.py:47
  90.7 4.5 %shared.1 = (bf16[128,64]{1,0:T(8,128)(2,1)}, bf16[128,128]{1,0:T(8,128)(2,1)}) custom-call(bf16[256,128]{1,0:T(8,128)(2,1)} %get-tuple-element.37.refs_0_.refs_9_, bf16[32,14464]{1,0:T(8,128)(2,1)} %copy-done, bf16[32,14464]{1,0:T(8,128)(2,1)} %collective-permute-done.7.refs_3_.refs_7_.refs_2_.refs_6_, bf16[32,14464]{1,0:T(8,128)(2,1)} %copy-done.2, ...), custom_call_target="tpu_custom_call" | custom-call | flops 352321536 | bytes 6451200 | tf_op jit(solution)/shard_map/shared/pallas_call | solution.py:93
  95.3 8.7 %collective-permute-done.14.refs_3_.refs_5_ = bf16[32,7168]{1,0:T(8,128)(2,1)S(1)} collective-permute-done((bf16[32,7168]{1,0:T(8,128)(2,1)S(1)}, bf16[32,7168]{1,0:T(8,128)(2,1)S(1)}, u32[]{:S(2)}, u32[]{:S(2)}) %collective-permute-start.14) | collective-permute-done | bytes 458784 | tf_op jit(solution)/shard_map/tok_route/ppermute | solution.py:47
  104.0 0.8 copy-done.9
  104.8 2.7 %shared_out.1 = (bf16[32,7168]{1,0:T(8,128)(2,1)}, bf16[32,7168]{1,0:T(8,128)(2,1)}, bf16[32,7168]{1,0:T(8,128)(2,1)}, bf16[32,7168]{1,0:T(8,128)(2,1)}) custom-call(bf16[32,7168]{1,0:T(8,128)(2,1)} %copy-done.4, bf16[32,7168]{1,0:T(8,128)(2,1)} %copy-done.5, bf16[32,7168]{1,0:T(8,128)(2,1)} %copy-done.6, bf16[32,7168]{1,0:T(8,128)(2,1)} %copy-done.9, ...), custom_call_target="tpu_custom_call" | custom-call | flops 117440512 | bytes 2752512 | tf_op jit(solution)/shard_map/shared_out/pallas_call | solution.py:93
  107.5 0.4 collective-permute-start.18
  107.9 1.6 collective-permute-start.19
  109.5 25.6 %expert.1 = (bf16[32,7168]{1,0:T(8,128)(2,1)}, bf16[32,7168]{1,0:T(8,128)(2,1)}, bf16[32,7168]{1,0:T(8,128)(2,1)}, bf16[32,7168]{1,0:T(8,128)(2,1)}, bf16[128,71...) custom-call(s32[2]{0:T(128)} %pad_add_fusion.refs_0_.refs_1_.at, bf16[32,7168]{1,0:T(8,128)(2,1)} %get-tuple-element.39._, ...), custom_call_target="tpu_custom_call" | custom-call | tf_op jit(solution)/shard_map/expert/pallas_call | solution.py:421
  135.3 2.2 fusion.7
  137.5 8.3 %all-to-all-start.1 = ((bf16[16,16,7168]{2,1,0:T(8,128)(2,1)}), bf16[16,16,7168]{2,1,0:T(8,128)(2,1)}, u32[]{:S(2)}, u32[]{:S(2)}) async-start(bf16[16,16,7168]{2,1,0:T(8,128)(2,1)} %bitcast.8), calls=%async_computation.1 | async-start | bytes 7340032 | tf_op jit(solution)/shard_map/out_route/all_to_all | solution.py:443
  145.8 0.9 collective-permute-start.20
  146.7 1.8 collective-permute-start.21
  148.5 0.9 fusion.8
  149.5 1.7 collective-permute-start.26
  151.1 3.0 %collective-permute-start.25 = (bf16[32,7168]{1,0:T(8,128)(2,1)S(1)}, bf16[32,7168]{1,0:T(8,128)(2,1)S(1)}, u32[]{:S(2)}, u32[]{:S(2)}) collective-permute-start(bf16[32,7168]{1,0:T(8,128)(2,1)S(1)} %get-tuple-element.63), channel_id=1, source_target_pairs={{0,64},{16,80},{32,96},{48,112},{64,0},{80,16},{96,32},{112,48},{1... | collective-permute-start | bytes 1376264 | tf_op jit(solution)/shard_map/back_route/ppermute | solution.py:47
  154.2 5.3 %collective-permute-done.20.refs_2_ = bf16[32,7168]{1,0:T(8,128)(2,1)S(1)} collective-permute-done((bf16[32,7168]{1,0:T(8,128)(2,1)}, bf16[32,7168]{1,0:T(8,128)(2,1)S(1)}, u32[]{:S(2)}, u32[]{:S(2)}) %collective-permute-start.20) | collective-permute-done | bytes 458784 | tf_op jit(solution)/shard_map/back_route/ppermute | solution.py:47
  159.4 1.4 collective-permute-start.24
  160.8 1.0 collective-permute-done.21.refs_3_
  161.8 8.8 %collective-permute-done.22.refs_4_ = bf16[32,7168]{1,0:T(8,128)(2,1)S(1)} collective-permute-done((bf16[32,7168]{1,0:T(8,128)(2,1)}, bf16[32,7168]{1,0:T(8,128)(2,1)S(1)}, u32[]{:S(2)}, u32[]{:S(2)}) %collective-permute-start.22) | collective-permute-done | bytes 458784 | tf_op jit(solution)/shard_map/back_route/ppermute | solution.py:47
  170.7 10.7 %collective-permute-done.26.refs_8_ = bf16[32,7168]{1,0:T(8,128)(2,1)S(1)} collective-permute-done((bf16[32,7168]{1,0:T(8,128)(2,1)S(1)}, bf16[32,7168]{1,0:T(8,128)(2,1)S(1)}, u32[]{:S(2)}, u32[]{:S(2)}) %collective-permute-start.26) | collective-permute-done | bytes 458784 | tf_op jit(solution)/shard_map/back_route/ppermute | solution.py:47
  181.4 8.9 %collective-permute-done.25.refs_7_ = bf16[32,7168]{1,0:T(8,128)(2,1)S(1)} collective-permute-done((bf16[32,7168]{1,0:T(8,128)(2,1)S(1)}, bf16[32,7168]{1,0:T(8,128)(2,1)S(1)}, u32[]{:S(2)}, u32[]{:S(2)}) %collective-permute-start.25) | collective-permute-done | bytes 458784 | tf_op jit(solution)/shard_map/back_route/ppermute | solution.py:47
  190.3 5.1 %all-to-all-done.1 = bf16[16,16,7168]{2,1,0:T(8,128)(2,1)} async-done(((bf16[16,16,7168]{2,1,0:T(8,128)(2,1)}), bf16[16,16,7168]{2,1,0:T(8,128)(2,1)}, u32[]{:S(2)}, u32[]{:S(2)}) %all-to-all-start.1) | async-done | bytes 3670048 | tf_op jit(solution)/shard_map/out_route/all_to_all | solution.py:443
  195.5 4.4 %back_route.1 = (bf16[32,7168]{1,0:T(8,128)(2,1)}, bf16[32,7168]{1,0:T(8,128)(2,1)}, bf16[32,7168]{1,0:T(8,128)(2,1)}, bf16[32,7168]{1,0:T(8,128)(2,1)}) custom-call(bf16[256,7168]{1,0:T(8,128)(2,1)} %bitcast.7.refs_0_.refs_1_, bf16[32,7168]{1,0:T(8,128)(2,1)} %get-tuple-element.46.refs_1_, bf16[32,7168]{1,0:T(8,128)(2,1)} %copy-done.14, ...), custom_call_target="tpu_custom_call" | custom-call | flops 469762048 | bytes 5734400 | tf_op jit(solution)/shard_map/back_route/pallas_call | solution.py:93
  199.8 3.4 %collective-permute-start.31 = (bf16[32,7168]{1,0:T(8,128)(2,1)}, bf16[32,7168]{1,0:T(8,128)(2,1)S(1)}, u32[]{:S(2)}, u32[]{:S(2)}) collective-permute-start(bf16[32,7168]{1,0:T(8,128)(2,1)} %get-tuple-element.55), channel_id=1, source_target_pairs={{0,3},{1,0},{2,1},{3,2},{4,7},{5,4},{6,5},{7,6},{8,11},{9,8},{10,9... | collective-permute-start | bytes 1376264 | tf_op jit(solution)/shard_map/back_route/ppermute | solution.py:66
  203.2 0.9 collective-permute-start.32
  204.1 1.3 collective-permute-start.33
  205.4 3.4 %out_sum.1 = (f32[32,7168]{1,0:T(8,128)}, bf16[32,7168]{1,0:T(8,128)(2,1)}) custom-call(bf16[32,7168]{1,0:T(8,128)(2,1)} %get-tuple-element.52.refs_0_, bf16[256,7168]{1,0:T(8,128)(2,1)} %bitcast.7.refs_0_.refs_1_, bf16[256,64]{1,0:T(8,128)(2,1)} %get-tuple-element.31.refs_0_.refs_2_), custom_call_target="tpu_custom_call" | custom-call | flops 234881024 | bytes 5046272 | tf_op jit(solution)/shard_map/out_sum/pallas_call | solution.py:93
  208.8 5.6 %collective-permute-done.31 = bf16[32,7168]{1,0:T(8,128)(2,1)S(1)} collective-permute-done((bf16[32,7168]{1,0:T(8,128)(2,1)}, bf16[32,7168]{1,0:T(8,128)(2,1)S(1)}, u32[]{:S(2)}, u32[]{:S(2)}) %collective-permute-start.31) | collective-permute-done | bytes 458784 | tf_op jit(solution)/shard_map/back_route/ppermute | solution.py:66
  214.5 3.9 %collective-permute-done.33 = bf16[32,7168]{1,0:T(8,128)(2,1)S(1)} collective-permute-done((bf16[32,7168]{1,0:T(8,128)(2,1)}, bf16[32,7168]{1,0:T(8,128)(2,1)S(1)}, u32[]{:S(2)}, u32[]{:S(2)}) %collective-permute-start.33) | collective-permute-done | bytes 458784 | tf_op jit(solution)/shard_map/back_route/ppermute | solution.py:66
  218.3 0.2 add_convert_fusion
  218.6 3.0 %collective-permute-start.34 = (bf16[8,14336]{1,0:T(8,128)(2,1)S(1)}, bf16[8,14336]{1,0:T(8,128)(2,1)S(1)}, u32[]{:S(2)}, u32[]{:S(2)}) collective-permute-start(bf16[8,14336]{1,0:T(8,128)(2,1)S(1)} %get-tuple-element.70), channel_id=1, source_target_pairs={{0,12},{1,13},{2,14},{3,15},{4,0},{5,1},{6,2},{7,3},{8,4},{9,5},{1... | collective-permute-start | bytes 688136 | tf_op jit(solution)/shard_map/back_route/ppermute | solution.py:66
  221.6 5.6 %collective-permute-start.35 = (bf16[8,14336]{1,0:T(8,128)(2,1)S(1)}, bf16[8,14336]{1,0:T(8,128)(2,1)S(1)}, u32[]{:S(2)}, u32[]{:S(2)}) collective-permute-start(bf16[8,14336]{1,0:T(8,128)(2,1)S(1)} %get-tuple-element.72), channel_id=1, source_target_pairs={{0,8},{1,9},{2,10},{3,11},{4,12},{5,13},{6,14},{7,15},{8,0},{9,1},... | collective-permute-start | bytes 688136 | tf_op jit(solution)/shard_map/back_route/ppermute | solution.py:66
  227.4 0.9 collective-permute-start.28
  228.3 1.2 collective-permute-start.30
  229.5 0.6 collective-permute-start.29
  230.1 3.6 %collective-permute-done.35 = bf16[8,14336]{1,0:T(8,128)(2,1)S(1)} collective-permute-done((bf16[8,14336]{1,0:T(8,128)(2,1)S(1)}, bf16[8,14336]{1,0:T(8,128)(2,1)S(1)}, u32[]{:S(2)}, u32[]{:S(2)}) %collective-permute-start.35) | collective-permute-done | bytes 229408 | tf_op jit(solution)/shard_map/back_route/ppermute | solution.py:66
  233.7 0.1 convert_add_fusion.2
  233.8 0.7 slice.135
  234.5 1.3 collective-permute-done.29
  235.8 0.7 fusion.3
  (82 shorter events, 0.7 us)
Async XLA Ops:
  2.5 21.8 %collective-permute-start.2 = (bf16[8,7296]{1,0:T(8,128)(2,1)}, bf16[8,7296]{1,0:T(8,128)(2,1)S(1)}, u32[]{:S(2)}, u32[]{:S(2)}) collective-permute-start(bf16[8,7296]{1,0:T(8,128)(2,1)} %get-tuple-element.30), channel_id=1, source_target_pairs={{0,64},{16,80},{32,96},{48,112},{64,0},{80,16},{96,32},{112,48},{1... | collective-permute-start | bytes 350216 | tf_op jit(solution)/shard_map/cot_gather/ppermute | solution.py:47
  5.8 6.4 %collective-permute-start = (bf16[8,7296]{1,0:T(8,128)(2,1)}, bf16[8,7296]{1,0:T(8,128)(2,1)S(1)}, u32[]{:S(2)}, u32[]{:S(2)}) collective-permute-start(bf16[8,7296]{1,0:T(8,128)(2,1)} %get-tuple-element.30), channel_id=1, source_target_pairs={{0,16},{16,0},{32,48},{48,32},{64,80},{80,64},{96,112},{112,96},{1... | collective-permute-start | bytes 350216 | tf_op jit(solution)/shard_map/cot_gather/ppermute | solution.py:55
  5.8 13.1 %collective-permute-start.6 = (bf16[8,14464]{1,0:T(8,128)(2,1)}, bf16[8,14464]{1,0:T(8,128)(2,1)S(1)}, u32[]{:S(2)}, u32[]{:S(2)}) collective-permute-start(bf16[8,14464]{1,0:T(8,128)(2,1)} %get-tuple-element.32), channel_id=1, source_target_pairs={{0,12},{1,13},{2,14},{3,15},{4,0},{5,1},{6,2},{7,3},{8,4},{9,5},{1... | collective-permute-start | bytes 694280 | tf_op jit(solution)/shard_map/gather_line/ppermute | solution.py:66
  8.5 10.3 %collective-permute-start.5 = (bf16[8,14464]{1,0:T(8,128)(2,1)}, bf16[8,14464]{1,0:T(8,128)(2,1)S(1)}, u32[]{:S(2)}, u32[]{:S(2)}) collective-permute-start(bf16[8,14464]{1,0:T(8,128)(2,1)} %get-tuple-element.32), channel_id=1, source_target_pairs={{0,8},{1,9},{2,10},{3,11},{4,12},{5,13},{6,14},{7,15},{8,0},{9,1},... | collective-permute-start | bytes 694280 | tf_op jit(solution)/shard_map/gather_line/ppermute | solution.py:66
  9.3 9.4 %collective-permute-start.4 = (bf16[8,14464]{1,0:T(8,128)(2,1)}, bf16[8,14464]{1,0:T(8,128)(2,1)S(1)}, u32[]{:S(2)}, u32[]{:S(2)}) collective-permute-start(bf16[8,14464]{1,0:T(8,128)(2,1)} %get-tuple-element.32), channel_id=1, source_target_pairs={{0,4},{1,5},{2,6},{3,7},{4,8},{5,9},{6,10},{7,11},{8,12},{9,13},{1... | collective-permute-start | bytes 694280 | tf_op jit(solution)/shard_map/gather_line/ppermute | solution.py:66
  12.1 14.0 %copy-start.12 = (bf16[16,7296]{1,0:T(8,128)(2,1)}, bf16[16,7296]{1,0:T(8,128)(2,1)S(1)}, u32[]{:S(2)}) copy-start(bf16[16,7296]{1,0:T(8,128)(2,1)S(1)} %constant_dynamic-update-slice_fusion.refs_1_.refs_4_) | copy-start | bytes 700420
  12.2 12.1 %collective-permute-start.1 = (bf16[16,7296]{1,0:T(8,128)(2,1)S(1)}, bf16[16,7296]{1,0:T(8,128)(2,1)S(1)}, u32[]{:S(2)}, u32[]{:S(2)}) collective-permute-start(bf16[16,7296]{1,0:T(8,128)(2,1)S(1)} %constant_dynamic-update-slice_fusion.refs_1_.refs_4_), channel_id=1, source_target_pairs={{0,32},{16,112},{32,64},{48,16},{64,96},{80,48},{96,0},{112,80},{1... | collective-permute-start | bytes 700424 | tf_op jit(solution)/shard_map/cot_gather/ppermute | solution.py:51
  18.9 28.8 %copy-start = (bf16[32,14464]{1,0:T(8,128)(2,1)}, bf16[32,14464]{1,0:T(8,128)(2,1)S(1)}, u32[]{:S(2)}) copy-start(bf16[32,14464]{1,0:T(8,128)(2,1)S(1)} %constant_dynamic-update-slice_fusion.4.refs_2_.refs_6_.refs_1_.refs_5_) | copy-start | bytes 2777092
  18.9 25.0 %collective-permute-start.9 = (bf16[32,14464]{1,0:T(8,128)(2,1)S(1)}, bf16[32,14464]{1,0:T(8,128)(2,1)S(1)}, u32[]{:S(2)}, u32[]{:S(2)}) collective-permute-start(bf16[32,14464]{1,0:T(8,128)(2,1)S(1)} %constant_dynamic-update-slice_fusion.4.refs_2_.refs_6_.refs_1_.refs_5_), channel_id=1, source_target_pairs={{0,3},{1,0},{2,1},{3,2},{4,7},{5,4},{6,5},{7,6},{8,11},{9,8},{10,9... | collective-permute-start | bytes 2777096 | tf_op jit(solution)/shard_map/gather_plane/ppermute | solution.py:66
  23.0 20.9 %collective-permute-start.8 = (bf16[32,14464]{1,0:T(8,128)(2,1)S(1)}, bf16[32,14464]{1,0:T(8,128)(2,1)S(1)}, u32[]{:S(2)}, u32[]{:S(2)}) collective-permute-start(bf16[32,14464]{1,0:T(8,128)(2,1)S(1)} %constant_dynamic-update-slice_fusion.4.refs_2_.refs_6_.refs_1_.refs_5_), channel_id=1, source_target_pairs={{0,2},{1,3},{2,0},{3,1},{4,6},{5,7},{6,4},{7,5},{8,10},{9,11},{10,... | collective-permute-start | bytes 2777096 | tf_op jit(solution)/shard_map/gather_plane/ppermute | solution.py:66
  23.0 24.7 %collective-permute-start.7 = (bf16[32,14464]{1,0:T(8,128)(2,1)S(1)}, bf16[32,14464]{1,0:T(8,128)(2,1)}, u32[]{:S(2)}, u32[]{:S(2)}) collective-permute-start(bf16[32,14464]{1,0:T(8,128)(2,1)S(1)} %constant_dynamic-update-slice_fusion.4.refs_2_.refs_6_.refs_1_.refs_5_), channel_id=1, source_target_pairs={{0,1},{1,2},{2,3},{3,0},{4,5},{5,6},{6,7},{7,4},{8,9},{9,10},{10,1... | collective-permute-start | bytes 2777096 | tf_op jit(solution)/shard_map/gather_plane/ppermute | solution.py:66
  24.3 1.9 copy-start.3
  24.3 1.9 collective-permute-start.3
  43.9 3.8 %copy-start.1 = (bf16[32,14464]{1,0:T(8,128)(2,1)}, bf16[32,14464]{1,0:T(8,128)(2,1)S(1)}, u32[]{:S(2)}) copy-start(bf16[32,14464]{1,0:T(8,128)(2,1)S(1)} %collective-permute-done.9.refs_5_.refs_9_.refs_4_.refs_8_) | copy-start | bytes 2777092
  43.9 3.8 %copy-start.2 = (bf16[32,14464]{1,0:T(8,128)(2,1)}, bf16[32,14464]{1,0:T(8,128)(2,1)S(1)}, u32[]{:S(2)}) copy-start(bf16[32,14464]{1,0:T(8,128)(2,1)S(1)} %collective-permute-done.8.refs_4_.refs_8_.refs_3_.refs_7_) | copy-start | bytes 2777092
  52.0 8.1 %collective-permute-start.13 = (bf16[128,7168]{1,0:T(8,128)(2,1)}, bf16[128,7168]{1,0:T(8,128)(2,1)S(1)}, u32[]{:S(2)}, u32[]{:S(2)}) collective-permute-start(bf16[128,7168]{1,0:T(8,128)(2,1)} %get-tuple-element.36), channel_id=1, source_target_pairs={{0,16},{16,0},{32,48},{48,32},{64,80},{80,64},{96,112},{112,96},{1... | collective-permute-start | bytes 5505032 | tf_op jit(solution)/shard_map/tok_route/ppermute | solution.py:55
  52.1 57.4 %all-to-all-start = ((bf16[16,16,7168]{2,1,0:T(8,128)(2,1)}), bf16[16,16,7168]{2,1,0:T(8,128)(2,1)}, u32[]{:S(2)}, u32[]{:S(2)}) async-start(bf16[16,16,7168]{2,1,0:T(8,128)(2,1)} %bitcast.13), calls=%async_computation | async-start | bytes 7340032 | tf_op jit(solution)/shard_map/cot_route/all_to_all | solution.py:368
  56.6 34.1 %collective-permute-start.10 = (bf16[32,7168]{1,0:T(8,128)(2,1)}, bf16[32,7168]{1,0:T(8,128)(2,1)S(1)}, u32[]{:S(2)}, u32[]{:S(2)}) collective-permute-start(bf16[32,7168]{1,0:T(8,128)(2,1)} %get-tuple-element.33), channel_id=1, source_target_pairs={{0,32},{16,48},{32,64},{48,80},{64,96},{80,112},{96,0},{112,16},{1... | collective-permute-start | bytes 1376264 | tf_op jit(solution)/shard_map/tok_route/ppermute | solution.py:47
  57.4 37.8 %collective-permute-start.11 = (bf16[32,7168]{1,0:T(8,128)(2,1)}, bf16[32,7168]{1,0:T(8,128)(2,1)S(1)}, u32[]{:S(2)}, u32[]{:S(2)}) collective-permute-start(bf16[32,7168]{1,0:T(8,128)(2,1)} %get-tuple-element.34), channel_id=1, source_target_pairs={{0,64},{16,80},{32,96},{48,112},{64,0},{80,16},{96,32},{112,48},{1... | collective-permute-start | bytes 1376264 | tf_op jit(solution)/shard_map/tok_route/ppermute | solution.py:47
  59.2 36.0 %collective-permute-start.12 = (bf16[32,7168]{1,0:T(8,128)(2,1)}, bf16[32,7168]{1,0:T(8,128)(2,1)S(1)}, u32[]{:S(2)}, u32[]{:S(2)}) collective-permute-start(bf16[32,7168]{1,0:T(8,128)(2,1)} %get-tuple-element.35), channel_id=1, source_target_pairs={{0,96},{16,112},{32,0},{48,16},{64,32},{80,48},{96,64},{112,80},{1... | collective-permute-start | bytes 1376264 | tf_op jit(solution)/shard_map/tok_route/ppermute | solution.py:47
  61.3 34.0 %collective-permute-start.16 = (bf16[32,7168]{1,0:T(8,128)(2,1)}, bf16[32,7168]{1,0:T(8,128)(2,1)S(1)}, u32[]{:S(2)}, u32[]{:S(2)}) collective-permute-start(bf16[32,7168]{1,0:T(8,128)(2,1)} %get-tuple-element.67), channel_id=1, source_target_pairs={{0,96},{16,112},{32,0},{48,16},{64,32},{80,48},{96,64},{112,80},{1... | collective-permute-start | bytes 1376264 | tf_op jit(solution)/shard_map/tok_route/ppermute | solution.py:47
  62.6 32.7 %collective-permute-start.15 = (bf16[32,7168]{1,0:T(8,128)(2,1)}, bf16[32,7168]{1,0:T(8,128)(2,1)S(1)}, u32[]{:S(2)}, u32[]{:S(2)}) collective-permute-start(bf16[32,7168]{1,0:T(8,128)(2,1)} %get-tuple-element.68), channel_id=1, source_target_pairs={{0,64},{16,80},{32,96},{48,112},{64,0},{80,16},{96,32},{112,48},{1... | collective-permute-start | bytes 1376264 | tf_op jit(solution)/shard_map/tok_route/ppermute | solution.py:47
  90.7 4.5 %copy-start.4 = (bf16[32,7168]{1,0:T(8,128)(2,1)}, bf16[32,7168]{1,0:T(8,128)(2,1)S(1)}, u32[]{:S(2)}) copy-start(bf16[32,7168]{1,0:T(8,128)(2,1)S(1)} %collective-permute-done.10.refs_0_.refs_1_) | copy-start | bytes 1376260
  90.7 13.3 %collective-permute-start.14 = (bf16[32,7168]{1,0:T(8,128)(2,1)S(1)}, bf16[32,7168]{1,0:T(8,128)(2,1)S(1)}, u32[]{:S(2)}, u32[]{:S(2)}) collective-permute-start(bf16[32,7168]{1,0:T(8,128)(2,1)S(1)} %get-tuple-element.69), channel_id=1, source_target_pairs={{0,32},{16,48},{32,64},{48,80},{64,96},{80,112},{96,0},{112,16},{1... | collective-permute-start | bytes 1376264 | tf_op jit(solution)/shard_map/tok_route/ppermute | solution.py:47
  95.2 8.8 %copy-start.5 = (bf16[32,7168]{1,0:T(8,128)(2,1)}, bf16[32,7168]{1,0:T(8,128)(2,1)S(1)}, u32[]{:S(2)}) copy-start(bf16[32,7168]{1,0:T(8,128)(2,1)S(1)} %collective-permute-done.11.refs_1_.refs_2_) | copy-start | bytes 1376260
  95.3 8.8 %copy-start.6 = (bf16[32,7168]{1,0:T(8,128)(2,1)}, bf16[32,7168]{1,0:T(8,128)(2,1)S(1)}, u32[]{:S(2)}) copy-start(bf16[32,7168]{1,0:T(8,128)(2,1)S(1)} %collective-permute-done.12.refs_2_.refs_3_) | copy-start | bytes 1376260
  95.3 8.7 %copy-start.7 = (bf16[32,7168]{1,0:T(8,128)(2,1)}, bf16[32,7168]{1,0:T(8,128)(2,1)S(1)}, u32[]{:S(2)}) copy-start(bf16[32,7168]{1,0:T(8,128)(2,1)S(1)} %collective-permute-done.16.refs_5_.refs_7_) | copy-start | bytes 1376260
  95.3 8.7 %copy-start.8 = (bf16[32,7168]{1,0:T(8,128)(2,1)}, bf16[32,7168]{1,0:T(8,128)(2,1)S(1)}, u32[]{:S(2)}) copy-start(bf16[32,7168]{1,0:T(8,128)(2,1)S(1)} %collective-permute-done.15.refs_4_.refs_6_) | copy-start | bytes 1376260
  104.0 0.8 copy-start.9
  107.5 27.7 %collective-permute-start.17 = (bf16[32,7168]{1,0:T(8,128)(2,1)}, bf16[32,7168]{1,0:T(8,128)(2,1)S(1)}, u32[]{:S(2)}, u32[]{:S(2)}) collective-permute-start(bf16[32,7168]{1,0:T(8,128)(2,1)} %get-tuple-element.43), channel_id=1, source_target_pairs={{0,3},{1,0},{2,1},{3,2},{4,7},{5,4},{6,5},{7,6},{8,11},{9,8},{10,9... | collective-permute-start | bytes 1376264 | tf_op jit(solution)/shard_map/shared_out/ppermute | solution.py:66
  107.5 27.7 %collective-permute-start.18 = (bf16[32,7168]{1,0:T(8,128)(2,1)}, bf16[32,7168]{1,0:T(8,128)(2,1)S(1)}, u32[]{:S(2)}, u32[]{:S(2)}) collective-permute-start(bf16[32,7168]{1,0:T(8,128)(2,1)} %get-tuple-element.44), channel_id=1, source_target_pairs={{0,2},{1,3},{2,0},{3,1},{4,6},{5,7},{6,4},{7,5},{8,10},{9,11},{10,... | collective-permute-start | bytes 1376264 | tf_op jit(solution)/shard_map/shared_out/ppermute | solution.py:66
  107.9 27.3 %collective-permute-start.19 = (bf16[32,7168]{1,0:T(8,128)(2,1)}, bf16[32,7168]{1,0:T(8,128)(2,1)}, u32[]{:S(2)}, u32[]{:S(2)}) collective-permute-start(bf16[32,7168]{1,0:T(8,128)(2,1)} %get-tuple-element.45), channel_id=1, source_target_pairs={{0,1},{1,2},{2,3},{3,0},{4,5},{5,6},{6,7},{7,4},{8,9},{9,10},{10,1... | collective-permute-start | bytes 1376264 | tf_op jit(solution)/shard_map/shared_out/ppermute | solution.py:66
  109.5 25.7 %copy-start.10 = (bf16[32,7168]{1,0:T(8,128)(2,1)S(1)}, bf16[32,7168]{1,0:T(8,128)(2,1)}, u32[]{:S(2)}) copy-start(bf16[32,7168]{1,0:T(8,128)(2,1)} %get-tuple-element.39._) | copy-start | bytes 1376260
  135.1 13.4 %collective-permute-start.23 = (bf16[128,7168]{1,0:T(8,128)(2,1)}, bf16[128,7168]{1,0:T(8,128)(2,1)S(1)}, u32[]{:S(2)}, u32[]{:S(2)}) collective-permute-start(bf16[128,7168]{1,0:T(8,128)(2,1)} %get-tuple-element.50), channel_id=1, source_target_pairs={{0,16},{16,0},{32,48},{48,32},{64,80},{80,64},{96,112},{112,96},{1... | collective-permute-start | bytes 5505032 | tf_op jit(solution)/shard_map/back_route/ppermute | solution.py:55
  137.5 57.9 %all-to-all-start.1 = ((bf16[16,16,7168]{2,1,0:T(8,128)(2,1)}), bf16[16,16,7168]{2,1,0:T(8,128)(2,1)}, u32[]{:S(2)}, u32[]{:S(2)}) async-start(bf16[16,16,7168]{2,1,0:T(8,128)(2,1)} %bitcast.8), calls=%async_computation.1 | async-start | bytes 7340032 | tf_op jit(solution)/shard_map/out_route/all_to_all | solution.py:443
  145.8 13.6 %collective-permute-start.20 = (bf16[32,7168]{1,0:T(8,128)(2,1)}, bf16[32,7168]{1,0:T(8,128)(2,1)S(1)}, u32[]{:S(2)}, u32[]{:S(2)}) collective-permute-start(bf16[32,7168]{1,0:T(8,128)(2,1)} %get-tuple-element.47), channel_id=1, source_target_pairs={{0,96},{16,112},{32,0},{48,16},{64,32},{80,48},{96,64},{112,80},{1... | collective-permute-start | bytes 1376264 | tf_op jit(solution)/shard_map/back_route/ppermute | solution.py:47
  146.7 15.2 %collective-permute-start.21 = (bf16[32,7168]{1,0:T(8,128)(2,1)}, bf16[32,7168]{1,0:T(8,128)(2,1)S(1)}, u32[]{:S(2)}, u32[]{:S(2)}) collective-permute-start(bf16[32,7168]{1,0:T(8,128)(2,1)} %get-tuple-element.48), channel_id=1, source_target_pairs={{0,64},{16,80},{32,96},{48,112},{64,0},{80,16},{96,32},{112,48},{1... | collective-permute-start | bytes 1376264 | tf_op jit(solution)/shard_map/back_route/ppermute | solution.py:47
  148.5 22.2 %collective-permute-start.22 = (bf16[32,7168]{1,0:T(8,128)(2,1)}, bf16[32,7168]{1,0:T(8,128)(2,1)S(1)}, u32[]{:S(2)}, u32[]{:S(2)}) collective-permute-start(bf16[32,7168]{1,0:T(8,128)(2,1)} %get-tuple-element.49), channel_id=1, source_target_pairs={{0,32},{16,48},{32,64},{48,80},{64,96},{80,112},{96,0},{112,16},{1... | collective-permute-start | bytes 1376264 | tf_op jit(solution)/shard_map/back_route/ppermute | solution.py:47
  149.5 32.0 %collective-permute-start.26 = (bf16[32,7168]{1,0:T(8,128)(2,1)S(1)}, bf16[32,7168]{1,0:T(8,128)(2,1)S(1)}, u32[]{:S(2)}, u32[]{:S(2)}) collective-permute-start(bf16[32,7168]{1,0:T(8,128)(2,1)S(1)} %get-tuple-element.62), channel_id=1, source_target_pairs={{0,32},{16,48},{32,64},{48,80},{64,96},{80,112},{96,0},{112,16},{1... | collective-permute-start | bytes 1376264 | tf_op jit(solution)/shard_map/back_route/ppermute | solution.py:47
  151.1 39.2 %collective-permute-start.25 = (bf16[32,7168]{1,0:T(8,128)(2,1)S(1)}, bf16[32,7168]{1,0:T(8,128)(2,1)S(1)}, u32[]{:S(2)}, u32[]{:S(2)}) collective-permute-start(bf16[32,7168]{1,0:T(8,128)(2,1)S(1)} %get-tuple-element.63), channel_id=1, source_target_pairs={{0,64},{16,80},{32,96},{48,112},{64,0},{80,16},{96,32},{112,48},{1... | collective-permute-start | bytes 1376264 | tf_op jit(solution)/shard_map/back_route/ppermute | solution.py:47
  159.4 36.0 %copy-start.14 = (bf16[32,7168]{1,0:T(8,128)(2,1)}, bf16[32,7168]{1,0:T(8,128)(2,1)S(1)}, u32[]{:S(2)}) copy-start(bf16[32,7168]{1,0:T(8,128)(2,1)S(1)} %collective-permute-done.20.refs_2_) | copy-start | bytes 1376260
  159.4 30.9 %collective-permute-start.24 = (bf16[32,7168]{1,0:T(8,128)(2,1)S(1)}, bf16[32,7168]{1,0:T(8,128)(2,1)S(1)}, u32[]{:S(2)}, u32[]{:S(2)}) collective-permute-start(bf16[32,7168]{1,0:T(8,128)(2,1)S(1)} %get-tuple-element.64), channel_id=1, source_target_pairs={{0,96},{16,112},{32,0},{48,16},{64,32},{80,48},{96,64},{112,80},{1... | collective-permute-start | bytes 1376264 | tf_op jit(solution)/shard_map/back_route/ppermute | solution.py:47
  161.8 33.6 %copy-start.15 = (bf16[32,7168]{1,0:T(8,128)(2,1)}, bf16[32,7168]{1,0:T(8,128)(2,1)S(1)}, u32[]{:S(2)}) copy-start(bf16[32,7168]{1,0:T(8,128)(2,1)S(1)} %collective-permute-done.21.refs_3_) | copy-start | bytes 1376260
  170.7 19.6 %copy-start.16 = (bf16[32,7168]{1,0:T(8,128)(2,1)}, bf16[32,7168]{1,0:T(8,128)(2,1)S(1)}, u32[]{:S(2)}) copy-start(bf16[32,7168]{1,0:T(8,128)(2,1)S(1)} %collective-permute-done.22.refs_4_) | copy-start | bytes 1376260
  181.4 14.0 %copy-start.17 = (bf16[32,7168]{1,0:T(8,128)(2,1)}, bf16[32,7168]{1,0:T(8,128)(2,1)S(1)}, u32[]{:S(2)}) copy-start(bf16[32,7168]{1,0:T(8,128)(2,1)S(1)} %collective-permute-done.26.refs_8_) | copy-start | bytes 1376260
  190.3 5.2 %copy-start.18 = (bf16[32,7168]{1,0:T(8,128)(2,1)}, bf16[32,7168]{1,0:T(8,128)(2,1)S(1)}, u32[]{:S(2)}) copy-start(bf16[32,7168]{1,0:T(8,128)(2,1)S(1)} %collective-permute-done.25.refs_7_) | copy-start | bytes 1376260
  190.3 5.2 %copy-start.19 = (bf16[32,7168]{1,0:T(8,128)(2,1)}, bf16[32,7168]{1,0:T(8,128)(2,1)S(1)}, u32[]{:S(2)}) copy-start(bf16[32,7168]{1,0:T(8,128)(2,1)S(1)} %collective-permute-done.24.refs_6_) | copy-start | bytes 1376260
  199.8 18.5 %copy-start.11 = (bf16[32,7168]{1,0:T(8,128)(2,1)S(1)}, bf16[32,7168]{1,0:T(8,128)(2,1)}, u32[]{:S(2)}) copy-start(bf16[32,7168]{1,0:T(8,128)(2,1)} %get-tuple-element.52.refs_0_) | copy-start | bytes 1376260
  199.8 14.6 %collective-permute-start.31 = (bf16[32,7168]{1,0:T(8,128)(2,1)}, bf16[32,7168]{1,0:T(8,128)(2,1)S(1)}, u32[]{:S(2)}, u32[]{:S(2)}) collective-permute-start(bf16[32,7168]{1,0:T(8,128)(2,1)} %get-tuple-element.55), channel_id=1, source_target_pairs={{0,3},{1,0},{2,1},{3,2},{4,7},{5,4},{6,5},{7,6},{8,11},{9,8},{10,9... | collective-permute-start | bytes 1376264 | tf_op jit(solution)/shard_map/back_route/ppermute | solution.py:66
  203.2 11.2 %collective-permute-start.32 = (bf16[32,7168]{1,0:T(8,128)(2,1)}, bf16[32,7168]{1,0:T(8,128)(2,1)S(1)}, u32[]{:S(2)}, u32[]{:S(2)}) collective-permute-start(bf16[32,7168]{1,0:T(8,128)(2,1)} %get-tuple-element.56), channel_id=1, source_target_pairs={{0,2},{1,3},{2,0},{3,1},{4,6},{5,7},{6,4},{7,5},{8,10},{9,11},{10,... | collective-permute-start | bytes 1376264 | tf_op jit(solution)/shard_map/back_route/ppermute | solution.py:66
  204.1 14.2 %collective-permute-start.33 = (bf16[32,7168]{1,0:T(8,128)(2,1)}, bf16[32,7168]{1,0:T(8,128)(2,1)S(1)}, u32[]{:S(2)}, u32[]{:S(2)}) collective-permute-start(bf16[32,7168]{1,0:T(8,128)(2,1)} %get-tuple-element.57), channel_id=1, source_target_pairs={{0,1},{1,2},{2,3},{3,0},{4,5},{5,6},{6,7},{7,4},{8,9},{9,10},{10,1... | collective-permute-start | bytes 1376264 | tf_op jit(solution)/shard_map/back_route/ppermute | solution.py:66
  208.8 18.4 %copy-start.13 = (f32[32,7168]{1,0:T(8,128)S(1)}, f32[32,7168]{1,0:T(8,128)}, u32[]{:S(2)}) copy-start(f32[32,7168]{1,0:T(8,128)} %get-tuple-element.53) | copy-start | bytes 2752516
  208.8 18.4 %collective-permute-start.27 = (bf16[32,7168]{1,0:T(8,128)(2,1)}, bf16[32,7168]{1,0:T(8,128)(2,1)S(1)}, u32[]{:S(2)}, u32[]{:S(2)}) collective-permute-start(bf16[32,7168]{1,0:T(8,128)(2,1)} %get-tuple-element.54), channel_id=1, source_target_pairs={{0,16},{16,0},{32,48},{48,32},{64,80},{80,64},{96,112},{112,96},{1... | collective-permute-start | bytes 1376264 | tf_op jit(solution)/shard_map/out_sum/ppermute | solution.py:55
  218.6 10.9 %collective-permute-start.34 = (bf16[8,14336]{1,0:T(8,128)(2,1)S(1)}, bf16[8,14336]{1,0:T(8,128)(2,1)S(1)}, u32[]{:S(2)}, u32[]{:S(2)}) collective-permute-start(bf16[8,14336]{1,0:T(8,128)(2,1)S(1)} %get-tuple-element.70), channel_id=1, source_target_pairs={{0,12},{1,13},{2,14},{3,15},{4,0},{5,1},{6,2},{7,3},{8,4},{9,5},{1... | collective-permute-start | bytes 688136 | tf_op jit(solution)/shard_map/back_route/ppermute | solution.py:66
  221.6 8.5 %collective-permute-start.36 = (bf16[8,14336]{1,0:T(8,128)(2,1)S(1)}, bf16[8,14336]{1,0:T(8,128)(2,1)S(1)}, u32[]{:S(2)}, u32[]{:S(2)}) collective-permute-start(bf16[8,14336]{1,0:T(8,128)(2,1)S(1)} %get-tuple-element.71), channel_id=1, source_target_pairs={{0,4},{1,5},{2,6},{3,7},{4,8},{5,9},{6,10},{7,11},{8,12},{9,13},{1... | collective-permute-start | bytes 688136 | tf_op jit(solution)/shard_map/back_route/ppermute | solution.py:66
  221.6 12.1 %collective-permute-start.35 = (bf16[8,14336]{1,0:T(8,128)(2,1)S(1)}, bf16[8,14336]{1,0:T(8,128)(2,1)S(1)}, u32[]{:S(2)}, u32[]{:S(2)}) collective-permute-start(bf16[8,14336]{1,0:T(8,128)(2,1)S(1)} %get-tuple-element.72), channel_id=1, source_target_pairs={{0,8},{1,9},{2,10},{3,11},{4,12},{5,13},{6,14},{7,15},{8,0},{9,1},... | collective-permute-start | bytes 688136 | tf_op jit(solution)/shard_map/back_route/ppermute | solution.py:66
  227.4 7.1 %collective-permute-start.28 = (bf16[8,7168]{1,0:T(8,128)(2,1)S(1)}, bf16[8,7168]{1,0:T(8,128)(2,1)S(1)}, u32[]{:S(2)}, u32[]{:S(2)}) collective-permute-start(bf16[8,7168]{1,0:T(8,128)(2,1)S(1)} %get-tuple-element.73), channel_id=1, source_target_pairs={{0,96},{16,112},{32,0},{48,16},{64,32},{80,48},{96,64},{112,80},{1... | collective-permute-start | bytes 344072 | tf_op jit(solution)/shard_map/out_sum/ppermute | solution.py:47
  228.3 6.2 %collective-permute-start.30 = (bf16[8,7168]{1,0:T(8,128)(2,1)S(1)}, bf16[8,7168]{1,0:T(8,128)(2,1)S(1)}, u32[]{:S(2)}, u32[]{:S(2)}) collective-permute-start(bf16[8,7168]{1,0:T(8,128)(2,1)S(1)} %get-tuple-element.74), channel_id=1, source_target_pairs={{0,32},{16,48},{32,64},{48,80},{64,96},{80,112},{96,0},{112,16},{1... | collective-permute-start | bytes 344072 | tf_op jit(solution)/shard_map/out_sum/ppermute | solution.py:47
  229.5 6.3 %collective-permute-start.29 = (bf16[8,7168]{1,0:T(8,128)(2,1)S(1)}, bf16[8,7168]{1,0:T(8,128)(2,1)S(1)}, u32[]{:S(2)}, u32[]{:S(2)}) collective-permute-start(bf16[8,7168]{1,0:T(8,128)(2,1)S(1)} %get-tuple-element.75), channel_id=1, source_target_pairs={{0,64},{16,80},{32,96},{48,112},{64,0},{80,16},{96,32},{112,48},{1... | collective-permute-start | bytes 344072 | tf_op jit(solution)/shard_map/out_sum/ppermute | solution.py:47

commit v4 on v3

--- a/solution.py
+++ b/solution.py
@@ -259,10 +259,23 @@
         outs[n][...] = total[n * 32 : n * 32 + 32].astype(BF16)
 
 
-def shared_out_kernel(hid, sd, *outs):
-    total = dot(hid[...], sd[...]).astype(BF16)
-    for n in range(4):
-        outs[n][...] = total[n * 32 : n * 32 + 32]
+def shared_out_kernel(hid, sd, l0, l1, l2, l3, mine, line, *both):
+    step = pl.program_id(0)
+    half = pl.num_programs(0) // 2
+
+    @pl.when(step < half)
+    def _():
+        total = dot(hid[...], sd[...]).astype(BF16)
+        mine[...] = total[:32]
+        for n in range(3):
+            both[n][...] = total[n * 32 + 32 : n * 32 + 64]
+
+    @pl.when(step >= half)
+    def _():
+        rows = jnp.concatenate([l0[...], l1[...], l2[...], l3[...]], axis=0)
+        line[...] = rows
+        for n in range(3):
+            both[n][...] = rows
 
 
 def pass_on(v, after):
@@ -284,26 +297,40 @@
 
 
 def shared_kernel(*refs):
-    xs, gs, (sg, su, sd), (hid, grads, acc, acc_g) = refs[:4], refs[4:8], refs[8:11], refs[11:]
+    xs, (sg, su, hid, act, slope, acc) = refs[:4], refs[4:]
     step = pl.program_id(0)
     part = sg.shape[0]
 
     @pl.when(step == 0)
     def _():
         acc[...] = jnp.zeros_like(acc)
-        acc_g[...] = jnp.zeros_like(acc_g)
-
-    rows = jnp.concatenate([x[...] for x in xs], axis=0)
-    acc[...] += dot_t(rows, jnp.concatenate([sg[...], su[...]], axis=0))
-    acc_g[...] += dot_t(jnp.concatenate([g[...] for g in gs], axis=0), sd[...])
+
+    acc[...] += dot_t(jnp.concatenate([x[...] for x in xs], axis=0), jnp.concatenate([sg[...], su[...]], axis=0))
 
     @pl.when(step == pl.num_programs(0) - 1)
     def _():
         up = acc[:, part:]
         silu, prime = silu_parts(acc[:, :part])
         hid[...] = (silu * up).astype(BF16)
-        grads[:, :part] = (acc_g[...] * up * prime).astype(BF16)
-        grads[:, part:] = (acc_g[...] * silu).astype(BF16)
+        act[...] = silu
+        slope[...] = up * prime
+
+
+def shared_grad_kernel(*refs):
+    gs, (sd, act, slope, grads, acc) = refs[:4], refs[4:]
+    step = pl.program_id(0)
+    part = sd.shape[0]
+
+    @pl.when(step == 0)
+    def _():
+        acc[...] = jnp.zeros_like(acc)
+
+    acc[...] += dot_t(jnp.concatenate([g[...] for g in gs], axis=0), sd[...])
+
+    @pl.when(step == pl.num_programs(0) - 1)
+    def _():
+        grads[:, :part] = (acc[...] * slope[...]).astype(BF16)
+        grads[:, part:] = (acc[...] * act[...]).astype(BF16)
 
 
 def local(
@@ -346,7 +373,7 @@
     with jax.named_scope("gather_line"):
         all_line = ring(move_a, all_wide)
     with jax.named_scope("gather_plane"):
-        plane = ring(move_b, jnp.concatenate(all_line, axis=0))
+        plane = ring(move_b, jnp.concatenate([v[:, width:] for v in all_line], axis=0))
     with jax.named_scope("cot_gather"):
         g_chip = jnp.concatenate([g_wide, swap_core(g_wide)], axis=0)
         g_half = jnp.concatenate([move_y_apart(g_chip), move_y(g_wide, 2)], axis=0)
@@ -373,8 +400,8 @@
             tok_pick_kernel,
             steps,
             [SM(at)]
-            + [(b, (32, BLK), lambda i: (0, steps + i)) for b in plane]
-            + [(b, (32, INFO), lambda i: (0, 2 * tail)) for b in plane],
+            + [(b, (32, BLK), COL) for b in plane]
+            + [(b, (32, INFO), info_at) for b in plane],
             [((32, width), BF16, (32, BLK), COL)] * 4
             + [((128, width), BF16, (128, BLK), COL), ((256, 128), BF16, (256, 128), FIX)],
             [pltpu.VMEM((256, 128), BF16)],
@@ -389,31 +416,33 @@
         x_rows += [x_over[0]] + [move_y(x_over[k], k) for k in (1, 2, 3)]
 
     with jax.named_scope("shared"):
-        s_hid, s_grads = call(
+        pre = ((128, part), F32, (128, part), FIX)
+        s_hid, s_act, s_slope = call(
             shared_kernel,
             steps,
-            [(v, (32, BLK), lambda i: (0, steps + i)) for v in plane]
-            + [(v, (32, BLK), COL) for v in plane]
-            + [(shared_gate.T, (part, BLK), COL), (shared_up.T, (part, BLK), COL), (shared_down, (part, BLK), COL)],
-            [((128, part), BF16, (128, part), FIX), ((128, 2 * part), BF16, (128, 2 * part), FIX)],
-            [pltpu.VMEM((128, 2 * part), F32), pltpu.VMEM((128, part), F32)],
-            6 * 128 * part * width,
-            2 * 450 * width,
+            [(v, (32, BLK), COL) for v in plane] + [(shared_gate.T, (part, BLK), COL), (shared_up.T, (part, BLK), COL)],
+            [((128, part), BF16, (128, part), FIX), pre, pre],
+            [pltpu.VMEM((128, 2 * part), F32)],
+            4 * 128 * part * width,
+            2 * 256 * width,
             after=[x_mix],
         )
-
     with jax.named_scope("shared_out"):
-        s_parts = call(
+        s_mine, c_line, *both = call(
             shared_out_kernel,
-            steps,
-            [(s_hid, (128, part), FIX), (shared_down, (part, BLK), COL)],
-            [((32, width), BF16, (32, BLK), COL)] * 4,
+            2 * steps,
+            [(s_hid, (128, part), FIX), (shared_down, (part, BLK), first)] + [(v, (8, BLK), later) for v in all_line],
+            [((32, width), BF16, (32, BLK), first), ((32, width), BF16, (32, BLK), later)]
+            + [((32, 2 * width), BF16, (32, BLK), COL)] * 3,
             [],
             2 * 128 * part * width,
             2 * 192 * width,
             after=x_rows[1:4] + x_rows[5:],
         )
-        s_line = ring_sum(move_b, s_parts)
+        both = [move_b(v, -k) for v, k in zip(both, (1, 2, 3), strict=True)]
+        s_line = s_mine.astype(F32)
+        for v in both:
+            s_line = s_line + v[:, :width].astype(F32)
 
     with jax.named_scope("expert"):
         chunks = width // CHUNK
@@ -437,15 +466,27 @@
                 pltpu.SemaphoreType.DMA((1, chunks)),
             ],
             compiler_params=pltpu.CompilerParams(vmem_limit_bytes=60 * 1024 * 1024),
-        )(at, s_parts[0], *x_rows, g_rows, expert_gate, expert_up, expert_down)
+        )(at, s_mine, *x_rows, g_rows, expert_gate, expert_up, expert_down)
     with jax.named_scope("out_route"):
-        y_rows = pass_on(y_rows, [s_line])
+        y_rows = pass_on(y_rows, [s_line, *both])
         y_home = lax.all_to_all(y_rows.reshape(16, 16, width), "exp", split_axis=0, concat_axis=0, tiled=True)
         y_home = y_home.reshape(256, width)
 
     with jax.named_scope("back_route"):
         dx_home = [dx_rows[0]] + [move_y(dx_rows[k], -k) for k in (1, 2, 3)]
-        dx_over = swap_core(dx_over)
+        (s_grads,) = call(
+            shared_grad_kernel,
+            steps,
+            [(c_line, (32, BLK), COL)]
+            + [(v, (32, BLK), lambda i: (0, steps + i)) for v in reversed(both)]
+            + [(shared_down, (part, BLK), COL), (s_act, (128, part), FIX), (s_slope, (128, part), FIX)],
+            [((128, 2 * part), BF16, (128, 2 * part), FIX)],
+            [pltpu.VMEM((128, part), F32)],
+            2 * 128 * part * width,
+            2 * 200 * width,
+            after=[y_rows],
+        )
+        dx_over = pass_on(swap_core(dx_over), [s_grads])
         dx_over = [dx_over[k * 32 : k * 32 + 32] for k in range(4)]
         dx_home += [dx_over[0]] + [move_y(dx_over[k], -k) for k in (1, 2, 3)]
         parts = call(

time: 237 us -> 229 us (0.966)
  waiting for transfers between devices: 113 us -> 95.7 us
  local copies, waits for them, and re-layouts: 5.6 us -> 9.74 us
  Pallas kernels: 51 us -> 54.8 us
    ppermute x15, waiting for transfers between devices: 36.2 us -> 24.5 us  [move_plane(): return lax.ppermute(v, ('grp', 'exp'), pairs)]
    ppermute x16, waiting for transfers between devices: 71 us -> 66.4 us  [move_y(): lax.ppermute(v, 'grp', [(y * 2 + c, (y + k) % N_Y * 2 + c) for y in range...]
    pallas_call x7 -> x8, Pallas kernels: 25.4 us -> 29.3 us  [call(): pl.pallas_call(lambda *refs: kernel(*refs[skip:]), grid=(grid,), in_specs...]
    ppermute x16, starting transfers between devices: 21.5 us -> 25 us  [move_y(): lax.ppermute(v, 'grp', [(y * 2 + c, (y + k) % N_Y * 2 + c) for y in range...]
  transfers between devices with their start and end apart: 39 -> 39, of which waited for: 16 -> 16; matrix products, arithmetic and copies ran while one was open for 3% -> 4% of each run, Pallas kernels for 17% -> 19%
where the time goes in v4:
time: 229 us; the launch traced here: 228 us
  waiting for transfers between devices  95.7 us (42%)
  starting transfers between devices  62.7 us (27%)
  Pallas kernels  54.8 us (24%)
  local copies, waits for them, and re-layouts  9.74 us (4%)
  other arithmetic  4.49 us (2%)
    ppermute x16, waiting for transfers between devices, move_y(): lax.ppermute(v, 'grp', [(y * 2 + c, (y + k) % N_Y * 2 + c) for y in range...  66.4 us
    pallas_call x8, Pallas kernels, call(): pl.pallas_call(lambda *refs: kernel(*refs[skip:]), grid=(grid,), in_specs...  29.3 us
    ppermute x15, starting transfers between devices, move_plane(): return lax.ppermute(v, ('grp', 'exp'), pairs)  26.1 us
    pallas_call x1, Pallas kernels, local(): pl.pallas_call(expert_kernel, in_specs=[pl.BlockSpec(memory_space=pltpu.S...  25.5 us
    ppermute x16, starting transfers between devices, move_y(): lax.ppermute(v, 'grp', [(y * 2 + c, (y + k) % N_Y * 2 + c) for y in range...  25 us
    ppermute x15, waiting for transfers between devices, move_plane(): return lax.ppermute(v, ('grp', 'exp'), pairs)  24.5 us
    all_to_all x1, starting transfers between devices, local(): lax.all_to_all(y_rows.reshape(16, 16, width), 'exp', split_axis=0, concat...  5.99 us
    all_to_all x1, starting transfers between devices, local(): lax.all_to_all(g_sent.reshape(16, 16, width), 'exp', split_axis=0, concat...  4.64 us
  transfers between devices with their start and end apart: 39, of which 16 were waited for; matrix products, arithmetic and copies ran while one was open for 4% of the time, Pallas kernels for 19%

profile of v4, /device:TPU:0, one launch (start us, length us, event | category | flops | bytes accessed | tf_op | source)
XLA Modules:
  0.0 228.5 jit_solution(1785870369447898827)
XLA Ops:
  0.6 1.8 widen.1
  2.4 3.3 %collective-permute-start.2 = (bf16[8,7296]{1,0:T(8,128)(2,1)}, bf16[8,7296]{1,0:T(8,128)(2,1)S(1)}, u32[]{:S(2)}, u32[]{:S(2)}) collective-permute-start(bf16[8,7296]{1,0:T(8,128)(2,1)} %get-tuple-element.32), channel_id=1, source_target_pairs={{0,64},{16,80},{32,96},{48,112},{64,0},{80,16},{96,32},{112,48},{1... | collective-permute-start | bytes 350216 | tf_op jit(solution)/shard_map/cot_gather/ppermute | solution.py:47
  5.7 2.8 %collective-permute-start.6 = (bf16[8,14464]{1,0:T(8,128)(2,1)}, bf16[8,14464]{1,0:T(8,128)(2,1)S(1)}, u32[]{:S(2)}, u32[]{:S(2)}) collective-permute-start(bf16[8,14464]{1,0:T(8,128)(2,1)} %get-tuple-element.34.refs_8_), channel_id=1, source_target_pairs={{0,12},{1,13},{2,14},{3,15},{4,0},{5,1},{6,2},{7,3},{8,4},{9,5},{1... | collective-permute-start | bytes 694280 | tf_op jit(solution)/shard_map/gather_line/ppermute | solution.py:66
  8.5 0.8 collective-permute-start.5
  9.3 0.9 collective-permute-start.4
  10.2 0.9 constant_dynamic-update-slice_fusion.1
  11.1 0.9 slice.87
  12.0 0.7 collective-permute-start.1
  12.8 2.1 collective-permute-done.6.refs_11_
  14.9 1.5 collective-permute-done.5.refs_10_
  16.4 2.4 %collective-permute-done.4.refs_9_ = bf16[8,14464]{1,0:T(8,128)(2,1)S(1)} collective-permute-done((bf16[8,14464]{1,0:T(8,128)(2,1)}, bf16[8,14464]{1,0:T(8,128)(2,1)S(1)}, u32[]{:S(2)}, u32[]{:S(2)}) %collective-permute-start.4) | collective-permute-done | bytes 231456 | tf_op jit(solution)/shard_map/gather_line/ppermute | solution.py:66
  18.8 4.1 %collective-permute-start.9 = (bf16[32,7296]{1,0:T(8,128)(2,1)S(1)}, bf16[32,7296]{1,0:T(8,128)(2,1)S(1)}, u32[]{:S(2)}, u32[]{:S(2)}) collective-permute-start(bf16[32,7296]{1,0:T(8,128)(2,1)S(1)} %pad_maximum_fusion.refs_2_.refs_6_.refs_1_), channel_id=1, source_target_pairs={{0,3},{1,0},{2,1},{3,2},{4,7},{5,4},{6,5},{7,6},{8,11},{9,8},{10,9... | collective-permute-start | bytes 1400840 | tf_op jit(solution)/shard_map/gather_plane/ppermute | solution.py:66
  22.9 1.3 collective-permute-start.7
  24.3 0.6 pad_add_fusion.refs_0_.refs_1_.at
  25.0 1.0 collective-permute-done.3.refs_3_.refs_6_
  26.0 0.7 copy-done.16
  26.7 4.3 %cot_pick.1 = (bf16[256,7168]{1,0:T(8,128)(2,1)}, bf16[256,64]{1,0:T(8,128)(2,1)}) custom-call(s32[2]{0:T(128)} %pad_add_fusion.refs_0_.refs_1_.at, bf16[16,7296]{1,0:T(8,128)(2,1)} %copy-done.15, bf16[24,7296]{1,0:T(8,128)(2,1)} %copy-done.6, bf16[24,7296]{1,0:T(8,128)(2,1)} %copy-done.16, bf16[16,7296]{1,0:T(8,128)(2,1)} %copy-done.15, ...), custom_call_target="tpu_custom_call" | custom-call | flops 234881024 | bytes 4587520 | tf_op jit(solution)/shard_map/cot_pick/pallas_call | solution.py:93
  31.0 3.0 %collective-permute-done.9.refs_5_.refs_9_.refs_4_ = bf16[32,7296]{1,0:T(8,128)(2,1)S(1)} collective-permute-done((bf16[32,7296]{1,0:T(8,128)(2,1)S(1)}, bf16[32,7296]{1,0:T(8,128)(2,1)S(1)}, u32[]{:S(2)}, u32[]{:S(2)}) %collective-permute-start.9) | collective-permute-done | bytes 466976 | tf_op jit(solution)/shard_map/gather_plane/ppermute | solution.py:66
  34.0 3.7 %collective-permute-done.7.refs_3_.refs_7_.refs_2_ = bf16[32,7296]{1,0:T(8,128)(2,1)S(1)} collective-permute-done((bf16[32,7296]{1,0:T(8,128)(2,1)S(1)}, bf16[32,7296]{1,0:T(8,128)(2,1)S(1)}, u32[]{:S(2)}, u32[]{:S(2)}) %collective-permute-start.7) | collective-permute-done | bytes 466976 | tf_op jit(solution)/shard_map/gather_plane/ppermute | solution.py:66
  37.7 0.8 copy-done.5
  38.5 4.3 %tok_pick.1 = (bf16[32,7168]{1,0:T(8,128)(2,1)}, bf16[32,7168]{1,0:T(8,128)(2,1)}, bf16[32,7168]{1,0:T(8,128)(2,1)}, bf16[32,7168]{1,0:T(8,128)(2,1)}, bf16[128,...) custom-call(bf16[256,64]{1,0:T(8,128)(2,1)} %get-tuple-element.33.refs_0_.refs_2_, s32[2]{0:T(128)} %pad_add_fusion.refs_0_.refs_1_.at, ...), custom_call_target="tpu_custom_call" | custom-call | flops 469762048 | bytes 5734400 | tf_op jit(solution)/shard_map/tok_pick/pallas_call | solution.py:93
  42.9 4.6 %all-to-all-start = ((bf16[16,16,7168]{2,1,0:T(8,128)(2,1)}), bf16[16,16,7168]{2,1,0:T(8,128)(2,1)}, u32[]{:S(2)}, u32[]{:S(2)}) async-start(bf16[16,16,7168]{2,1,0:T(8,128)(2,1)} %bitcast.13), calls=%async_computation | async-start | bytes 7340032 | tf_op jit(solution)/shard_map/cot_route/all_to_all | solution.py:395
  47.5 0.7 collective-permute-start.10
  48.3 1.8 collective-permute-start.11
  50.1 0.9 collective-permute-start.12
  51.0 1.3 fusion.9
  52.3 1.3 collective-permute-start.16
  53.6 1.8 collective-permute-start.15
  55.5 26.1 %collective-permute-done.10.refs_0_.refs_1_ = bf16[32,7168]{1,0:T(8,128)(2,1)S(1)} collective-permute-done((bf16[32,7168]{1,0:T(8,128)(2,1)}, bf16[32,7168]{1,0:T(8,128)(2,1)S(1)}, u32[]{:S(2)}, u32[]{:S(2)}) %collective-permute-start.10) | collective-permute-done | bytes 458784 | tf_op jit(solution)/shard_map/tok_route/ppermute | solution.py:47
  81.6 3.6 %shared.1 = (bf16[128,64]{1,0:T(8,128)(2,1)}, f32[128,64]{1,0:T(8,128)}, f32[128,64]{1,0:T(8,128)}) custom-call(bf16[256,128]{1,0:T(8,128)(2,1)} %get-tuple-element.39.refs_0_.refs_9_, bf16[32,7296]{1,0:T(8,128)(2,1)} %copy-done, bf16[32,7296]{1,0:T(8,128)(2,1)} %copy-done.5, bf16[32,7296]{1,0:T(8,128)(2,1)} %copy-done.4, bf16[32,7296]{1,0:T(8,128)(2,1)} %copy-done.3, ...), custom_call_target="tpu_custom_call" | custom-call | flops 234881024 | bytes 3670016 | tf_op jit(solution)/shard_map/shared/pallas_call | solution.py:93
  85.2 9.8 %collective-permute-done.14.refs_3_.refs_5_ = bf16[32,7168]{1,0:T(8,128)(2,1)S(1)} collective-permute-done((bf16[32,7168]{1,0:T(8,128)(2,1)}, bf16[32,7168]{1,0:T(8,128)(2,1)S(1)}, u32[]{:S(2)}, u32[]{:S(2)}) %collective-permute-start.14) | collective-permute-done | bytes 458784 | tf_op jit(solution)/shard_map/tok_route/ppermute | solution.py:47
  95.0 0.7 copy-done.12
  95.8 4.5 %shared_out.1 = (bf16[32,7168]{1,0:T(8,128)(2,1)}, bf16[32,7168]{1,0:T(8,128)(2,1)}, bf16[32,14336]{1,0:T(8,128)(2,1)}, bf16[32,14336]{1,0:T(8,128)(2,1)}, bf16[32,14336]{1,0:T(8,128)(2,1)}) custom-call(bf16[32,7168]{1,0:T(8,128)(2,1)} %copy-done.7, bf16[32,7168]{1,0:T(8,128)(2,1)} %copy-done.8, bf16[32,7168]{1,0:T(8,128)(2,1)} %copy-done.9, ...), custom_call_target="tpu_custom_call" | custom-call | flops 117440512 | bytes 2752512 | tf_op jit(solution)/shard_map/shared_out/pallas_call | solution.py:93
  100.3 0.5 collective-permute-start.18
  100.8 1.5 collective-permute-start.19
  102.3 25.5 %expert.1 = (bf16[32,7168]{1,0:T(8,128)(2,1)}, bf16[32,7168]{1,0:T(8,128)(2,1)}, bf16[32,7168]{1,0:T(8,128)(2,1)}, bf16[32,7168]{1,0:T(8,128)(2,1)}, bf16[128,71...) custom-call(s32[2]{0:T(128)} %pad_add_fusion.refs_0_.refs_1_.at, bf16[32,7168]{1,0:T(8,128)(2,1)} %get-tuple-element.41._, ...), custom_call_target="tpu_custom_call" | custom-call | tf_op jit(solution)/shard_map/expert/pallas_call | solution.py:450
  128.0 2.7 %fusion.7 = (bf16[32,7168]{1,0:T(8,128)(2,1)S(1)}, f32[32,7168]{1,0:T(8,128)}) fusion(bf16[32,14336]{1,0:T(8,128)(2,1)} %collective-permute-done.19.refs_4_.refs_2_, bf16[32,14336]{1,0:T(8,128)(2,1)} %collective-permute-done.18.refs_3_, bf16[32,14336]{1,0:T(8,128)(2,1)S(1)} %collective-permute-done.17.refs_2_.refs_4_, bf16[32,7168]{1,0:T(8,128)(2,1)S(1)} %copy-done.13), kind=kLoop, calls=%fused_computation.27 | loop fusion | flops 1835008 | bytes 3211264 | tf_op jit(solution)/shard_map/convert.2
  130.7 6.0 %all-to-all-start.1 = ((bf16[16,16,7168]{2,1,0:T(8,128)(2,1)}), bf16[16,16,7168]{2,1,0:T(8,128)(2,1)}, u32[]{:S(2)}, u32[]{:S(2)}) async-start(bf16[16,16,7168]{2,1,0:T(8,128)(2,1)} %bitcast.8), calls=%async_computation.1 | async-start | bytes 7340032 | tf_op jit(solution)/shard_map/out_route/all_to_all | solution.py:472
  136.7 2.3 %collective-permute-start.20 = (bf16[32,7168]{1,0:T(8,128)(2,1)}, bf16[32,7168]{1,0:T(8,128)(2,1)S(1)}, u32[]{:S(2)}, u32[]{:S(2)}) collective-permute-start(bf16[32,7168]{1,0:T(8,128)(2,1)} %get-tuple-element.49), channel_id=1, source_target_pairs={{0,96},{16,112},{32,0},{48,16},{64,32},{80,48},{96,64},{112,80},{1... | collective-permute-start | bytes 1376264 | tf_op jit(solution)/shard_map/back_route/ppermute | solution.py:47
  139.0 0.5 collective-permute-start.21
  139.9 3.1 %back_route.3.refs_1_.refs_10_ = bf16[128,128]{1,0:T(8,128)(2,1)} custom-call(bf16[256,7168]{1,0:T(8,128)(2,1)} %out_route.1.refs_0_, bf16[32,7168]{1,0:T(8,128)(2,1)} %get-tuple-element.53.refs_1_, bf16[32,14336]{1,0:T(8,128)(2,1)} %collective-permute-done.19.refs_4_.refs_2_, bf16[32,14336]{1,0:T(8,128)(2,1)} %collective-permute-done.18.refs_3_, ...), custom_call_target="tpu_custom_call" | custom-call | flops 117440512 | bytes 2867200 | tf_op jit(solution)/shard_map/back_route/pallas_call | solution.py:93
  143.0 1.2 copy-done.1
  144.2 2.3 %fusion.8 = (bf16[32,7168]{1,0:T(8,128)(2,1)S(1)}, bf16[32,7168]{1,0:T(8,128)(2,1)S(1)}, bf16[32,7168]{1,0:T(8,128)(2,1)S(1)}, bf16[32,7168]{1,0:T(8,128)(2,1)}) fusion(bf16[128,7168]{1,0:T(8,128)(2,1)} %back_route.4), kind=kLoop, calls=%fused_computation.28 | loop fusion | bytes 3670016 | tf_op jit(solution)/shard_map/back_route/slice | solution.py:490
  146.5 2.5 %collective-permute-start.26 = (bf16[32,7168]{1,0:T(8,128)(2,1)S(1)}, bf16[32,7168]{1,0:T(8,128)(2,1)S(1)}, u32[]{:S(2)}, u32[]{:S(2)}) collective-permute-start(bf16[32,7168]{1,0:T(8,128)(2,1)S(1)} %get-tuple-element.66), channel_id=1, source_target_pairs={{0,32},{16,48},{32,64},{48,80},{64,96},{80,112},{96,0},{112,16},{1... | collective-permute-start | bytes 1376264 | tf_op jit(solution)/shard_map/back_route/ppermute | solution.py:47
  149.1 1.7 collective-permute-start.25
  150.8 18.8 %collective-permute-done.20.refs_2_ = bf16[32,7168]{1,0:T(8,128)(2,1)S(1)} collective-permute-done((bf16[32,7168]{1,0:T(8,128)(2,1)}, bf16[32,7168]{1,0:T(8,128)(2,1)S(1)}, u32[]{:S(2)}, u32[]{:S(2)}) %collective-permute-start.20) | collective-permute-done | bytes 458784 | tf_op jit(solution)/shard_map/back_route/ppermute | solution.py:47
  169.6 3.7 %collective-permute-start.24 = (bf16[32,7168]{1,0:T(8,128)(2,1)S(1)}, bf16[32,7168]{1,0:T(8,128)(2,1)S(1)}, u32[]{:S(2)}, u32[]{:S(2)}) collective-permute-start(bf16[32,7168]{1,0:T(8,128)(2,1)S(1)} %get-tuple-element.68), channel_id=1, source_target_pairs={{0,96},{16,112},{32,0},{48,16},{64,32},{80,48},{96,64},{112,80},{1... | collective-permute-start | bytes 1376264 | tf_op jit(solution)/shard_map/back_route/ppermute | solution.py:47
  173.5 9.0 %collective-permute-done.25.refs_7_ = bf16[32,7168]{1,0:T(8,128)(2,1)S(1)} collective-permute-done((bf16[32,7168]{1,0:T(8,128)(2,1)S(1)}, bf16[32,7168]{1,0:T(8,128)(2,1)S(1)}, u32[]{:S(2)}, u32[]{:S(2)}) %collective-permute-start.25) | collective-permute-done | bytes 458784 | tf_op jit(solution)/shard_map/back_route/ppermute | solution.py:47
  182.6 3.7 %all-to-all-done.1 = bf16[16,16,7168]{2,1,0:T(8,128)(2,1)} async-done(((bf16[16,16,7168]{2,1,0:T(8,128)(2,1)}), bf16[16,16,7168]{2,1,0:T(8,128)(2,1)}, u32[]{:S(2)}, u32[]{:S(2)}) %all-to-all-start.1) | async-done | bytes 3670048 | tf_op jit(solution)/shard_map/out_route/all_to_all | solution.py:472
  186.4 4.4 %back_route.5 = (bf16[32,7168]{1,0:T(8,128)(2,1)}, bf16[32,7168]{1,0:T(8,128)(2,1)}, bf16[32,7168]{1,0:T(8,128)(2,1)}, bf16[32,7168]{1,0:T(8,128)(2,1)}) custom-call(bf16[256,7168]{1,0:T(8,128)(2,1)} %bitcast.7.refs_0_.refs_1_, bf16[32,7168]{1,0:T(8,128)(2,1)} %get-tuple-element.48.refs_1_, bf16[32,7168]{1,0:T(8,128)(2,1)} %copy-done.21, ...), custom_call_target="tpu_custom_call" | custom-call | flops 469762048 | bytes 5734400 | tf_op jit(solution)/shard_map/back_route/pallas_call | solution.py:93
  190.8 3.4 %collective-permute-start.31 = (bf16[32,7168]{1,0:T(8,128)(2,1)}, bf16[32,7168]{1,0:T(8,128)(2,1)S(1)}, u32[]{:S(2)}, u32[]{:S(2)}) collective-permute-start(bf16[32,7168]{1,0:T(8,128)(2,1)} %get-tuple-element.59), channel_id=1, source_target_pairs={{0,3},{1,0},{2,1},{3,2},{4,7},{5,4},{6,5},{7,6},{8,11},{9,8},{10,9... | collective-permute-start | bytes 1376264 | tf_op jit(solution)/shard_map/back_route/ppermute | solution.py:66
  194.2 1.0 collective-permute-start.32
  195.1 1.3 collective-permute-start.33
  196.5 3.4 %out_sum.1 = (f32[32,7168]{1,0:T(8,128)}, bf16[32,7168]{1,0:T(8,128)(2,1)}) custom-call(bf16[32,7168]{1,0:T(8,128)(2,1)} %get-tuple-element.56.refs_0_, bf16[256,7168]{1,0:T(8,128)(2,1)} %bitcast.7.refs_0_.refs_1_, bf16[256,64]{1,0:T(8,128)(2,1)} %get-tuple-element.33.refs_0_.refs_2_), custom_call_target="tpu_custom_call" | custom-call | flops 234881024 | bytes 5046272 | tf_op jit(solution)/shard_map/out_sum/pallas_call | solution.py:93
  199.9 5.5 %collective-permute-done.31 = bf16[32,7168]{1,0:T(8,128)(2,1)S(1)} collective-permute-done((bf16[32,7168]{1,0:T(8,128)(2,1)}, bf16[32,7168]{1,0:T(8,128)(2,1)S(1)}, u32[]{:S(2)}, u32[]{:S(2)}) %collective-permute-start.31) | collective-permute-done | bytes 458784 | tf_op jit(solution)/shard_map/back_route/ppermute | solution.py:66
  205.4 3.9 %collective-permute-done.33 = bf16[32,7168]{1,0:T(8,128)(2,1)S(1)} collective-permute-done((bf16[32,7168]{1,0:T(8,128)(2,1)}, bf16[32,7168]{1,0:T(8,128)(2,1)S(1)}, u32[]{:S(2)}, u32[]{:S(2)}) %collective-permute-start.33) | collective-permute-done | bytes 458784 | tf_op jit(solution)/shard_map/back_route/ppermute | solution.py:66
  209.6 2.9 %collective-permute-start.34 = (bf16[8,14336]{1,0:T(8,128)(2,1)S(1)}, bf16[8,14336]{1,0:T(8,128)(2,1)S(1)}, u32[]{:S(2)}, u32[]{:S(2)}) collective-permute-start(bf16[8,14336]{1,0:T(8,128)(2,1)S(1)} %get-tuple-element.74), channel_id=1, source_target_pairs={{0,12},{1,13},{2,14},{3,15},{4,0},{5,1},{6,2},{7,3},{8,4},{9,5},{1... | collective-permute-start | bytes 688136 | tf_op jit(solution)/shard_map/back_route/ppermute | solution.py:66
  212.5 5.6 %collective-permute-start.35 = (bf16[8,14336]{1,0:T(8,128)(2,1)S(1)}, bf16[8,14336]{1,0:T(8,128)(2,1)S(1)}, u32[]{:S(2)}, u32[]{:S(2)}) collective-permute-start(bf16[8,14336]{1,0:T(8,128)(2,1)S(1)} %get-tuple-element.76), channel_id=1, source_target_pairs={{0,8},{1,9},{2,10},{3,11},{4,12},{5,13},{6,14},{7,15},{8,0},{9,1},... | collective-permute-start | bytes 688136 | tf_op jit(solution)/shard_map/back_route/ppermute | solution.py:66
  218.2 2.3 %collective-permute-start.28 = (bf16[8,7168]{1,0:T(8,128)(2,1)S(1)}, bf16[8,7168]{1,0:T(8,128)(2,1)S(1)}, u32[]{:S(2)}, u32[]{:S(2)}) collective-permute-start(bf16[8,7168]{1,0:T(8,128)(2,1)S(1)} %get-tuple-element.77), channel_id=1, source_target_pairs={{0,96},{16,112},{32,0},{48,16},{64,32},{80,48},{96,64},{112,80},{1... | collective-permute-start | bytes 344072 | tf_op jit(solution)/shard_map/out_sum/ppermute | solution.py:47
  220.6 1.5 collective-permute-start.29
  222.1 2.5 %collective-permute-done.35 = bf16[8,14336]{1,0:T(8,128)(2,1)S(1)} collective-permute-done((bf16[8,14336]{1,0:T(8,128)(2,1)S(1)}, bf16[8,14336]{1,0:T(8,128)(2,1)S(1)}, u32[]{:S(2)}, u32[]{:S(2)}) %collective-permute-start.35) | collective-permute-done | bytes 229408 | tf_op jit(solution)/shard_map/back_route/ppermute | solution.py:66
  224.7 0.7 slice.172
  225.3 2.5 %collective-permute-done.30 = bf16[8,7168]{1,0:T(8,128)(2,1)S(1)} collective-permute-done((bf16[8,7168]{1,0:T(8,128)(2,1)S(1)}, bf16[8,7168]{1,0:T(8,128)(2,1)S(1)}, u32[]{:S(2)}, u32[]{:S(2)}) %collective-permute-start.30) | collective-permute-done | bytes 114720 | tf_op jit(solution)/shard_map/out_sum/ppermute | solution.py:47
  227.8 0.7 fusion.3
  (103 shorter events, 1.7 us)
Async XLA Ops:
  2.4 21.7 %collective-permute-start.2 = (bf16[8,7296]{1,0:T(8,128)(2,1)}, bf16[8,7296]{1,0:T(8,128)(2,1)S(1)}, u32[]{:S(2)}, u32[]{:S(2)}) collective-permute-start(bf16[8,7296]{1,0:T(8,128)(2,1)} %get-tuple-element.32), channel_id=1, source_target_pairs={{0,64},{16,80},{32,96},{48,112},{64,0},{80,16},{96,32},{112,48},{1... | collective-permute-start | bytes 350216 | tf_op jit(solution)/shard_map/cot_gather/ppermute | solution.py:47
  5.7 6.3 %collective-permute-start = (bf16[8,7296]{1,0:T(8,128)(2,1)}, bf16[8,7296]{1,0:T(8,128)(2,1)S(1)}, u32[]{:S(2)}, u32[]{:S(2)}) collective-permute-start(bf16[8,7296]{1,0:T(8,128)(2,1)} %get-tuple-element.32), channel_id=1, source_target_pairs={{0,16},{16,0},{32,48},{48,32},{64,80},{80,64},{96,112},{112,96},{1... | collective-permute-start | bytes 350216 | tf_op jit(solution)/shard_map/cot_gather/ppermute | solution.py:55
  5.7 9.1 %collective-permute-start.6 = (bf16[8,14464]{1,0:T(8,128)(2,1)}, bf16[8,14464]{1,0:T(8,128)(2,1)S(1)}, u32[]{:S(2)}, u32[]{:S(2)}) collective-permute-start(bf16[8,14464]{1,0:T(8,128)(2,1)} %get-tuple-element.34.refs_8_), channel_id=1, source_target_pairs={{0,12},{1,13},{2,14},{3,15},{4,0},{5,1},{6,2},{7,3},{8,4},{9,5},{1... | collective-permute-start | bytes 694280 | tf_op jit(solution)/shard_map/gather_line/ppermute | solution.py:66
  8.5 7.9 %collective-permute-start.5 = (bf16[8,14464]{1,0:T(8,128)(2,1)}, bf16[8,14464]{1,0:T(8,128)(2,1)S(1)}, u32[]{:S(2)}, u32[]{:S(2)}) collective-permute-start(bf16[8,14464]{1,0:T(8,128)(2,1)} %get-tuple-element.34.refs_8_), channel_id=1, source_target_pairs={{0,8},{1,9},{2,10},{3,11},{4,12},{5,13},{6,14},{7,15},{8,0},{9,1},... | collective-permute-start | bytes 694280 | tf_op jit(solution)/shard_map/gather_line/ppermute | solution.py:66
  9.3 9.4 %collective-permute-start.4 = (bf16[8,14464]{1,0:T(8,128)(2,1)}, bf16[8,14464]{1,0:T(8,128)(2,1)S(1)}, u32[]{:S(2)}, u32[]{:S(2)}) collective-permute-start(bf16[8,14464]{1,0:T(8,128)(2,1)} %get-tuple-element.34.refs_8_), channel_id=1, source_target_pairs={{0,4},{1,5},{2,6},{3,7},{4,8},{5,9},{6,10},{7,11},{8,12},{9,13},{1... | collective-permute-start | bytes 694280 | tf_op jit(solution)/shard_map/gather_line/ppermute | solution.py:66
  12.0 14.0 %copy-start.15 = (bf16[16,7296]{1,0:T(8,128)(2,1)}, bf16[16,7296]{1,0:T(8,128)(2,1)S(1)}, u32[]{:S(2)}) copy-start(bf16[16,7296]{1,0:T(8,128)(2,1)S(1)} %constant_dynamic-update-slice_fusion.refs_1_.refs_4_) | copy-start | bytes 700420
  12.0 12.1 %collective-permute-start.1 = (bf16[16,7296]{1,0:T(8,128)(2,1)S(1)}, bf16[16,7296]{1,0:T(8,128)(2,1)S(1)}, u32[]{:S(2)}, u32[]{:S(2)}) collective-permute-start(bf16[16,7296]{1,0:T(8,128)(2,1)S(1)} %constant_dynamic-update-slice_fusion.refs_1_.refs_4_), channel_id=1, source_target_pairs={{0,32},{16,112},{32,64},{48,16},{64,96},{80,48},{96,0},{112,80},{1... | collective-permute-start | bytes 700424 | tf_op jit(solution)/shard_map/cot_gather/ppermute | solution.py:51
  14.9 27.9 %copy-start.18 = (bf16[8,14464]{1,0:T(8,128)(2,1)}, bf16[8,14464]{1,0:T(8,128)(2,1)S(1)}, u32[]{:S(2)}) copy-start(bf16[8,14464]{1,0:T(8,128)(2,1)S(1)} %collective-permute-done.6.refs_11_) | copy-start | bytes 694276
  16.4 7.8 %copy-start.19 = (bf16[8,14464]{1,0:T(8,128)(2,1)}, bf16[8,14464]{1,0:T(8,128)(2,1)S(1)}, u32[]{:S(2)}) copy-start(bf16[8,14464]{1,0:T(8,128)(2,1)S(1)} %collective-permute-done.5.refs_10_) | copy-start | bytes 694276
  18.7 5.5 %copy-start.20 = (bf16[8,14464]{1,0:T(8,128)(2,1)}, bf16[8,14464]{1,0:T(8,128)(2,1)S(1)}, u32[]{:S(2)}) copy-start(bf16[8,14464]{1,0:T(8,128)(2,1)S(1)} %collective-permute-done.4.refs_9_) | copy-start | bytes 694276
  18.8 18.9 %copy-start = (bf16[32,7296]{1,0:T(8,128)(2,1)}, bf16[32,7296]{1,0:T(8,128)(2,1)S(1)}, u32[]{:S(2)}) copy-start(bf16[32,7296]{1,0:T(8,128)(2,1)S(1)} %pad_maximum_fusion.refs_2_.refs_6_.refs_1_) | copy-start | bytes 1400836
  18.8 15.2 %collective-permute-start.9 = (bf16[32,7296]{1,0:T(8,128)(2,1)S(1)}, bf16[32,7296]{1,0:T(8,128)(2,1)S(1)}, u32[]{:S(2)}, u32[]{:S(2)}) collective-permute-start(bf16[32,7296]{1,0:T(8,128)(2,1)S(1)} %pad_maximum_fusion.refs_2_.refs_6_.refs_1_), channel_id=1, source_target_pairs={{0,3},{1,0},{2,1},{3,2},{4,7},{5,4},{6,5},{7,6},{8,11},{9,8},{10,9... | collective-permute-start | bytes 1400840 | tf_op jit(solution)/shard_map/gather_plane/ppermute | solution.py:66
  22.9 11.1 %collective-permute-start.8 = (bf16[32,7296]{1,0:T(8,128)(2,1)S(1)}, bf16[32,7296]{1,0:T(8,128)(2,1)S(1)}, u32[]{:S(2)}, u32[]{:S(2)}) collective-permute-start(bf16[32,7296]{1,0:T(8,128)(2,1)S(1)} %pad_maximum_fusion.refs_2_.refs_6_.refs_1_), channel_id=1, source_target_pairs={{0,2},{1,3},{2,0},{3,1},{4,6},{5,7},{6,4},{7,5},{8,10},{9,11},{10,... | collective-permute-start | bytes 1400840 | tf_op jit(solution)/shard_map/gather_plane/ppermute | solution.py:66
  22.9 14.8 %collective-permute-start.7 = (bf16[32,7296]{1,0:T(8,128)(2,1)S(1)}, bf16[32,7296]{1,0:T(8,128)(2,1)S(1)}, u32[]{:S(2)}, u32[]{:S(2)}) collective-permute-start(bf16[32,7296]{1,0:T(8,128)(2,1)S(1)} %pad_maximum_fusion.refs_2_.refs_6_.refs_1_), channel_id=1, source_target_pairs={{0,1},{1,2},{2,3},{3,0},{4,5},{5,6},{6,7},{7,4},{8,9},{9,10},{10,1... | collective-permute-start | bytes 1400840 | tf_op jit(solution)/shard_map/gather_plane/ppermute | solution.py:66
  24.2 1.8 copy-start.6
  24.2 1.7 collective-permute-start.3
  34.0 3.7 %copy-start.3 = (bf16[32,7296]{1,0:T(8,128)(2,1)}, bf16[32,7296]{1,0:T(8,128)(2,1)S(1)}, u32[]{:S(2)}) copy-start(bf16[32,7296]{1,0:T(8,128)(2,1)S(1)} %collective-permute-done.9.refs_5_.refs_9_.refs_4_) | copy-start | bytes 1400836
  34.0 3.7 %copy-start.4 = (bf16[32,7296]{1,0:T(8,128)(2,1)}, bf16[32,7296]{1,0:T(8,128)(2,1)S(1)}, u32[]{:S(2)}) copy-start(bf16[32,7296]{1,0:T(8,128)(2,1)S(1)} %collective-permute-done.8.refs_4_.refs_8_.refs_3_) | copy-start | bytes 1400836
  42.8 8.3 %collective-permute-start.13 = (bf16[128,7168]{1,0:T(8,128)(2,1)}, bf16[128,7168]{1,0:T(8,128)(2,1)S(1)}, u32[]{:S(2)}, u32[]{:S(2)}) collective-permute-start(bf16[128,7168]{1,0:T(8,128)(2,1)} %get-tuple-element.38), channel_id=1, source_target_pairs={{0,16},{16,0},{32,48},{48,32},{64,80},{80,64},{96,112},{112,96},{1... | collective-permute-start | bytes 5505032 | tf_op jit(solution)/shard_map/tok_route/ppermute | solution.py:55
  42.8 5.4 %copy-start.28 = (bf16[32,7168]{1,0:T(8,128)(2,1)S(1)}, bf16[32,7168]{1,0:T(8,128)(2,1)}, u32[]{:S(2)}) copy-start(bf16[32,7168]{1,0:T(8,128)(2,1)} %get-tuple-element.36) | copy-start | bytes 1376260
  42.9 7.2 %copy-start.27 = (bf16[32,7168]{1,0:T(8,128)(2,1)S(1)}, bf16[32,7168]{1,0:T(8,128)(2,1)}, u32[]{:S(2)}) copy-start(bf16[32,7168]{1,0:T(8,128)(2,1)} %get-tuple-element.37) | copy-start | bytes 1376260
  42.9 59.5 %all-to-all-start = ((bf16[16,16,7168]{2,1,0:T(8,128)(2,1)}), bf16[16,16,7168]{2,1,0:T(8,128)(2,1)}, u32[]{:S(2)}, u32[]{:S(2)}) async-start(bf16[16,16,7168]{2,1,0:T(8,128)(2,1)} %bitcast.13), calls=%async_computation | async-start | bytes 7340032 | tf_op jit(solution)/shard_map/cot_route/all_to_all | solution.py:395
  47.5 34.0 %collective-permute-start.10 = (bf16[32,7168]{1,0:T(8,128)(2,1)}, bf16[32,7168]{1,0:T(8,128)(2,1)S(1)}, u32[]{:S(2)}, u32[]{:S(2)}) collective-permute-start(bf16[32,7168]{1,0:T(8,128)(2,1)} %get-tuple-element.35), channel_id=1, source_target_pairs={{0,32},{16,48},{32,64},{48,80},{64,96},{80,112},{96,0},{112,16},{1... | collective-permute-start | bytes 1376264 | tf_op jit(solution)/shard_map/tok_route/ppermute | solution.py:47
  48.3 36.9 %collective-permute-start.11 = (bf16[32,7168]{1,0:T(8,128)(2,1)S(1)}, bf16[32,7168]{1,0:T(8,128)(2,1)S(1)}, u32[]{:S(2)}, u32[]{:S(2)}) collective-permute-start(bf16[32,7168]{1,0:T(8,128)(2,1)S(1)} %copy-done.28), channel_id=1, source_target_pairs={{0,64},{16,80},{32,96},{48,112},{64,0},{80,16},{96,32},{112,48},{1... | collective-permute-start | bytes 1376264 | tf_op jit(solution)/shard_map/tok_route/ppermute | solution.py:47
  50.1 35.0 %collective-permute-start.12 = (bf16[32,7168]{1,0:T(8,128)(2,1)S(1)}, bf16[32,7168]{1,0:T(8,128)(2,1)S(1)}, u32[]{:S(2)}, u32[]{:S(2)}) collective-permute-start(bf16[32,7168]{1,0:T(8,128)(2,1)S(1)} %copy-done.27), channel_id=1, source_target_pairs={{0,96},{16,112},{32,0},{48,16},{64,32},{80,48},{96,64},{112,80},{1... | collective-permute-start | bytes 1376264 | tf_op jit(solution)/shard_map/tok_route/ppermute | solution.py:47
  52.3 32.8 %collective-permute-start.16 = (bf16[32,7168]{1,0:T(8,128)(2,1)}, bf16[32,7168]{1,0:T(8,128)(2,1)S(1)}, u32[]{:S(2)}, u32[]{:S(2)}) collective-permute-start(bf16[32,7168]{1,0:T(8,128)(2,1)} %get-tuple-element.71), channel_id=1, source_target_pairs={{0,96},{16,112},{32,0},{48,16},{64,32},{80,48},{96,64},{112,80},{1... | collective-permute-start | bytes 1376264 | tf_op jit(solution)/shard_map/tok_route/ppermute | solution.py:47
  53.6 31.5 %collective-permute-start.15 = (bf16[32,7168]{1,0:T(8,128)(2,1)}, bf16[32,7168]{1,0:T(8,128)(2,1)S(1)}, u32[]{:S(2)}, u32[]{:S(2)}) collective-permute-start(bf16[32,7168]{1,0:T(8,128)(2,1)} %get-tuple-element.72), channel_id=1, source_target_pairs={{0,64},{16,80},{32,96},{48,112},{64,0},{80,16},{96,32},{112,48},{1... | collective-permute-start | bytes 1376264 | tf_op jit(solution)/shard_map/tok_route/ppermute | solution.py:47
  81.6 13.4 %copy-start.7 = (bf16[32,7168]{1,0:T(8,128)(2,1)}, bf16[32,7168]{1,0:T(8,128)(2,1)S(1)}, u32[]{:S(2)}) copy-start(bf16[32,7168]{1,0:T(8,128)(2,1)S(1)} %collective-permute-done.10.refs_0_.refs_1_) | copy-start | bytes 1376260
  81.6 13.4 %collective-permute-start.14 = (bf16[32,7168]{1,0:T(8,128)(2,1)}, bf16[32,7168]{1,0:T(8,128)(2,1)S(1)}, u32[]{:S(2)}, u32[]{:S(2)}) collective-permute-start(bf16[32,7168]{1,0:T(8,128)(2,1)} %get-tuple-element.73), channel_id=1, source_target_pairs={{0,32},{16,48},{32,64},{48,80},{64,96},{80,112},{96,0},{112,16},{1... | collective-permute-start | bytes 1376264 | tf_op jit(solution)/shard_map/tok_route/ppermute | solution.py:47
  85.1 9.9 %copy-start.8 = (bf16[32,7168]{1,0:T(8,128)(2,1)}, bf16[32,7168]{1,0:T(8,128)(2,1)S(1)}, u32[]{:S(2)}) copy-start(bf16[32,7168]{1,0:T(8,128)(2,1)S(1)} %collective-permute-done.11.refs_1_.refs_2_) | copy-start | bytes 1376260
  85.1 9.9 %copy-start.9 = (bf16[32,7168]{1,0:T(8,128)(2,1)}, bf16[32,7168]{1,0:T(8,128)(2,1)S(1)}, u32[]{:S(2)}) copy-start(bf16[32,7168]{1,0:T(8,128)(2,1)S(1)} %collective-permute-done.12.refs_2_.refs_3_) | copy-start | bytes 1376260
  85.2 9.9 %copy-start.10 = (bf16[32,7168]{1,0:T(8,128)(2,1)}, bf16[32,7168]{1,0:T(8,128)(2,1)S(1)}, u32[]{:S(2)}) copy-start(bf16[32,7168]{1,0:T(8,128)(2,1)S(1)} %collective-permute-done.16.refs_5_.refs_7_) | copy-start | bytes 1376260
  85.2 9.8 %copy-start.11 = (bf16[32,7168]{1,0:T(8,128)(2,1)}, bf16[32,7168]{1,0:T(8,128)(2,1)S(1)}, u32[]{:S(2)}) copy-start(bf16[32,7168]{1,0:T(8,128)(2,1)S(1)} %collective-permute-done.15.refs_4_.refs_6_) | copy-start | bytes 1376260
  100.3 27.7 %collective-permute-start.17 = (bf16[32,14336]{1,0:T(8,128)(2,1)}, bf16[32,14336]{1,0:T(8,128)(2,1)S(1)}, u32[]{:S(2)}, u32[]{:S(2)}) collective-permute-start(bf16[32,14336]{1,0:T(8,128)(2,1)} %get-tuple-element.45), channel_id=1, source_target_pairs={{0,3},{1,0},{2,1},{3,2},{4,7},{5,4},{6,5},{7,6},{8,11},{9,8},{10,9... | collective-permute-start | bytes 2752520 | tf_op jit(solution)/shard_map/shared_out/ppermute | solution.py:66
  100.3 27.7 %collective-permute-start.18 = (bf16[32,14336]{1,0:T(8,128)(2,1)}, bf16[32,14336]{1,0:T(8,128)(2,1)}, u32[]{:S(2)}, u32[]{:S(2)}) collective-permute-start(bf16[32,14336]{1,0:T(8,128)(2,1)} %get-tuple-element.46), channel_id=1, source_target_pairs={{0,2},{1,3},{2,0},{3,1},{4,6},{5,7},{6,4},{7,5},{8,10},{9,11},{10,... | collective-permute-start | bytes 2752520 | tf_op jit(solution)/shard_map/shared_out/ppermute | solution.py:66
  100.8 27.2 %collective-permute-start.19 = (bf16[32,14336]{1,0:T(8,128)(2,1)}, bf16[32,14336]{1,0:T(8,128)(2,1)}, u32[]{:S(2)}, u32[]{:S(2)}) collective-permute-start(bf16[32,14336]{1,0:T(8,128)(2,1)} %get-tuple-element.47), channel_id=1, source_target_pairs={{0,1},{1,2},{2,3},{3,0},{4,5},{5,6},{6,7},{7,4},{8,9},{9,10},{10,1... | collective-permute-start | bytes 2752520 | tf_op jit(solution)/shard_map/shared_out/ppermute | solution.py:66
  102.3 25.7 %copy-start.13 = (bf16[32,7168]{1,0:T(8,128)(2,1)S(1)}, bf16[32,7168]{1,0:T(8,128)(2,1)}, u32[]{:S(2)}) copy-start(bf16[32,7168]{1,0:T(8,128)(2,1)} %get-tuple-element.41._) | copy-start | bytes 1376260
  127.9 15.1 %collective-permute-start.23 = (bf16[128,7168]{1,0:T(8,128)(2,1)}, bf16[128,7168]{1,0:T(8,128)(2,1)S(1)}, u32[]{:S(2)}, u32[]{:S(2)}) collective-permute-start(bf16[128,7168]{1,0:T(8,128)(2,1)} %get-tuple-element.52), channel_id=1, source_target_pairs={{0,16},{16,0},{32,48},{48,32},{64,80},{80,64},{96,112},{112,96},{1... | collective-permute-start | bytes 5505032 | tf_op jit(solution)/shard_map/back_route/ppermute | solution.py:55
  128.0 2.7 %copy-start.2 = (bf16[32,14336]{1,0:T(8,128)(2,1)}, bf16[32,14336]{1,0:T(8,128)(2,1)S(1)}, u32[]{:S(2)}) copy-start(bf16[32,14336]{1,0:T(8,128)(2,1)S(1)} %collective-permute-done.17.refs_2_.refs_4_) | copy-start | bytes 2752516
  130.7 55.7 %all-to-all-start.1 = ((bf16[16,16,7168]{2,1,0:T(8,128)(2,1)}), bf16[16,16,7168]{2,1,0:T(8,128)(2,1)}, u32[]{:S(2)}, u32[]{:S(2)}) async-start(bf16[16,16,7168]{2,1,0:T(8,128)(2,1)} %bitcast.8), calls=%async_computation.1 | async-start | bytes 7340032 | tf_op jit(solution)/shard_map/out_route/all_to_all | solution.py:472
  136.7 32.9 %collective-permute-start.20 = (bf16[32,7168]{1,0:T(8,128)(2,1)}, bf16[32,7168]{1,0:T(8,128)(2,1)S(1)}, u32[]{:S(2)}, u32[]{:S(2)}) collective-permute-start(bf16[32,7168]{1,0:T(8,128)(2,1)} %get-tuple-element.49), channel_id=1, source_target_pairs={{0,96},{16,112},{32,0},{48,16},{64,32},{80,48},{96,64},{112,80},{1... | collective-permute-start | bytes 1376264 | tf_op jit(solution)/shard_map/back_route/ppermute | solution.py:47
  139.0 34.3 %collective-permute-start.21 = (bf16[32,7168]{1,0:T(8,128)(2,1)}, bf16[32,7168]{1,0:T(8,128)(2,1)S(1)}, u32[]{:S(2)}, u32[]{:S(2)}) collective-permute-start(bf16[32,7168]{1,0:T(8,128)(2,1)} %get-tuple-element.50), channel_id=1, source_target_pairs={{0,64},{16,80},{32,96},{48,112},{64,0},{80,16},{96,32},{112,48},{1... | collective-permute-start | bytes 1376264 | tf_op jit(solution)/shard_map/back_route/ppermute | solution.py:47
  139.5 33.8 %collective-permute-start.22 = (bf16[32,7168]{1,0:T(8,128)(2,1)}, bf16[32,7168]{1,0:T(8,128)(2,1)S(1)}, u32[]{:S(2)}, u32[]{:S(2)}) collective-permute-start(bf16[32,7168]{1,0:T(8,128)(2,1)} %get-tuple-element.51), channel_id=1, source_target_pairs={{0,32},{16,48},{32,64},{48,80},{64,96},{80,112},{96,0},{112,16},{1... | collective-permute-start | bytes 1376264 | tf_op jit(solution)/shard_map/back_route/ppermute | solution.py:47
  146.5 27.0 %collective-permute-start.26 = (bf16[32,7168]{1,0:T(8,128)(2,1)S(1)}, bf16[32,7168]{1,0:T(8,128)(2,1)S(1)}, u32[]{:S(2)}, u32[]{:S(2)}) collective-permute-start(bf16[32,7168]{1,0:T(8,128)(2,1)S(1)} %get-tuple-element.66), channel_id=1, source_target_pairs={{0,32},{16,48},{32,64},{48,80},{64,96},{80,112},{96,0},{112,16},{1... | collective-permute-start | bytes 1376264 | tf_op jit(solution)/shard_map/back_route/ppermute | solution.py:47
  149.1 33.5 %collective-permute-start.25 = (bf16[32,7168]{1,0:T(8,128)(2,1)S(1)}, bf16[32,7168]{1,0:T(8,128)(2,1)S(1)}, u32[]{:S(2)}, u32[]{:S(2)}) collective-permute-start(bf16[32,7168]{1,0:T(8,128)(2,1)S(1)} %get-tuple-element.67), channel_id=1, source_target_pairs={{0,64},{16,80},{32,96},{48,112},{64,0},{80,16},{96,32},{112,48},{1... | collective-permute-start | bytes 1376264 | tf_op jit(solution)/shard_map/back_route/ppermute | solution.py:47
  169.6 16.8 %copy-start.21 = (bf16[32,7168]{1,0:T(8,128)(2,1)}, bf16[32,7168]{1,0:T(8,128)(2,1)S(1)}, u32[]{:S(2)}) copy-start(bf16[32,7168]{1,0:T(8,128)(2,1)S(1)} %collective-permute-done.20.refs_2_) | copy-start | bytes 1376260
  169.6 13.0 %collective-permute-start.24 = (bf16[32,7168]{1,0:T(8,128)(2,1)S(1)}, bf16[32,7168]{1,0:T(8,128)(2,1)S(1)}, u32[]{:S(2)}, u32[]{:S(2)}) collective-permute-start(bf16[32,7168]{1,0:T(8,128)(2,1)S(1)} %get-tuple-element.68), channel_id=1, source_target_pairs={{0,96},{16,112},{32,0},{48,16},{64,32},{80,48},{96,64},{112,80},{1... | collective-permute-start | bytes 1376264 | tf_op jit(solution)/shard_map/back_route/ppermute | solution.py:47
  173.3 13.0 %copy-start.22 = (bf16[32,7168]{1,0:T(8,128)(2,1)}, bf16[32,7168]{1,0:T(8,128)(2,1)S(1)}, u32[]{:S(2)}) copy-start(bf16[32,7168]{1,0:T(8,128)(2,1)S(1)} %collective-permute-done.21.refs_3_) | copy-start | bytes 1376260
  173.3 9.3 %copy-start.23 = (bf16[32,7168]{1,0:T(8,128)(2,1)}, bf16[32,7168]{1,0:T(8,128)(2,1)S(1)}, u32[]{:S(2)}) copy-start(bf16[32,7168]{1,0:T(8,128)(2,1)S(1)} %collective-permute-done.22.refs_4_) | copy-start | bytes 1376260
  173.5 12.8 %copy-start.24 = (bf16[32,7168]{1,0:T(8,128)(2,1)}, bf16[32,7168]{1,0:T(8,128)(2,1)S(1)}, u32[]{:S(2)}) copy-start(bf16[32,7168]{1,0:T(8,128)(2,1)S(1)} %collective-permute-done.26.refs_8_) | copy-start | bytes 1376260
  182.6 3.8 %copy-start.25 = (bf16[32,7168]{1,0:T(8,128)(2,1)}, bf16[32,7168]{1,0:T(8,128)(2,1)S(1)}, u32[]{:S(2)}) copy-start(bf16[32,7168]{1,0:T(8,128)(2,1)S(1)} %collective-permute-done.25.refs_7_) | copy-start | bytes 1376260
  182.6 3.8 %copy-start.26 = (bf16[32,7168]{1,0:T(8,128)(2,1)}, bf16[32,7168]{1,0:T(8,128)(2,1)S(1)}, u32[]{:S(2)}) copy-start(bf16[32,7168]{1,0:T(8,128)(2,1)S(1)} %collective-permute-done.24.refs_6_) | copy-start | bytes 1376260
  190.7 18.6 %copy-start.14 = (bf16[32,7168]{1,0:T(8,128)(2,1)S(1)}, bf16[32,7168]{1,0:T(8,128)(2,1)}, u32[]{:S(2)}) copy-start(bf16[32,7168]{1,0:T(8,128)(2,1)} %get-tuple-element.56.refs_0_) | copy-start | bytes 1376260
  190.8 14.7 %collective-permute-start.31 = (bf16[32,7168]{1,0:T(8,128)(2,1)}, bf16[32,7168]{1,0:T(8,128)(2,1)S(1)}, u32[]{:S(2)}, u32[]{:S(2)}) collective-permute-start(bf16[32,7168]{1,0:T(8,128)(2,1)} %get-tuple-element.59), channel_id=1, source_target_pairs={{0,3},{1,0},{2,1},{3,2},{4,7},{5,4},{6,5},{7,6},{8,11},{9,8},{10,9... | collective-permute-start | bytes 1376264 | tf_op jit(solution)/shard_map/back_route/ppermute | solution.py:66
  194.2 11.2 %collective-permute-start.32 = (bf16[32,7168]{1,0:T(8,128)(2,1)}, bf16[32,7168]{1,0:T(8,128)(2,1)S(1)}, u32[]{:S(2)}, u32[]{:S(2)}) collective-permute-start(bf16[32,7168]{1,0:T(8,128)(2,1)} %get-tuple-element.60), channel_id=1, source_target_pairs={{0,2},{1,3},{2,0},{3,1},{4,6},{5,7},{6,4},{7,5},{8,10},{9,11},{10,... | collective-permute-start | bytes 1376264 | tf_op jit(solution)/shard_map/back_route/ppermute | solution.py:66
  195.1 14.2 %collective-permute-start.33 = (bf16[32,7168]{1,0:T(8,128)(2,1)}, bf16[32,7168]{1,0:T(8,128)(2,1)S(1)}, u32[]{:S(2)}, u32[]{:S(2)}) collective-permute-start(bf16[32,7168]{1,0:T(8,128)(2,1)} %get-tuple-element.61), channel_id=1, source_target_pairs={{0,1},{1,2},{2,3},{3,0},{4,5},{5,6},{6,7},{7,4},{8,9},{9,10},{10,1... | collective-permute-start | bytes 1376264 | tf_op jit(solution)/shard_map/back_route/ppermute | solution.py:66
  199.9 18.2 %copy-start.17 = (f32[32,7168]{1,0:T(8,128)S(1)}, f32[32,7168]{1,0:T(8,128)}, u32[]{:S(2)}) copy-start(f32[32,7168]{1,0:T(8,128)} %get-tuple-element.57) | copy-start | bytes 2752516
  199.9 18.2 %collective-permute-start.27 = (bf16[32,7168]{1,0:T(8,128)(2,1)}, bf16[32,7168]{1,0:T(8,128)(2,1)S(1)}, u32[]{:S(2)}, u32[]{:S(2)}) collective-permute-start(bf16[32,7168]{1,0:T(8,128)(2,1)} %get-tuple-element.58), channel_id=1, source_target_pairs={{0,16},{16,0},{32,48},{48,32},{64,80},{80,64},{96,112},{112,96},{1... | collective-permute-start | bytes 1376264 | tf_op jit(solution)/shard_map/out_sum/ppermute | solution.py:55
  209.6 11.0 %collective-permute-start.34 = (bf16[8,14336]{1,0:T(8,128)(2,1)S(1)}, bf16[8,14336]{1,0:T(8,128)(2,1)S(1)}, u32[]{:S(2)}, u32[]{:S(2)}) collective-permute-start(bf16[8,14336]{1,0:T(8,128)(2,1)S(1)} %get-tuple-element.74), channel_id=1, source_target_pairs={{0,12},{1,13},{2,14},{3,15},{4,0},{5,1},{6,2},{7,3},{8,4},{9,5},{1... | collective-permute-start | bytes 688136 | tf_op jit(solution)/shard_map/back_route/ppermute | solution.py:66
  212.5 9.6 %collective-permute-start.36 = (bf16[8,14336]{1,0:T(8,128)(2,1)S(1)}, bf16[8,14336]{1,0:T(8,128)(2,1)S(1)}, u32[]{:S(2)}, u32[]{:S(2)}) collective-permute-start(bf16[8,14336]{1,0:T(8,128)(2,1)S(1)} %get-tuple-element.75), channel_id=1, source_target_pairs={{0,4},{1,5},{2,6},{3,7},{4,8},{5,9},{6,10},{7,11},{8,12},{9,13},{1... | collective-permute-start | bytes 688136 | tf_op jit(solution)/shard_map/back_route/ppermute | solution.py:66
  212.5 12.1 %collective-permute-start.35 = (bf16[8,14336]{1,0:T(8,128)(2,1)S(1)}, bf16[8,14336]{1,0:T(8,128)(2,1)S(1)}, u32[]{:S(2)}, u32[]{:S(2)}) collective-permute-start(bf16[8,14336]{1,0:T(8,128)(2,1)S(1)} %get-tuple-element.76), channel_id=1, source_target_pairs={{0,8},{1,9},{2,10},{3,11},{4,12},{5,13},{6,14},{7,15},{8,0},{9,1},... | collective-permute-start | bytes 688136 | tf_op jit(solution)/shard_map/back_route/ppermute | solution.py:66
  218.2 7.1 %collective-permute-start.28 = (bf16[8,7168]{1,0:T(8,128)(2,1)S(1)}, bf16[8,7168]{1,0:T(8,128)(2,1)S(1)}, u32[]{:S(2)}, u32[]{:S(2)}) collective-permute-start(bf16[8,7168]{1,0:T(8,128)(2,1)S(1)} %get-tuple-element.77), channel_id=1, source_target_pairs={{0,96},{16,112},{32,0},{48,16},{64,32},{80,48},{96,64},{112,80},{1... | collective-permute-start | bytes 344072 | tf_op jit(solution)/shard_map/out_sum/ppermute | solution.py:47
  220.6 7.2 %collective-permute-start.30 = (bf16[8,7168]{1,0:T(8,128)(2,1)S(1)}, bf16[8,7168]{1,0:T(8,128)(2,1)S(1)}, u32[]{:S(2)}, u32[]{:S(2)}) collective-permute-start(bf16[8,7168]{1,0:T(8,128)(2,1)S(1)} %get-tuple-element.78), channel_id=1, source_target_pairs={{0,32},{16,48},{32,64},{48,80},{64,96},{80,112},{96,0},{112,16},{1... | collective-permute-start | bytes 344072 | tf_op jit(solution)/shard_map/out_sum/ppermute | solution.py:47
  220.6 7.2 %collective-permute-start.29 = (bf16[8,7168]{1,0:T(8,128)(2,1)S(1)}, bf16[8,7168]{1,0:T(8,128)(2,1)S(1)}, u32[]{:S(2)}, u32[]{:S(2)}) collective-permute-start(bf16[8,7168]{1,0:T(8,128)(2,1)S(1)} %get-tuple-element.79), channel_id=1, source_target_pairs={{0,64},{16,80},{32,96},{48,112},{64,0},{80,16},{96,32},{112,48},{1... | collective-permute-start | bytes 344072 | tf_op jit(solution)/shard_map/out_sum/ppermute | solution.py:47
  (4 other events, 3.5 us)

commit v5 on v4

--- a/solution.py
+++ b/solution.py
@@ -505,9 +505,6 @@
             2 * 400 * width,
             after=[y_home],
         )
-        line = jnp.concatenate([ring_sum(move_b, parts), s_line], axis=1).astype(BF16).reshape(4, 8, 2 * width)
-        both = ring_sum(move_a, [line[k] for k in range(4)])
-        token_grad, s_out = both[:, :width].astype(BF16), both[:, width:]
     with jax.named_scope("out_sum"):
         mine, other = call(
             out_sum_kernel,
@@ -520,8 +517,16 @@
             after=[parts[0]],
         )
         line = (mine + swap_core(other).astype(F32)).reshape(4, 8, width)
-        line = [line[0]] + [line[k].astype(BF16) for k in (1, 2, 3)]
-        mixed = (ring_sum(move_y, line) + s_out).astype(BF16)
+        home = [move_y(line[k].astype(BF16), -k) for k in (1, 2, 3)]
+        s_line = pass_on(s_line, home)
+    with jax.named_scope("back_sum"):
+        y_sum = line[0]
+        for v in home:
+            y_sum = y_sum + v.astype(F32)
+        line = jnp.concatenate([ring_sum(move_b, parts), s_line], axis=1).astype(BF16).reshape(4, 8, 2 * width)
+        both = ring_sum(move_a, [line[k] for k in range(4)])
+        token_grad, s_out = both[:, :width].astype(BF16), both[:, width:]
+        mixed = (y_sum + s_out).astype(BF16)
     return (mixed, token_grad)
 
 

time: 229 us -> 233 us (1.017)
  other arithmetic: 4.49 us -> 6.93 us
    add x0 -> x1, other arithmetic: none -> 2.59 us  [local(): s_line = s_line + v[:, :width].astype(F32)]
    unnamed x60 -> x72, local copies, waits for them, and re-layouts: 4.49 us -> 5.18 us
  transfers between devices with their start and end apart: 39 -> 39, of which waited for: 16 -> 17; matrix products, arithmetic and copies ran while one was open for 4% -> 4% of each run, Pallas kernels for 19% -> 18%
where the time goes in v5:
time: 233 us; the launch traced here: 232 us
  waiting for transfers between devices  94.6 us (41%)
  starting transfers between devices  64.1 us (28%)
  Pallas kernels  55 us (24%)
  local copies, waits for them, and re-layouts  10.4 us (4%)
  other arithmetic  6.93 us (3%)
    ppermute x16, waiting for transfers between devices, move_y(): lax.ppermute(v, 'grp', [(y * 2 + c, (y + k) % N_Y * 2 + c) for y in range...  65.4 us
    pallas_call x8, Pallas kernels, call(): pl.pallas_call(lambda *refs: kernel(*refs[skip:]), grid=(grid,), in_specs...  29.3 us
    ppermute x16, starting transfers between devices, move_y(): lax.ppermute(v, 'grp', [(y * 2 + c, (y + k) % N_Y * 2 + c) for y in range...  27.2 us
    pallas_call x1, Pallas kernels, local(): pl.pallas_call(expert_kernel, in_specs=[pl.BlockSpec(memory_space=pltpu.S...  25.7 us
    ppermute x15, starting transfers between devices, move_plane(): return lax.ppermute(v, ('grp', 'exp'), pairs)  25.3 us
    ppermute x15, waiting for transfers between devices, move_plane(): return lax.ppermute(v, ('grp', 'exp'), pairs)  24.4 us
    all_to_all x1, starting transfers between devices, local(): lax.all_to_all(y_rows.reshape(16, 16, width), 'exp', split_axis=0, concat...  6.11 us
    unnamed x72, local copies, waits for them, and re-layouts  5.18 us
  transfers between devices with their start and end apart: 39, of which 17 were waited for; matrix products, arithmetic and copies ran while one was open for 4% of the time, Pallas kernels for 18%

profile of v5, /device:TPU:0, one launch (start us, length us, event | category | flops | bytes accessed | tf_op | source)
XLA Modules:
  0.0 232.3 jit_solution(10500752931027815910)
XLA Ops:
  0.6 1.8 widen.1
  2.5 3.3 %collective-permute-start.2 = (bf16[8,7296]{1,0:T(8,128)(2,1)}, bf16[8,7296]{1,0:T(8,128)(2,1)S(1)}, u32[]{:S(2)}, u32[]{:S(2)}) collective-permute-start(bf16[8,7296]{1,0:T(8,128)(2,1)} %get-tuple-element.32), channel_id=1, source_target_pairs={{0,64},{16,80},{32,96},{48,112},{64,0},{80,16},{96,32},{112,48},{1... | collective-permute-start | bytes 350216 | tf_op jit(solution)/shard_map/cot_gather/ppermute | solution.py:47
  5.7 2.8 %collective-permute-start.6 = (bf16[8,14464]{1,0:T(8,128)(2,1)}, bf16[8,14464]{1,0:T(8,128)(2,1)S(1)}, u32[]{:S(2)}, u32[]{:S(2)}) collective-permute-start(bf16[8,14464]{1,0:T(8,128)(2,1)} %get-tuple-element.34.refs_8_), channel_id=1, source_target_pairs={{0,12},{1,13},{2,14},{3,15},{4,0},{5,1},{6,2},{7,3},{8,4},{9,5},{1... | collective-permute-start | bytes 694280 | tf_op jit(solution)/shard_map/gather_line/ppermute | solution.py:66
  8.5 0.8 collective-permute-start.5
  9.3 0.9 collective-permute-start.4
  10.2 0.9 constant_dynamic-update-slice_fusion.1
  11.1 0.9 slice.87
  12.0 0.7 collective-permute-start.1
  12.8 2.1 collective-permute-done.6.refs_11_
  14.9 1.5 collective-permute-done.5.refs_10_
  16.4 2.4 %collective-permute-done.4.refs_9_ = bf16[8,14464]{1,0:T(8,128)(2,1)S(1)} collective-permute-done((bf16[8,14464]{1,0:T(8,128)(2,1)}, bf16[8,14464]{1,0:T(8,128)(2,1)S(1)}, u32[]{:S(2)}, u32[]{:S(2)}) %collective-permute-start.4) | collective-permute-done | bytes 231456 | tf_op jit(solution)/shard_map/gather_line/ppermute | solution.py:66
  18.8 4.1 %collective-permute-start.9 = (bf16[32,7296]{1,0:T(8,128)(2,1)S(1)}, bf16[32,7296]{1,0:T(8,128)(2,1)S(1)}, u32[]{:S(2)}, u32[]{:S(2)}) collective-permute-start(bf16[32,7296]{1,0:T(8,128)(2,1)S(1)} %pad_maximum_fusion.refs_2_.refs_6_.refs_1_), channel_id=1, source_target_pairs={{0,3},{1,0},{2,1},{3,2},{4,7},{5,4},{6,5},{7,6},{8,11},{9,8},{10,9... | collective-permute-start | bytes 1400840 | tf_op jit(solution)/shard_map/gather_plane/ppermute | solution.py:66
  22.9 1.3 collective-permute-start.7
  25.0 1.0 collective-permute-done.3.refs_3_.refs_6_
  26.0 0.7 copy-done.16
  26.8 4.2 %cot_pick.1 = (bf16[256,7168]{1,0:T(8,128)(2,1)}, bf16[256,64]{1,0:T(8,128)(2,1)}) custom-call(s32[2]{0:T(128)} %pad_add_fusion.refs_0_.refs_1_.at, bf16[16,7296]{1,0:T(8,128)(2,1)} %copy-done.15, bf16[24,7296]{1,0:T(8,128)(2,1)} %copy-done.6, bf16[24,7296]{1,0:T(8,128)(2,1)} %copy-done.16, bf16[16,7296]{1,0:T(8,128)(2,1)} %copy-done.15, ...), custom_call_target="tpu_custom_call" | custom-call | flops 234881024 | bytes 4587520 | tf_op jit(solution)/shard_map/cot_pick/pallas_call | solution.py:93
  31.0 3.0 %collective-permute-done.9.refs_5_.refs_9_.refs_4_ = bf16[32,7296]{1,0:T(8,128)(2,1)S(1)} collective-permute-done((bf16[32,7296]{1,0:T(8,128)(2,1)S(1)}, bf16[32,7296]{1,0:T(8,128)(2,1)S(1)}, u32[]{:S(2)}, u32[]{:S(2)}) %collective-permute-start.9) | collective-permute-done | bytes 466976 | tf_op jit(solution)/shard_map/gather_plane/ppermute | solution.py:66
  34.0 3.7 %collective-permute-done.7.refs_3_.refs_7_.refs_2_ = bf16[32,7296]{1,0:T(8,128)(2,1)S(1)} collective-permute-done((bf16[32,7296]{1,0:T(8,128)(2,1)S(1)}, bf16[32,7296]{1,0:T(8,128)(2,1)S(1)}, u32[]{:S(2)}, u32[]{:S(2)}) %collective-permute-start.7) | collective-permute-done | bytes 466976 | tf_op jit(solution)/shard_map/gather_plane/ppermute | solution.py:66
  37.7 0.8 copy-done.5
  38.5 4.3 %tok_pick.1 = (bf16[32,7168]{1,0:T(8,128)(2,1)}, bf16[32,7168]{1,0:T(8,128)(2,1)}, bf16[32,7168]{1,0:T(8,128)(2,1)}, bf16[32,7168]{1,0:T(8,128)(2,1)}, bf16[128,...) custom-call(bf16[256,64]{1,0:T(8,128)(2,1)} %get-tuple-element.33.refs_0_.refs_2_, s32[2]{0:T(128)} %pad_add_fusion.refs_0_.refs_1_.at, ...), custom_call_target="tpu_custom_call" | custom-call | flops 469762048 | bytes 5734400 | tf_op jit(solution)/shard_map/tok_pick/pallas_call | solution.py:93
  42.9 4.5 %all-to-all-start = ((bf16[16,16,7168]{2,1,0:T(8,128)(2,1)}), bf16[16,16,7168]{2,1,0:T(8,128)(2,1)}, u32[]{:S(2)}, u32[]{:S(2)}) async-start(bf16[16,16,7168]{2,1,0:T(8,128)(2,1)} %bitcast.13), calls=%async_computation | async-start | bytes 7340032 | tf_op jit(solution)/shard_map/cot_route/all_to_all | solution.py:395
  47.4 0.7 collective-permute-start.10
  48.2 1.8 collective-permute-start.11
  50.0 0.9 collective-permute-start.12
  50.9 1.3 fusion.8
  52.2 1.3 collective-permute-start.16
  53.5 1.8 collective-permute-start.15
  55.3 26.1 %collective-permute-done.10.refs_0_.refs_1_ = bf16[32,7168]{1,0:T(8,128)(2,1)S(1)} collective-permute-done((bf16[32,7168]{1,0:T(8,128)(2,1)}, bf16[32,7168]{1,0:T(8,128)(2,1)S(1)}, u32[]{:S(2)}, u32[]{:S(2)}) %collective-permute-start.10) | collective-permute-done | bytes 458784 | tf_op jit(solution)/shard_map/tok_route/ppermute | solution.py:47
  81.5 3.5 %shared.1 = (bf16[128,64]{1,0:T(8,128)(2,1)}, f32[128,64]{1,0:T(8,128)}, f32[128,64]{1,0:T(8,128)}) custom-call(bf16[256,128]{1,0:T(8,128)(2,1)} %get-tuple-element.39.refs_0_.refs_9_, bf16[32,7296]{1,0:T(8,128)(2,1)} %copy-done, bf16[32,7296]{1,0:T(8,128)(2,1)} %copy-done.5, bf16[32,7296]{1,0:T(8,128)(2,1)} %copy-done.4, bf16[32,7296]{1,0:T(8,128)(2,1)} %copy-done.3, ...), custom_call_target="tpu_custom_call" | custom-call | flops 234881024 | bytes 3670016 | tf_op jit(solution)/shard_map/shared/pallas_call | solution.py:93
  85.1 9.9 %collective-permute-done.14.refs_3_.refs_5_ = bf16[32,7168]{1,0:T(8,128)(2,1)S(1)} collective-permute-done((bf16[32,7168]{1,0:T(8,128)(2,1)}, bf16[32,7168]{1,0:T(8,128)(2,1)S(1)}, u32[]{:S(2)}, u32[]{:S(2)}) %collective-permute-start.14) | collective-permute-done | bytes 458784 | tf_op jit(solution)/shard_map/tok_route/ppermute | solution.py:47
  95.0 0.8 copy-done.12
  95.8 4.4 %shared_out.1 = (bf16[32,7168]{1,0:T(8,128)(2,1)}, bf16[32,7168]{1,0:T(8,128)(2,1)}, bf16[32,14336]{1,0:T(8,128)(2,1)}, bf16[32,14336]{1,0:T(8,128)(2,1)}, bf16[32,14336]{1,0:T(8,128)(2,1)}) custom-call(bf16[32,7168]{1,0:T(8,128)(2,1)} %copy-done.7, bf16[32,7168]{1,0:T(8,128)(2,1)} %copy-done.8, bf16[32,7168]{1,0:T(8,128)(2,1)} %copy-done.9, ...), custom_call_target="tpu_custom_call" | custom-call | flops 117440512 | bytes 2752512 | tf_op jit(solution)/shard_map/shared_out/pallas_call | solution.py:93
  100.6 1.6 collective-permute-start.19
  102.3 25.7 %expert.1 = (bf16[32,7168]{1,0:T(8,128)(2,1)}, bf16[32,7168]{1,0:T(8,128)(2,1)}, bf16[32,7168]{1,0:T(8,128)(2,1)}, bf16[32,7168]{1,0:T(8,128)(2,1)}, bf16[128,71...) custom-call(s32[2]{0:T(128)} %pad_add_fusion.refs_0_.refs_1_.at, bf16[32,7168]{1,0:T(8,128)(2,1)} %get-tuple-element.41._, ...), custom_call_target="tpu_custom_call" | custom-call | tf_op jit(solution)/shard_map/expert/pallas_call | solution.py:450
  128.1 2.6 %convert_add_fusion.1.refs_1_.refs_0_ = f32[32,7168]{1,0:T(8,128)} fusion(bf16[32,7168]{1,0:T(8,128)(2,1)S(1)} %copy-done.13, bf16[32,14336]{1,0:T(8,128)(2,1)} %collective-permute-done.19.refs_4_.refs_2_, bf16[32,14336]{1,0:T(8,128)(2,1)} %collective-permute-done.18.refs_3_, bf16[32,14336]{1,0:T(8,128)(2,1)S(1)} %collective-permute-done.17.refs_2_.refs_4_), kind=kLoop, calls=%fused_computation.8 | loop fusion | flops 1605632 | bytes 2752512 | tf_op jit(solution)/shard_map/shared_out/add | solution.py:445
  130.7 6.1 %all-to-all-start.1 = ((bf16[16,16,7168]{2,1,0:T(8,128)(2,1)}), bf16[16,16,7168]{2,1,0:T(8,128)(2,1)}, u32[]{:S(2)}, u32[]{:S(2)}) async-start(bf16[16,16,7168]{2,1,0:T(8,128)(2,1)} %bitcast.8), calls=%async_computation.1 | async-start | bytes 7340032 | tf_op jit(solution)/shard_map/out_route/all_to_all | solution.py:472
  136.8 2.3 collective-permute-start.20
  140.0 3.1 %back_route.3.refs_1_.refs_10_ = bf16[128,128]{1,0:T(8,128)(2,1)} custom-call(bf16[256,7168]{1,0:T(8,128)(2,1)} %out_route.1.refs_0_, bf16[32,7168]{1,0:T(8,128)(2,1)} %get-tuple-element.53.refs_1_, bf16[32,14336]{1,0:T(8,128)(2,1)} %collective-permute-done.19.refs_4_.refs_2_, bf16[32,14336]{1,0:T(8,128)(2,1)} %collective-permute-done.18.refs_3_, ...), custom_call_target="tpu_custom_call" | custom-call | flops 117440512 | bytes 2867200 | tf_op jit(solution)/shard_map/back_route/pallas_call | solution.py:93
  143.1 1.2 copy-done.1
  144.3 2.3 %fusion.7 = (bf16[32,7168]{1,0:T(8,128)(2,1)S(1)}, bf16[32,7168]{1,0:T(8,128)(2,1)S(1)}, bf16[32,7168]{1,0:T(8,128)(2,1)S(1)}, bf16[32,7168]{1,0:T(8,128)(2,1)}) fusion(bf16[128,7168]{1,0:T(8,128)(2,1)} %back_route.4), kind=kLoop, calls=%fused_computation.27 | loop fusion | bytes 3670016 | tf_op jit(solution)/shard_map/back_route/slice | solution.py:490
  146.7 2.5 %collective-permute-start.26 = (bf16[32,7168]{1,0:T(8,128)(2,1)S(1)}, bf16[32,7168]{1,0:T(8,128)(2,1)S(1)}, u32[]{:S(2)}, u32[]{:S(2)}) collective-permute-start(bf16[32,7168]{1,0:T(8,128)(2,1)S(1)} %get-tuple-element.64), channel_id=1, source_target_pairs={{0,32},{16,48},{32,64},{48,80},{64,96},{80,112},{96,0},{112,16},{1... | collective-permute-start | bytes 1376264 | tf_op jit(solution)/shard_map/back_route/ppermute | solution.py:47
  149.2 1.7 collective-permute-start.25
  151.0 18.7 %collective-permute-done.20.refs_2_ = bf16[32,7168]{1,0:T(8,128)(2,1)S(1)} collective-permute-done((bf16[32,7168]{1,0:T(8,128)(2,1)}, bf16[32,7168]{1,0:T(8,128)(2,1)S(1)}, u32[]{:S(2)}, u32[]{:S(2)}) %collective-permute-start.20) | collective-permute-done | bytes 458784 | tf_op jit(solution)/shard_map/back_route/ppermute | solution.py:47
  169.7 3.7 %collective-permute-start.24 = (bf16[32,7168]{1,0:T(8,128)(2,1)S(1)}, bf16[32,7168]{1,0:T(8,128)(2,1)S(1)}, u32[]{:S(2)}, u32[]{:S(2)}) collective-permute-start(bf16[32,7168]{1,0:T(8,128)(2,1)S(1)} %get-tuple-element.66), channel_id=1, source_target_pairs={{0,96},{16,112},{32,0},{48,16},{64,32},{80,48},{96,64},{112,80},{1... | collective-permute-start | bytes 1376264 | tf_op jit(solution)/shard_map/back_route/ppermute | solution.py:47
  173.7 9.0 %collective-permute-done.25.refs_7_ = bf16[32,7168]{1,0:T(8,128)(2,1)S(1)} collective-permute-done((bf16[32,7168]{1,0:T(8,128)(2,1)S(1)}, bf16[32,7168]{1,0:T(8,128)(2,1)S(1)}, u32[]{:S(2)}, u32[]{:S(2)}) %collective-permute-start.25) | collective-permute-done | bytes 458784 | tf_op jit(solution)/shard_map/back_route/ppermute | solution.py:47
  182.7 3.8 %all-to-all-done.1 = bf16[16,16,7168]{2,1,0:T(8,128)(2,1)} async-done(((bf16[16,16,7168]{2,1,0:T(8,128)(2,1)}), bf16[16,16,7168]{2,1,0:T(8,128)(2,1)}, u32[]{:S(2)}, u32[]{:S(2)}) %all-to-all-start.1) | async-done | bytes 3670048 | tf_op jit(solution)/shard_map/out_route/all_to_all | solution.py:472
  186.5 4.4 %back_route.5 = (bf16[32,7168]{1,0:T(8,128)(2,1)}, bf16[32,7168]{1,0:T(8,128)(2,1)}, bf16[32,7168]{1,0:T(8,128)(2,1)}, bf16[32,7168]{1,0:T(8,128)(2,1)}) custom-call(bf16[256,7168]{1,0:T(8,128)(2,1)} %bitcast.7.refs_0_.refs_1_, bf16[32,7168]{1,0:T(8,128)(2,1)} %get-tuple-element.48.refs_1_, bf16[32,7168]{1,0:T(8,128)(2,1)} %copy-done.26, ...), custom_call_target="tpu_custom_call" | custom-call | flops 469762048 | bytes 5734400 | tf_op jit(solution)/shard_map/back_route/pallas_call | solution.py:93
  191.0 3.5 %out_sum.2 = (f32[32,7168]{1,0:T(8,128)}, bf16[32,7168]{1,0:T(8,128)(2,1)}) custom-call(bf16[32,7168]{1,0:T(8,128)(2,1)} %get-tuple-element.56.refs_0_, bf16[256,7168]{1,0:T(8,128)(2,1)} %bitcast.7.refs_0_.refs_1_, bf16[256,64]{1,0:T(8,128)(2,1)} %get-tuple-element.33.refs_0_.refs_2_), custom_call_target="tpu_custom_call" | custom-call | flops 234881024 | bytes 5046272 | tf_op jit(solution)/shard_map/out_sum/pallas_call | solution.py:93
  194.5 3.4 %collective-permute-start.31 = (bf16[32,7168]{1,0:T(8,128)(2,1)S(1)}, bf16[32,7168]{1,0:T(8,128)(2,1)S(1)}, u32[]{:S(2)}, u32[]{:S(2)}) collective-permute-start(bf16[32,7168]{1,0:T(8,128)(2,1)S(1)} %copy-done.34), channel_id=1, source_target_pairs={{0,3},{1,0},{2,1},{3,2},{4,7},{5,4},{6,5},{7,6},{8,11},{9,8},{10,9... | collective-permute-start | bytes 1376264 | tf_op jit(solution)/shard_map/back_sum/ppermute | solution.py:66
  197.9 1.0 collective-permute-start.32
  198.9 1.3 collective-permute-start.33
  200.2 1.3 fusion.6
  201.5 0.8 collective-permute-start.30
  202.3 3.0 %collective-permute-start.29 = (bf16[8,7168]{1,0:T(8,128)(2,1)S(1)}, bf16[8,7168]{1,0:T(8,128)(2,1)S(1)}, u32[]{:S(2)}, u32[]{:S(2)}) collective-permute-start(bf16[8,7168]{1,0:T(8,128)(2,1)S(1)} %get-tuple-element.76), channel_id=1, source_target_pairs={{0,64},{16,80},{32,96},{48,112},{64,0},{80,16},{96,32},{112,48},{1... | collective-permute-start | bytes 344072 | tf_op jit(solution)/shard_map/out_sum/ppermute | solution.py:47
  205.3 3.6 %collective-permute-done.31 = bf16[32,7168]{1,0:T(8,128)(2,1)S(1)} collective-permute-done((bf16[32,7168]{1,0:T(8,128)(2,1)S(1)}, bf16[32,7168]{1,0:T(8,128)(2,1)S(1)}, u32[]{:S(2)}, u32[]{:S(2)}) %collective-permute-start.31) | collective-permute-done | bytes 458784 | tf_op jit(solution)/shard_map/back_sum/ppermute | solution.py:66
  208.9 2.2 collective-permute-start.28
  211.1 1.8 collective-permute-done.33
  213.1 1.4 collective-permute-done.28.refs_1_
  215.2 1.3 convert.16
  216.5 2.2 collective-permute-start.34
  218.7 5.6 %collective-permute-start.35 = (bf16[8,14336]{1,0:T(8,128)(2,1)S(1)}, bf16[8,14336]{1,0:T(8,128)(2,1)S(1)}, u32[]{:S(2)}, u32[]{:S(2)}) collective-permute-start(bf16[8,14336]{1,0:T(8,128)(2,1)S(1)} %get-tuple-element.74), channel_id=1, source_target_pairs={{0,8},{1,9},{2,10},{3,11},{4,12},{5,13},{6,14},{7,15},{8,0},{9,1},... | collective-permute-start | bytes 688136 | tf_op jit(solution)/shard_map/back_sum/ppermute | solution.py:66
  224.3 2.5 %collective-permute-done.36 = bf16[8,14336]{1,0:T(8,128)(2,1)S(1)} collective-permute-done((bf16[8,14336]{1,0:T(8,128)(2,1)S(1)}, bf16[8,14336]{1,0:T(8,128)(2,1)S(1)}, u32[]{:S(2)}, u32[]{:S(2)}) %collective-permute-start.36) | collective-permute-done | bytes 229408 | tf_op jit(solution)/shard_map/back_sum/ppermute | solution.py:66
  226.8 3.9 %collective-permute-done.35 = bf16[8,14336]{1,0:T(8,128)(2,1)S(1)} collective-permute-done((bf16[8,14336]{1,0:T(8,128)(2,1)S(1)}, bf16[8,14336]{1,0:T(8,128)(2,1)S(1)}, u32[]{:S(2)}, u32[]{:S(2)}) %collective-permute-start.35) | collective-permute-done | bytes 229408 | tf_op jit(solution)/shard_map/back_sum/ppermute | solution.py:66
  231.6 0.7 fusion.3
  (117 shorter events, 4.6 us)
Async XLA Ops:
  2.5 21.7 %collective-permute-start.2 = (bf16[8,7296]{1,0:T(8,128)(2,1)}, bf16[8,7296]{1,0:T(8,128)(2,1)S(1)}, u32[]{:S(2)}, u32[]{:S(2)}) collective-permute-start(bf16[8,7296]{1,0:T(8,128)(2,1)} %get-tuple-element.32), channel_id=1, source_target_pairs={{0,64},{16,80},{32,96},{48,112},{64,0},{80,16},{96,32},{112,48},{1... | collective-permute-start | bytes 350216 | tf_op jit(solution)/shard_map/cot_gather/ppermute | solution.py:47
  5.7 6.3 %collective-permute-start = (bf16[8,7296]{1,0:T(8,128)(2,1)}, bf16[8,7296]{1,0:T(8,128)(2,1)S(1)}, u32[]{:S(2)}, u32[]{:S(2)}) collective-permute-start(bf16[8,7296]{1,0:T(8,128)(2,1)} %get-tuple-element.32), channel_id=1, source_target_pairs={{0,16},{16,0},{32,48},{48,32},{64,80},{80,64},{96,112},{112,96},{1... | collective-permute-start | bytes 350216 | tf_op jit(solution)/shard_map/cot_gather/ppermute | solution.py:55
  5.7 9.1 %collective-permute-start.6 = (bf16[8,14464]{1,0:T(8,128)(2,1)}, bf16[8,14464]{1,0:T(8,128)(2,1)S(1)}, u32[]{:S(2)}, u32[]{:S(2)}) collective-permute-start(bf16[8,14464]{1,0:T(8,128)(2,1)} %get-tuple-element.34.refs_8_), channel_id=1, source_target_pairs={{0,12},{1,13},{2,14},{3,15},{4,0},{5,1},{6,2},{7,3},{8,4},{9,5},{1... | collective-permute-start | bytes 694280 | tf_op jit(solution)/shard_map/gather_line/ppermute | solution.py:66
  8.5 7.9 %collective-permute-start.5 = (bf16[8,14464]{1,0:T(8,128)(2,1)}, bf16[8,14464]{1,0:T(8,128)(2,1)S(1)}, u32[]{:S(2)}, u32[]{:S(2)}) collective-permute-start(bf16[8,14464]{1,0:T(8,128)(2,1)} %get-tuple-element.34.refs_8_), channel_id=1, source_target_pairs={{0,8},{1,9},{2,10},{3,11},{4,12},{5,13},{6,14},{7,15},{8,0},{9,1},... | collective-permute-start | bytes 694280 | tf_op jit(solution)/shard_map/gather_line/ppermute | solution.py:66
  9.3 9.4 %collective-permute-start.4 = (bf16[8,14464]{1,0:T(8,128)(2,1)}, bf16[8,14464]{1,0:T(8,128)(2,1)S(1)}, u32[]{:S(2)}, u32[]{:S(2)}) collective-permute-start(bf16[8,14464]{1,0:T(8,128)(2,1)} %get-tuple-element.34.refs_8_), channel_id=1, source_target_pairs={{0,4},{1,5},{2,6},{3,7},{4,8},{5,9},{6,10},{7,11},{8,12},{9,13},{1... | collective-permute-start | bytes 694280 | tf_op jit(solution)/shard_map/gather_line/ppermute | solution.py:66
  12.0 14.0 %copy-start.15 = (bf16[16,7296]{1,0:T(8,128)(2,1)}, bf16[16,7296]{1,0:T(8,128)(2,1)S(1)}, u32[]{:S(2)}) copy-start(bf16[16,7296]{1,0:T(8,128)(2,1)S(1)} %constant_dynamic-update-slice_fusion.refs_1_.refs_4_) | copy-start | bytes 700420
  12.0 12.1 %collective-permute-start.1 = (bf16[16,7296]{1,0:T(8,128)(2,1)S(1)}, bf16[16,7296]{1,0:T(8,128)(2,1)S(1)}, u32[]{:S(2)}, u32[]{:S(2)}) collective-permute-start(bf16[16,7296]{1,0:T(8,128)(2,1)S(1)} %constant_dynamic-update-slice_fusion.refs_1_.refs_4_), channel_id=1, source_target_pairs={{0,32},{16,112},{32,64},{48,16},{64,96},{80,48},{96,0},{112,80},{1... | collective-permute-start | bytes 700424 | tf_op jit(solution)/shard_map/cot_gather/ppermute | solution.py:51
  14.9 27.9 %copy-start.17 = (bf16[8,14464]{1,0:T(8,128)(2,1)}, bf16[8,14464]{1,0:T(8,128)(2,1)S(1)}, u32[]{:S(2)}) copy-start(bf16[8,14464]{1,0:T(8,128)(2,1)S(1)} %collective-permute-done.6.refs_11_) | copy-start | bytes 694276
  16.4 7.8 %copy-start.18 = (bf16[8,14464]{1,0:T(8,128)(2,1)}, bf16[8,14464]{1,0:T(8,128)(2,1)S(1)}, u32[]{:S(2)}) copy-start(bf16[8,14464]{1,0:T(8,128)(2,1)S(1)} %collective-permute-done.5.refs_10_) | copy-start | bytes 694276
  18.7 5.5 %copy-start.19 = (bf16[8,14464]{1,0:T(8,128)(2,1)}, bf16[8,14464]{1,0:T(8,128)(2,1)S(1)}, u32[]{:S(2)}) copy-start(bf16[8,14464]{1,0:T(8,128)(2,1)S(1)} %collective-permute-done.4.refs_9_) | copy-start | bytes 694276
  18.8 18.9 %copy-start = (bf16[32,7296]{1,0:T(8,128)(2,1)}, bf16[32,7296]{1,0:T(8,128)(2,1)S(1)}, u32[]{:S(2)}) copy-start(bf16[32,7296]{1,0:T(8,128)(2,1)S(1)} %pad_maximum_fusion.refs_2_.refs_6_.refs_1_) | copy-start | bytes 1400836
  18.8 15.2 %collective-permute-start.9 = (bf16[32,7296]{1,0:T(8,128)(2,1)S(1)}, bf16[32,7296]{1,0:T(8,128)(2,1)S(1)}, u32[]{:S(2)}, u32[]{:S(2)}) collective-permute-start(bf16[32,7296]{1,0:T(8,128)(2,1)S(1)} %pad_maximum_fusion.refs_2_.refs_6_.refs_1_), channel_id=1, source_target_pairs={{0,3},{1,0},{2,1},{3,2},{4,7},{5,4},{6,5},{7,6},{8,11},{9,8},{10,9... | collective-permute-start | bytes 1400840 | tf_op jit(solution)/shard_map/gather_plane/ppermute | solution.py:66
  22.9 11.1 %collective-permute-start.8 = (bf16[32,7296]{1,0:T(8,128)(2,1)S(1)}, bf16[32,7296]{1,0:T(8,128)(2,1)S(1)}, u32[]{:S(2)}, u32[]{:S(2)}) collective-permute-start(bf16[32,7296]{1,0:T(8,128)(2,1)S(1)} %pad_maximum_fusion.refs_2_.refs_6_.refs_1_), channel_id=1, source_target_pairs={{0,2},{1,3},{2,0},{3,1},{4,6},{5,7},{6,4},{7,5},{8,10},{9,11},{10,... | collective-permute-start | bytes 1400840 | tf_op jit(solution)/shard_map/gather_plane/ppermute | solution.py:66
  22.9 14.8 %collective-permute-start.7 = (bf16[32,7296]{1,0:T(8,128)(2,1)S(1)}, bf16[32,7296]{1,0:T(8,128)(2,1)S(1)}, u32[]{:S(2)}, u32[]{:S(2)}) collective-permute-start(bf16[32,7296]{1,0:T(8,128)(2,1)S(1)} %pad_maximum_fusion.refs_2_.refs_6_.refs_1_), channel_id=1, source_target_pairs={{0,1},{1,2},{2,3},{3,0},{4,5},{5,6},{6,7},{7,4},{8,9},{9,10},{10,1... | collective-permute-start | bytes 1400840 | tf_op jit(solution)/shard_map/gather_plane/ppermute | solution.py:66
  24.3 1.7 collective-permute-start.3
  34.0 3.7 %copy-start.3 = (bf16[32,7296]{1,0:T(8,128)(2,1)}, bf16[32,7296]{1,0:T(8,128)(2,1)S(1)}, u32[]{:S(2)}) copy-start(bf16[32,7296]{1,0:T(8,128)(2,1)S(1)} %collective-permute-done.9.refs_5_.refs_9_.refs_4_) | copy-start | bytes 1400836
  34.0 3.7 %copy-start.4 = (bf16[32,7296]{1,0:T(8,128)(2,1)}, bf16[32,7296]{1,0:T(8,128)(2,1)S(1)}, u32[]{:S(2)}) copy-start(bf16[32,7296]{1,0:T(8,128)(2,1)S(1)} %collective-permute-done.8.refs_4_.refs_8_.refs_3_) | copy-start | bytes 1400836
  42.8 8.1 %collective-permute-start.13 = (bf16[128,7168]{1,0:T(8,128)(2,1)}, bf16[128,7168]{1,0:T(8,128)(2,1)S(1)}, u32[]{:S(2)}, u32[]{:S(2)}) collective-permute-start(bf16[128,7168]{1,0:T(8,128)(2,1)} %get-tuple-element.38), channel_id=1, source_target_pairs={{0,16},{16,0},{32,48},{48,32},{64,80},{80,64},{96,112},{112,96},{1... | collective-permute-start | bytes 5505032 | tf_op jit(solution)/shard_map/tok_route/ppermute | solution.py:55
  42.9 59.4 %all-to-all-start = ((bf16[16,16,7168]{2,1,0:T(8,128)(2,1)}), bf16[16,16,7168]{2,1,0:T(8,128)(2,1)}, u32[]{:S(2)}, u32[]{:S(2)}) async-start(bf16[16,16,7168]{2,1,0:T(8,128)(2,1)} %bitcast.13), calls=%async_computation | async-start | bytes 7340032 | tf_op jit(solution)/shard_map/cot_route/all_to_all | solution.py:395
  47.4 34.1 %collective-permute-start.10 = (bf16[32,7168]{1,0:T(8,128)(2,1)}, bf16[32,7168]{1,0:T(8,128)(2,1)S(1)}, u32[]{:S(2)}, u32[]{:S(2)}) collective-permute-start(bf16[32,7168]{1,0:T(8,128)(2,1)} %get-tuple-element.35), channel_id=1, source_target_pairs={{0,32},{16,48},{32,64},{48,80},{64,96},{80,112},{96,0},{112,16},{1... | collective-permute-start | bytes 1376264 | tf_op jit(solution)/shard_map/tok_route/ppermute | solution.py:47
  48.2 36.9 %collective-permute-start.11 = (bf16[32,7168]{1,0:T(8,128)(2,1)}, bf16[32,7168]{1,0:T(8,128)(2,1)S(1)}, u32[]{:S(2)}, u32[]{:S(2)}) collective-permute-start(bf16[32,7168]{1,0:T(8,128)(2,1)} %get-tuple-element.36), channel_id=1, source_target_pairs={{0,64},{16,80},{32,96},{48,112},{64,0},{80,16},{96,32},{112,48},{1... | collective-permute-start | bytes 1376264 | tf_op jit(solution)/shard_map/tok_route/ppermute | solution.py:47
  50.0 35.0 %collective-permute-start.12 = (bf16[32,7168]{1,0:T(8,128)(2,1)}, bf16[32,7168]{1,0:T(8,128)(2,1)S(1)}, u32[]{:S(2)}, u32[]{:S(2)}) collective-permute-start(bf16[32,7168]{1,0:T(8,128)(2,1)} %get-tuple-element.37), channel_id=1, source_target_pairs={{0,96},{16,112},{32,0},{48,16},{64,32},{80,48},{96,64},{112,80},{1... | collective-permute-start | bytes 1376264 | tf_op jit(solution)/shard_map/tok_route/ppermute | solution.py:47
  52.2 32.9 %collective-permute-start.16 = (bf16[32,7168]{1,0:T(8,128)(2,1)}, bf16[32,7168]{1,0:T(8,128)(2,1)S(1)}, u32[]{:S(2)}, u32[]{:S(2)}) collective-permute-start(bf16[32,7168]{1,0:T(8,128)(2,1)} %get-tuple-element.69), channel_id=1, source_target_pairs={{0,96},{16,112},{32,0},{48,16},{64,32},{80,48},{96,64},{112,80},{1... | collective-permute-start | bytes 1376264 | tf_op jit(solution)/shard_map/tok_route/ppermute | solution.py:47
  53.5 31.6 %collective-permute-start.15 = (bf16[32,7168]{1,0:T(8,128)(2,1)}, bf16[32,7168]{1,0:T(8,128)(2,1)S(1)}, u32[]{:S(2)}, u32[]{:S(2)}) collective-permute-start(bf16[32,7168]{1,0:T(8,128)(2,1)} %get-tuple-element.70), channel_id=1, source_target_pairs={{0,64},{16,80},{32,96},{48,112},{64,0},{80,16},{96,32},{112,48},{1... | collective-permute-start | bytes 1376264 | tf_op jit(solution)/shard_map/tok_route/ppermute | solution.py:47
  81.5 13.5 %copy-start.7 = (bf16[32,7168]{1,0:T(8,128)(2,1)}, bf16[32,7168]{1,0:T(8,128)(2,1)S(1)}, u32[]{:S(2)}) copy-start(bf16[32,7168]{1,0:T(8,128)(2,1)S(1)} %collective-permute-done.10.refs_0_.refs_1_) | copy-start | bytes 1376260
  81.5 13.5 %collective-permute-start.14 = (bf16[32,7168]{1,0:T(8,128)(2,1)}, bf16[32,7168]{1,0:T(8,128)(2,1)S(1)}, u32[]{:S(2)}, u32[]{:S(2)}) collective-permute-start(bf16[32,7168]{1,0:T(8,128)(2,1)} %get-tuple-element.71), channel_id=1, source_target_pairs={{0,32},{16,48},{32,64},{48,80},{64,96},{80,112},{96,0},{112,16},{1... | collective-permute-start | bytes 1376264 | tf_op jit(solution)/shard_map/tok_route/ppermute | solution.py:47
  85.0 10.0 %copy-start.8 = (bf16[32,7168]{1,0:T(8,128)(2,1)}, bf16[32,7168]{1,0:T(8,128)(2,1)S(1)}, u32[]{:S(2)}) copy-start(bf16[32,7168]{1,0:T(8,128)(2,1)S(1)} %collective-permute-done.11.refs_1_.refs_2_) | copy-start | bytes 1376260
  85.0 10.0 %copy-start.9 = (bf16[32,7168]{1,0:T(8,128)(2,1)}, bf16[32,7168]{1,0:T(8,128)(2,1)S(1)}, u32[]{:S(2)}) copy-start(bf16[32,7168]{1,0:T(8,128)(2,1)S(1)} %collective-permute-done.12.refs_2_.refs_3_) | copy-start | bytes 1376260
  85.1 9.9 %copy-start.10 = (bf16[32,7168]{1,0:T(8,128)(2,1)}, bf16[32,7168]{1,0:T(8,128)(2,1)S(1)}, u32[]{:S(2)}) copy-start(bf16[32,7168]{1,0:T(8,128)(2,1)S(1)} %collective-permute-done.16.refs_5_.refs_7_) | copy-start | bytes 1376260
  85.1 9.9 %copy-start.11 = (bf16[32,7168]{1,0:T(8,128)(2,1)}, bf16[32,7168]{1,0:T(8,128)(2,1)S(1)}, u32[]{:S(2)}) copy-start(bf16[32,7168]{1,0:T(8,128)(2,1)S(1)} %collective-permute-done.15.refs_4_.refs_6_) | copy-start | bytes 1376260
  100.2 27.8 %collective-permute-start.17 = (bf16[32,14336]{1,0:T(8,128)(2,1)}, bf16[32,14336]{1,0:T(8,128)(2,1)S(1)}, u32[]{:S(2)}, u32[]{:S(2)}) collective-permute-start(bf16[32,14336]{1,0:T(8,128)(2,1)} %get-tuple-element.45), channel_id=1, source_target_pairs={{0,3},{1,0},{2,1},{3,2},{4,7},{5,4},{6,5},{7,6},{8,11},{9,8},{10,9... | collective-permute-start | bytes 2752520 | tf_op jit(solution)/shard_map/shared_out/ppermute | solution.py:66
  100.2 27.8 %collective-permute-start.18 = (bf16[32,14336]{1,0:T(8,128)(2,1)}, bf16[32,14336]{1,0:T(8,128)(2,1)}, u32[]{:S(2)}, u32[]{:S(2)}) collective-permute-start(bf16[32,14336]{1,0:T(8,128)(2,1)} %get-tuple-element.46), channel_id=1, source_target_pairs={{0,2},{1,3},{2,0},{3,1},{4,6},{5,7},{6,4},{7,5},{8,10},{9,11},{10,... | collective-permute-start | bytes 2752520 | tf_op jit(solution)/shard_map/shared_out/ppermute | solution.py:66
  100.6 27.4 %collective-permute-start.19 = (bf16[32,14336]{1,0:T(8,128)(2,1)}, bf16[32,14336]{1,0:T(8,128)(2,1)}, u32[]{:S(2)}, u32[]{:S(2)}) collective-permute-start(bf16[32,14336]{1,0:T(8,128)(2,1)} %get-tuple-element.47), channel_id=1, source_target_pairs={{0,1},{1,2},{2,3},{3,0},{4,5},{5,6},{6,7},{7,4},{8,9},{9,10},{10,1... | collective-permute-start | bytes 2752520 | tf_op jit(solution)/shard_map/shared_out/ppermute | solution.py:66
  102.3 25.8 %copy-start.13 = (bf16[32,7168]{1,0:T(8,128)(2,1)S(1)}, bf16[32,7168]{1,0:T(8,128)(2,1)}, u32[]{:S(2)}) copy-start(bf16[32,7168]{1,0:T(8,128)(2,1)} %get-tuple-element.41._) | copy-start | bytes 1376260
  128.0 15.1 %collective-permute-start.23 = (bf16[128,7168]{1,0:T(8,128)(2,1)}, bf16[128,7168]{1,0:T(8,128)(2,1)S(1)}, u32[]{:S(2)}, u32[]{:S(2)}) collective-permute-start(bf16[128,7168]{1,0:T(8,128)(2,1)} %get-tuple-element.52), channel_id=1, source_target_pairs={{0,16},{16,0},{32,48},{48,32},{64,80},{80,64},{96,112},{112,96},{1... | collective-permute-start | bytes 5505032 | tf_op jit(solution)/shard_map/back_route/ppermute | solution.py:55
  130.7 55.8 %all-to-all-start.1 = ((bf16[16,16,7168]{2,1,0:T(8,128)(2,1)}), bf16[16,16,7168]{2,1,0:T(8,128)(2,1)}, u32[]{:S(2)}, u32[]{:S(2)}) async-start(bf16[16,16,7168]{2,1,0:T(8,128)(2,1)} %bitcast.8), calls=%async_computation.1 | async-start | bytes 7340032 | tf_op jit(solution)/shard_map/out_route/all_to_all | solution.py:472
  136.8 32.8 %collective-permute-start.20 = (bf16[32,7168]{1,0:T(8,128)(2,1)}, bf16[32,7168]{1,0:T(8,128)(2,1)S(1)}, u32[]{:S(2)}, u32[]{:S(2)}) collective-permute-start(bf16[32,7168]{1,0:T(8,128)(2,1)} %get-tuple-element.49), channel_id=1, source_target_pairs={{0,96},{16,112},{32,0},{48,16},{64,32},{80,48},{96,64},{112,80},{1... | collective-permute-start | bytes 1376264 | tf_op jit(solution)/shard_map/back_route/ppermute | solution.py:47
  139.1 34.3 %collective-permute-start.21 = (bf16[32,7168]{1,0:T(8,128)(2,1)}, bf16[32,7168]{1,0:T(8,128)(2,1)S(1)}, u32[]{:S(2)}, u32[]{:S(2)}) collective-permute-start(bf16[32,7168]{1,0:T(8,128)(2,1)} %get-tuple-element.50), channel_id=1, source_target_pairs={{0,64},{16,80},{32,96},{48,112},{64,0},{80,16},{96,32},{112,48},{1... | collective-permute-start | bytes 1376264 | tf_op jit(solution)/shard_map/back_route/ppermute | solution.py:47
  139.6 33.8 %collective-permute-start.22 = (bf16[32,7168]{1,0:T(8,128)(2,1)}, bf16[32,7168]{1,0:T(8,128)(2,1)S(1)}, u32[]{:S(2)}, u32[]{:S(2)}) collective-permute-start(bf16[32,7168]{1,0:T(8,128)(2,1)} %get-tuple-element.51), channel_id=1, source_target_pairs={{0,32},{16,48},{32,64},{48,80},{64,96},{80,112},{96,0},{112,16},{1... | collective-permute-start | bytes 1376264 | tf_op jit(solution)/shard_map/back_route/ppermute | solution.py:47
  146.7 27.0 %collective-permute-start.26 = (bf16[32,7168]{1,0:T(8,128)(2,1)S(1)}, bf16[32,7168]{1,0:T(8,128)(2,1)S(1)}, u32[]{:S(2)}, u32[]{:S(2)}) collective-permute-start(bf16[32,7168]{1,0:T(8,128)(2,1)S(1)} %get-tuple-element.64), channel_id=1, source_target_pairs={{0,32},{16,48},{32,64},{48,80},{64,96},{80,112},{96,0},{112,16},{1... | collective-permute-start | bytes 1376264 | tf_op jit(solution)/shard_map/back_route/ppermute | solution.py:47
  149.2 33.5 %collective-permute-start.25 = (bf16[32,7168]{1,0:T(8,128)(2,1)S(1)}, bf16[32,7168]{1,0:T(8,128)(2,1)S(1)}, u32[]{:S(2)}, u32[]{:S(2)}) collective-permute-start(bf16[32,7168]{1,0:T(8,128)(2,1)S(1)} %get-tuple-element.65), channel_id=1, source_target_pairs={{0,64},{16,80},{32,96},{48,112},{64,0},{80,16},{96,32},{112,48},{1... | collective-permute-start | bytes 1376264 | tf_op jit(solution)/shard_map/back_route/ppermute | solution.py:47
  169.7 16.8 %copy-start.26 = (bf16[32,7168]{1,0:T(8,128)(2,1)}, bf16[32,7168]{1,0:T(8,128)(2,1)S(1)}, u32[]{:S(2)}) copy-start(bf16[32,7168]{1,0:T(8,128)(2,1)S(1)} %collective-permute-done.20.refs_2_) | copy-start | bytes 1376260
  169.7 13.0 %collective-permute-start.24 = (bf16[32,7168]{1,0:T(8,128)(2,1)S(1)}, bf16[32,7168]{1,0:T(8,128)(2,1)S(1)}, u32[]{:S(2)}, u32[]{:S(2)}) collective-permute-start(bf16[32,7168]{1,0:T(8,128)(2,1)S(1)} %get-tuple-element.66), channel_id=1, source_target_pairs={{0,96},{16,112},{32,0},{48,16},{64,32},{80,48},{96,64},{112,80},{1... | collective-permute-start | bytes 1376264 | tf_op jit(solution)/shard_map/back_route/ppermute | solution.py:47
  173.4 13.1 %copy-start.27 = (bf16[32,7168]{1,0:T(8,128)(2,1)}, bf16[32,7168]{1,0:T(8,128)(2,1)S(1)}, u32[]{:S(2)}) copy-start(bf16[32,7168]{1,0:T(8,128)(2,1)S(1)} %collective-permute-done.21.refs_3_) | copy-start | bytes 1376260
  173.4 13.1 %copy-start.28 = (bf16[32,7168]{1,0:T(8,128)(2,1)}, bf16[32,7168]{1,0:T(8,128)(2,1)S(1)}, u32[]{:S(2)}) copy-start(bf16[32,7168]{1,0:T(8,128)(2,1)S(1)} %collective-permute-done.22.refs_4_) | copy-start | bytes 1376260
  173.7 12.8 %copy-start.29 = (bf16[32,7168]{1,0:T(8,128)(2,1)}, bf16[32,7168]{1,0:T(8,128)(2,1)S(1)}, u32[]{:S(2)}) copy-start(bf16[32,7168]{1,0:T(8,128)(2,1)S(1)} %collective-permute-done.26.refs_8_) | copy-start | bytes 1376260
  182.7 3.8 %copy-start.30 = (bf16[32,7168]{1,0:T(8,128)(2,1)}, bf16[32,7168]{1,0:T(8,128)(2,1)S(1)}, u32[]{:S(2)}) copy-start(bf16[32,7168]{1,0:T(8,128)(2,1)S(1)} %collective-permute-done.25.refs_7_) | copy-start | bytes 1376260
  182.7 3.8 %copy-start.31 = (bf16[32,7168]{1,0:T(8,128)(2,1)}, bf16[32,7168]{1,0:T(8,128)(2,1)S(1)}, u32[]{:S(2)}) copy-start(bf16[32,7168]{1,0:T(8,128)(2,1)S(1)} %collective-permute-done.24.refs_6_) | copy-start | bytes 1376260
  190.9 7.0 %copy-start.33 = (bf16[32,7168]{1,0:T(8,128)(2,1)S(1)}, bf16[32,7168]{1,0:T(8,128)(2,1)}, u32[]{:S(2)}) copy-start(bf16[32,7168]{1,0:T(8,128)(2,1)} %get-tuple-element.60) | copy-start | bytes 1376260
  190.9 8.0 %copy-start.32 = (bf16[32,7168]{1,0:T(8,128)(2,1)S(1)}, bf16[32,7168]{1,0:T(8,128)(2,1)}, u32[]{:S(2)}) copy-start(bf16[32,7168]{1,0:T(8,128)(2,1)} %get-tuple-element.61) | copy-start | bytes 1376260
  191.0 21.9 %copy-start.14 = (bf16[32,7168]{1,0:T(8,128)(2,1)S(1)}, bf16[32,7168]{1,0:T(8,128)(2,1)}, u32[]{:S(2)}) copy-start(bf16[32,7168]{1,0:T(8,128)(2,1)} %get-tuple-element.56.refs_0_) | copy-start | bytes 1376260
  194.5 5.7 %collective-permute-start.27 = (bf16[32,7168]{1,0:T(8,128)(2,1)}, bf16[32,7168]{1,0:T(8,128)(2,1)S(1)}, u32[]{:S(2)}, u32[]{:S(2)}) collective-permute-start(bf16[32,7168]{1,0:T(8,128)(2,1)} %get-tuple-element.58), channel_id=1, source_target_pairs={{0,16},{16,0},{32,48},{48,32},{64,80},{80,64},{96,112},{112,96},{1... | collective-permute-start | bytes 1376264 | tf_op jit(solution)/shard_map/out_sum/ppermute | solution.py:55
  194.5 14.3 %collective-permute-start.31 = (bf16[32,7168]{1,0:T(8,128)(2,1)S(1)}, bf16[32,7168]{1,0:T(8,128)(2,1)S(1)}, u32[]{:S(2)}, u32[]{:S(2)}) collective-permute-start(bf16[32,7168]{1,0:T(8,128)(2,1)S(1)} %copy-done.34), channel_id=1, source_target_pairs={{0,3},{1,0},{2,1},{3,2},{4,7},{5,4},{6,5},{7,6},{8,11},{9,8},{10,9... | collective-permute-start | bytes 1376264 | tf_op jit(solution)/shard_map/back_sum/ppermute | solution.py:66
  197.9 13.1 %collective-permute-start.32 = (bf16[32,7168]{1,0:T(8,128)(2,1)S(1)}, bf16[32,7168]{1,0:T(8,128)(2,1)S(1)}, u32[]{:S(2)}, u32[]{:S(2)}) collective-permute-start(bf16[32,7168]{1,0:T(8,128)(2,1)S(1)} %copy-done.33), channel_id=1, source_target_pairs={{0,2},{1,3},{2,0},{3,1},{4,6},{5,7},{6,4},{7,5},{8,10},{9,11},{10,... | collective-permute-start | bytes 1376264 | tf_op jit(solution)/shard_map/back_sum/ppermute | solution.py:66
  198.9 13.9 %collective-permute-start.33 = (bf16[32,7168]{1,0:T(8,128)(2,1)S(1)}, bf16[32,7168]{1,0:T(8,128)(2,1)S(1)}, u32[]{:S(2)}, u32[]{:S(2)}) collective-permute-start(bf16[32,7168]{1,0:T(8,128)(2,1)S(1)} %copy-done.32), channel_id=1, source_target_pairs={{0,1},{1,2},{2,3},{3,0},{4,5},{5,6},{6,7},{7,4},{8,9},{9,10},{10,1... | collective-permute-start | bytes 1376264 | tf_op jit(solution)/shard_map/back_sum/ppermute | solution.py:66
  201.5 11.5 %collective-permute-start.30 = (bf16[8,7168]{1,0:T(8,128)(2,1)S(1)}, bf16[8,7168]{1,0:T(8,128)(2,1)S(1)}, u32[]{:S(2)}, u32[]{:S(2)}) collective-permute-start(bf16[8,7168]{1,0:T(8,128)(2,1)S(1)} %get-tuple-element.75), channel_id=1, source_target_pairs={{0,32},{16,48},{32,64},{48,80},{64,96},{80,112},{96,0},{112,16},{1... | collective-permute-start | bytes 344072 | tf_op jit(solution)/shard_map/out_sum/ppermute | solution.py:47
  202.3 10.8 %collective-permute-start.29 = (bf16[8,7168]{1,0:T(8,128)(2,1)S(1)}, bf16[8,7168]{1,0:T(8,128)(2,1)S(1)}, u32[]{:S(2)}, u32[]{:S(2)}) collective-permute-start(bf16[8,7168]{1,0:T(8,128)(2,1)S(1)} %get-tuple-element.76), channel_id=1, source_target_pairs={{0,64},{16,80},{32,96},{48,112},{64,0},{80,16},{96,32},{112,48},{1... | collective-permute-start | bytes 344072 | tf_op jit(solution)/shard_map/out_sum/ppermute | solution.py:47
  208.9 5.7 %collective-permute-start.28 = (bf16[8,7168]{1,0:T(8,128)(2,1)S(1)}, bf16[8,7168]{1,0:T(8,128)(2,1)S(1)}, u32[]{:S(2)}, u32[]{:S(2)}) collective-permute-start(bf16[8,7168]{1,0:T(8,128)(2,1)S(1)} %get-tuple-element.77), channel_id=1, source_target_pairs={{0,96},{16,112},{32,0},{48,16},{64,32},{80,48},{96,64},{112,80},{1... | collective-permute-start | bytes 344072 | tf_op jit(solution)/shard_map/out_sum/ppermute | solution.py:47
  215.2 16.4 %copy-start.21 = (bf16[8,7168]{1,0:T(8,128)(2,1)S(1)}, bf16[8,7168]{1,0:T(8,128)(2,1)}, u32[]{:S(2)}) copy-start(bf16[8,7168]{1,0:T(8,128)(2,1)} %copy-done.20) | copy-start | bytes 344068
  215.2 16.4 %copy-start.23 = (bf16[8,7168]{1,0:T(8,128)(2,1)S(1)}, bf16[8,7168]{1,0:T(8,128)(2,1)}, u32[]{:S(2)}) copy-start(bf16[8,7168]{1,0:T(8,128)(2,1)} %copy-done.22) | copy-start | bytes 344068
  215.2 16.4 %copy-start.25 = (bf16[8,7168]{1,0:T(8,128)(2,1)S(1)}, bf16[8,7168]{1,0:T(8,128)(2,1)}, u32[]{:S(2)}) copy-start(bf16[8,7168]{1,0:T(8,128)(2,1)} %copy-done.24) | copy-start | bytes 344068
  216.5 7.8 %collective-permute-start.34 = (bf16[8,14336]{1,0:T(8,128)(2,1)S(1)}, bf16[8,14336]{1,0:T(8,128)(2,1)S(1)}, u32[]{:S(2)}, u32[]{:S(2)}) collective-permute-start(bf16[8,14336]{1,0:T(8,128)(2,1)S(1)} %get-tuple-element.72), channel_id=1, source_target_pairs={{0,12},{1,13},{2,14},{3,15},{4,0},{5,1},{6,2},{7,3},{8,4},{9,5},{1... | collective-permute-start | bytes 688136 | tf_op jit(solution)/shard_map/back_sum/ppermute | solution.py:66
  218.7 8.2 %collective-permute-start.36 = (bf16[8,14336]{1,0:T(8,128)(2,1)S(1)}, bf16[8,14336]{1,0:T(8,128)(2,1)S(1)}, u32[]{:S(2)}, u32[]{:S(2)}) collective-permute-start(bf16[8,14336]{1,0:T(8,128)(2,1)S(1)} %get-tuple-element.73), channel_id=1, source_target_pairs={{0,4},{1,5},{2,6},{3,7},{4,8},{5,9},{6,10},{7,11},{8,12},{9,13},{1... | collective-permute-start | bytes 688136 | tf_op jit(solution)/shard_map/back_sum/ppermute | solution.py:66
  218.7 12.1 %collective-permute-start.35 = (bf16[8,14336]{1,0:T(8,128)(2,1)S(1)}, bf16[8,14336]{1,0:T(8,128)(2,1)S(1)}, u32[]{:S(2)}, u32[]{:S(2)}) collective-permute-start(bf16[8,14336]{1,0:T(8,128)(2,1)S(1)} %get-tuple-element.74), channel_id=1, source_target_pairs={{0,8},{1,9},{2,10},{3,11},{4,12},{5,13},{6,14},{7,15},{8,0},{9,1},... | collective-permute-start | bytes 688136 | tf_op jit(solution)/shard_map/back_sum/ppermute | solution.py:66
  (10 other events, 15.0 us)
